TPU v7x, 512 devices: a whole 4x4x16 slice. The times are simulated.
512 devices in a mesh: wide: 64 (over x_lo, z, core), narrow: 8 (over y, x_hi).
Axes of the slice: x: 4 (x_hi: 2, x_lo: 2; x = x_hi * 2 + x_lo), y: 4, z: 16, core: 2. Of those that a mesh axis runs over, the one named last changes fastest.
Arguments:
- grad_out: bfloat16 [896, 28672], P('wide', 'narrow'), may hold values from -6 to 6
- inputs: bfloat16 [896, 8192], P(None, 'wide'), may hold values from -16 to 16
- out_basis: bfloat16 [28672, 28672], P('narrow', 'wide'), may hold values from -0.03125 to 0.03125
- in_basis: bfloat16 [8192, 8192], P('wide', 'narrow'), may hold values from -0.0625 to 0.0625
- eigen_values: bfloat16 [28672, 8192], P('wide', 'narrow'), may hold values from 1e-05 to 1500
Outputs:
- scores: float32 [4, 384], replicated
All inputs are finite; a program needn't handle non-finite values.
Results may differ from a plain program's by a relative error of at most 0.02.
Values may be sent and summed in bfloat16 or wider, within the bound.
No kernel may reach another device: no remote copies, remote signals or barrier semaphores. Data moves between devices by JAX's collectives and lax.ppermute only.
A program may use at most 64 MiB of HBM per device.

v0:
```python
import math

import jax
import jax.numpy as jnp
from jax import lax
from jax.sharding import PartitionSpec as P

D = 8192
FF = 28672
QUERIES = 4
QTOK = 128


def on_device(grad_out, inputs, out_basis, in_basis, eigen_values):
    partial_out = jnp.dot(
        lax.all_gather(grad_out, "wide", axis=0, tiled=True),
        out_basis,
        preferred_element_type=jnp.float32,
    )
    summed = lax.psum(partial_out.astype(jnp.bfloat16), "narrow")
    local_sum = jnp.sum(eigen_values, dtype=jnp.float32)
    overall = lax.psum(local_sum, ("wide", "narrow"))
    in_share = lax.psum_scatter(
        jnp.dot(inputs, in_basis, preferred_element_type=jnp.float32),
        "wide",
        scatter_dimension=0,
        tiled=True,
    )
    rotated_in = lax.all_gather(in_share.astype(jnp.bfloat16), "wide", axis=0, tiled=True)
    damping = 0.1 * overall / (FF * D)
    divisor = eigen_values.astype(jnp.float32) + damping
    query_rows = QUERIES * QTOK
    query_out = summed[:query_rows].reshape(QUERIES, QTOK, summed.shape[1])
    query_in = rotated_in[:query_rows].reshape(QUERIES, QTOK, rotated_in.shape[1])
    query_grads = jnp.einsum(
        "qta,qtb->qab", query_out, query_in, preferred_element_type=jnp.float32
    )
    precond = (query_grads / divisor[None]).astype(jnp.bfloat16)
    projected = jnp.einsum(
        "sb,qab->qsa", rotated_in[query_rows:], precond, preferred_element_type=jnp.float32
    )
    train_out = summed[query_rows:].astype(jnp.float32)
    norm_factor = 1.0 / math.sqrt(QTOK * FF * D)
    partial_scores = jnp.sum(train_out[None] * projected, axis=2) * norm_factor
    return lax.psum(partial_scores, ("wide", "narrow"))


def solution(mesh):
    return jax.shard_map(
        on_device,
        mesh=mesh,
        in_specs=(
            P("wide", "narrow"),
            P(None, "wide"),
            P("narrow", "wide"),
            P("wide", "narrow"),
            P("wide", "narrow"),
        ),
        out_specs=P(),
        check_vma=False,
    )
```

profile of v0, /device:TPU:1, one launch (start us, length us, event | category | flops | bytes accessed | tf_op | source)
XLA Modules:
  0.0 532.6 jit_solution(15346600932222465478)
XLA Ops:
  7.3 3.8 fusion.11
  11.1 135.8 %fusion = f32[16,1024]{1,0:T(8,128)S(1)} fusion(f32[896,1024]{1,0:T(8,128)} %fusion.11), kind=kCustom, calls=%all-reduce-scatter | all-reduce-scatter fusion | flops 1048577 | bytes 3737600
  147.0 1.3 collective-permute-start.1
  148.3 1.3 collective-permute-start.2
  149.6 5.9 %collective-permute-start.7 = (bf16[14,1024]{1,0:T(8,128)(2,1)S(1)}, bf16[14,1024]{1,0:T(8,128)(2,1)S(1)}, u32[]{:S(2)}, u32[]{:S(2)}) collective-permute-start(bf16[14,1024]{1,0:T(8,128)(2,1)S(1)} %slice.20), channel_id=1, source_target_pairs={{0,64},{8,72},{16,80},{24,88},{32,96},{40,104},{48,112},{56,120},{... | collective-permute-start | bytes 86024
  155.5 6.0 %collective-permute-start.3 = (bf16[16,1024]{1,0:T(8,128)(2,1)S(1)}, bf16[16,1024]{1,0:T(8,128)(2,1)S(1)}, u32[]{:S(2)}, u32[]{:S(2)}) collective-permute-start(bf16[16,1024]{1,0:T(8,128)(2,1)S(1)} %convert.14), channel_id=1, source_target_pairs={{0,32},{8,40},{16,48},{24,56},{32,64},{40,72},{48,80},{56,88},{64,... | collective-permute-start | bytes 98312
  161.5 4.6 collective-permute-start.4
  166.1 4.7 collective-permute-start.5
  170.8 5.8 %collective-permute-start.6 = (bf16[16,1024]{1,0:T(8,128)(2,1)S(1)}, bf16[16,1024]{1,0:T(8,128)(2,1)S(1)}, u32[]{:S(2)}, u32[]{:S(2)}) collective-permute-start(bf16[16,1024]{1,0:T(8,128)(2,1)S(1)} %convert.14), channel_id=1, source_target_pairs={{0,56},{8,64},{16,72},{24,80},{32,88},{40,96},{48,104},{56,112},{6... | collective-permute-start | bytes 98312
  176.7 1.9 collective-permute-start
  178.6 1.3 dynamic-slice.4
  180.6 12.0 %concatenate = bf16[142,1024]{1,0:T(8,128)(2,1)} concatenate(bf16[14,1024]{1,0:T(8,128)(2,1)S(1)} %collective-permute-done.7, bf16[16,1024]{1,0:T(8,128)(2,1)S(1)} %collective-permute-done.6, bf16[16,1024]{1,0:T(8,128)(2,1)S(1)} %collective-permute-done.5, bf16[16,1024]{1,0:T(8,128)(2,1)S(1)} %collective-permute-done.4, bf16[16,1024]{1,0:T(8,128)(2,1)S(1)} %collective-permute-done.3, ...), dimensions={0} | concatenate | bytes 614400
  192.6 1.4 fusion.9
  194.1 8.7 %reshape.11 = bf16[896,3584]{1,0:T(8,128)(2,1)} reshape(bf16[64,14,3584]{2,1,0:T(8,128)(2,1)} %all-gather.5.cloned.1.call-done) | data formatting | bytes 12845056
  202.9 6.6 %convolution_convert_fusion = bf16[896,448]{0,1:T(8,128)(2,1)} fusion(bf16[896,3584]{1,0:T(8,128)(2,1)} %reshape.11, bf16[3584,448]{0,1:T(8,128)(2,1)S(1)} %copy-done), kind=kOutput, calls=%fused_computation.7 | convolution fusion | flops 2877693952 | bytes 10436608 | tf_op jit(solution)/shard_map/dot_general | solution.py:15
  209.5 2.3 convert_reduce_fusion
  211.8 102.5 %psum.22 = f32[]{:T(128)} all-reduce(f32[]{:T(128)} %convert_reduce_fusion), channel_id=1, replica_groups=mesh['wide'=64,'narrow'=8] {'wide','narrow'}, use_global_device_ids=true, to_apply=%region_3.0 | all-reduce | flops 1 | bytes 8 | tf_op jit(solution)/shard_map/psum | solution.py:22
  314.9 2.7 convert_add_fusion
  317.6 3.8 reshape.13
  321.4 2.3 slice.18
  323.6 87.4 %all-reduce.4.cloned.1.call-done = bf16[896,448]{0,1:T(8,128)(2,1)} async-done(((bf16[896,448]{0,1:T(8,128)(2,1)}), bf16[896,448]{0,1:T(8,128)(2,1)}) %all-reduce.4.cloned.1.call-update) | async-done | bytes 802832 | tf_op jit(solution)/shard_map/psum | solution.py:20
  411.0 1.9 slice_convert_fusion
  412.9 5.4 %fusion.4 = f32[4,384]{1,0:T(4,128)S(1)} fusion(f32[448,1024]{1,0:T(8,128)} %convert_add_fusion, bf16[4,128,1024]{2,1,0:T(8,128)(2,1)} %bitcast.28, f32[384,448]{0,1:T(8,128)} %slice_convert_fusion, bf16[896,1024]{1,0:T(8,128)(2,1)} %reshape.13, bf16[896,448]{0,1:T(8,128)(2,1)} %all-reduce.4.cloned.1.call-done), kind=kOutput, calls=%fused_computation.4 | convolution fusion | flops 1884092928 | bytes 4823040 | tf_op jit(solution)/shard_map/sb,qab->qsa/dot_general | solution.py:39
  418.3 107.8 %psum.23 = f32[4,384]{1,0:T(4,128)} all-reduce(f32[4,384]{1,0:T(4,128)S(1)} %broadcast_multiply_fusion), channel_id=1, replica_groups=mesh['wide'=64,'narrow'=8] {'wide','narrow'}, use_global_device_ids=true, to_apply=%region_5.0 | all-reduce | flops 1536 | bytes 12288 | tf_op jit(solution)/shard_map/psum | solution.py:45
  (21 shorter events, 0.9 us)
Async XLA Ops:
  6.5 196.3 %copy-start = (bf16[3584,448]{0,1:T(8,128)(2,1)S(1)}, bf16[3584,448]{0,1:T(8,128)(2,1)}, u32[]{:S(2)}) copy-start(bf16[3584,448]{0,1:T(8,128)(2,1)} %param.7) | copy-start | bytes 9633796
  6.5 187.6 %all-gather.5.cloned.1.call-start = ((), (), s32[]{:S(2)}) async-start(), calls=%async_computation.1 | async-start | bytes 7454720 | tf_op jit(solution)/shard_map/all_gather | solution.py:16
  7.3 310.3 %all-gather.7.cloned.1.call-start = ((), (), s32[]{:S(2)}) async-start(), calls=%async_computation.2 | async-start | bytes 2129920 | tf_op jit(solution)/shard_map/all_gather | solution.py:29
  147.0 23.9 %collective-permute-start.1 = (bf16[16,1024]{1,0:T(8,128)(2,1)S(1)}, bf16[16,1024]{1,0:T(8,128)(2,1)S(1)}, u32[]{:S(2)}, u32[]{:S(2)}) collective-permute-start(bf16[16,1024]{1,0:T(8,128)(2,1)S(1)} %convert.14), channel_id=1, source_target_pairs={{0,16},{8,24},{16,32},{24,40},{32,48},{40,56},{48,64},{56,72},{64,... | collective-permute-start | bytes 98312
  148.3 28.4 %collective-permute-start.2 = (bf16[16,1024]{1,0:T(8,128)(2,1)S(1)}, bf16[16,1024]{1,0:T(8,128)(2,1)S(1)}, u32[]{:S(2)}, u32[]{:S(2)}) collective-permute-start(bf16[16,1024]{1,0:T(8,128)(2,1)S(1)} %convert.14), channel_id=1, source_target_pairs={{0,24},{8,32},{16,40},{24,48},{32,56},{40,64},{48,72},{56,80},{64,... | collective-permute-start | bytes 98312
  149.6 16.6 %collective-permute-start.7 = (bf16[14,1024]{1,0:T(8,128)(2,1)S(1)}, bf16[14,1024]{1,0:T(8,128)(2,1)S(1)}, u32[]{:S(2)}, u32[]{:S(2)}) collective-permute-start(bf16[14,1024]{1,0:T(8,128)(2,1)S(1)} %slice.20), channel_id=1, source_target_pairs={{0,64},{8,72},{16,80},{24,88},{32,96},{40,104},{48,112},{56,120},{... | collective-permute-start | bytes 86024
  155.5 25.0 %collective-permute-start.3 = (bf16[16,1024]{1,0:T(8,128)(2,1)S(1)}, bf16[16,1024]{1,0:T(8,128)(2,1)S(1)}, u32[]{:S(2)}, u32[]{:S(2)}) collective-permute-start(bf16[16,1024]{1,0:T(8,128)(2,1)S(1)} %convert.14), channel_id=1, source_target_pairs={{0,32},{8,40},{16,48},{24,56},{32,64},{40,72},{48,80},{56,88},{64,... | collective-permute-start | bytes 98312
  161.5 19.0 %collective-permute-start.4 = (bf16[16,1024]{1,0:T(8,128)(2,1)S(1)}, bf16[16,1024]{1,0:T(8,128)(2,1)S(1)}, u32[]{:S(2)}, u32[]{:S(2)}) collective-permute-start(bf16[16,1024]{1,0:T(8,128)(2,1)S(1)} %convert.14), channel_id=1, source_target_pairs={{0,40},{8,48},{16,56},{24,64},{32,72},{40,80},{48,88},{56,96},{64,... | collective-permute-start | bytes 98312
  166.1 14.4 %collective-permute-start.5 = (bf16[16,1024]{1,0:T(8,128)(2,1)S(1)}, bf16[16,1024]{1,0:T(8,128)(2,1)S(1)}, u32[]{:S(2)}, u32[]{:S(2)}) collective-permute-start(bf16[16,1024]{1,0:T(8,128)(2,1)S(1)} %convert.14), channel_id=1, source_target_pairs={{0,48},{8,56},{16,64},{24,72},{32,80},{40,88},{48,96},{56,104},{64... | collective-permute-start | bytes 98312
  170.8 9.8 %collective-permute-start.6 = (bf16[16,1024]{1,0:T(8,128)(2,1)S(1)}, bf16[16,1024]{1,0:T(8,128)(2,1)S(1)}, u32[]{:S(2)}, u32[]{:S(2)}) collective-permute-start(bf16[16,1024]{1,0:T(8,128)(2,1)S(1)} %convert.14), channel_id=1, source_target_pairs={{0,56},{8,64},{16,72},{24,80},{32,88},{40,96},{48,104},{56,112},{6... | collective-permute-start | bytes 98312
  176.7 3.9 collective-permute-start
  194.0 217.0 %all-reduce.4.cloned.1.call-start = ((), (), s32[]{:S(2)}) async-start(), calls=%async_computation | async-start | bytes 1605632 | tf_op jit(solution)/shard_map/psum | solution.py:20
Sparse Core Ops, SparseCore 0:
  9.5 134.3 all-gather.4
  194.2 118.4 all-gather.6
  315.6 95.3 all-reduce.3
where the time goes:
time: 535 us; the launch traced here: 533 us
  blocking collectives  346 us (65%)
  waiting for transfers between devices  88.1 us (16%)
  starting transfers between devices  31.6 us (6%)
  local copies, waits for them, and re-layouts  29.5 us (6%)
  matrix products  15.8 us (3%)
  between operations  14.6 us (3%)
  other arithmetic  6.87 us (1%)
    unnamed x1, blocking collectives  136 us
    psum x1, blocking collectives, on_device(): return lax.psum(partial_scores, ('wide', 'narrow'))  108 us
    psum x1, blocking collectives, on_device(): overall = lax.psum(local_sum, ('wide', 'narrow'))  102 us
    psum x1, waiting for transfers between devices, on_device(): summed = lax.psum(partial_out.astype(jnp.bfloat16), 'narrow')  87.4 us
    unnamed x8, starting transfers between devices  31.5 us
    unnamed x8, local copies, waits for them, and re-layouts  27.3 us
  transfers between devices with their start and end apart: 11, of which 1 were waited for; matrix products, arithmetic and copies ran while one was open for 34% of the time, Pallas kernels for 0%

commit v1 on v0

v1 whole, which is shorter than its diff:
```python
import math

import jax
import jax.numpy as jnp
import numpy as np
from jax import lax
from jax.experimental import pallas as pl
from jax.experimental.pallas import tpu as pltpu
from jax.sharding import Mesh, PartitionSpec as P

D = 8192
FF = 28672
QUERIES = 4
QTOK = 128
TOKENS = 896
SCORED = TOKENS - QUERIES * QTOK
X, Z, C, N = 2, 16, 2, 8
OWN = 14
ROWS = 16
RUN = Z * ROWS
HALF = X * RUN
ALL = C * HALF
PIECES = ALL // ROWS
TRAIN_Z = 2
AXES = {"x_lo": 2, "zh": 4, "zl": 4, "core": 2, "y": 4, "x_hi": 2}
ZZ = ("zh", "zl")
WIDE = ("x_lo", "zh", "zl", "core")
NARROW = ("y", "x_hi")

NEAR, MID, FAR = [0, 5, -5], [1, 6, -4, -1, 4, -6, 8], [2, 7, -3, -2, 3, -7]
OUT_HALF = [(0, z) for z in NEAR + MID] + [(1, z) for z in NEAR]
OUT_HALF += [(0, z) for z in FAR] + [(1, z) for z in MID + FAR]
SHARE = HALF // N
PER = SHARE // ROWS
OUT_ORDER = np.array([(c,) + OUT_HALF[n * PER + i] for n in range(N) for c in range(C) for i in range(PER)], np.int32)
IN_ORDER = np.array([(c, x, z) for c in range(C) for z in NEAR + MID + FAR for x in range(X)], np.int32)
OWNERS = np.array([(c, x, z) for x in range(X) for z in range(Z) for c in range(C)], np.int32)

VMEM = pl.BlockSpec(memory_space=pltpu.VMEM)
SMEM = pl.BlockSpec(memory_space=pltpu.SMEM)


def params():
    return pltpu.CompilerParams(vmem_limit_bytes=48 * 2**20)


def shift(x, axis, by):
    size = math.prod(AXES[a] for a in (axis if isinstance(axis, tuple) else (axis,)))
    return lax.ppermute(x, axis, [(i, (i + by) % size) for i in range(size)])


def from_z(x, distance):
    return shift(x, ZZ, -distance)


def cat(*parts):
    return jnp.concatenate(parts, 0)


def half(v):
    return v.astype(jnp.bfloat16)


def f32(v):
    return v.astype(jnp.float32)


def dot(a, b, over_a=1, over_b=0):
    return lax.dot_general(a, b, (((over_a,), (over_b,)), ((), ())), preferred_element_type=jnp.float32)


def rotate_in_kernel(at_ref, in_ref, basis_ref, keep_ref, send_ref, wide_s, rows_s):
    wide_s[:TOKENS, :] = f32(in_ref[...])
    wide_s[TOKENS:, :] = jnp.zeros((8, in_ref.shape[1]), jnp.float32)
    real = lax.broadcasted_iota(jnp.int32, (ROWS, 1), 0) < OWN
    for i in range(PIECES):
        block = jnp.where(real, wide_s[i * OWN:i * OWN + ROWS, :], 0.0)
        rows_s[pl.ds(pl.multiple_of(at_ref[i] * ROWS, ROWS), ROWS), :] = block
    for i in range(0, HALF, RUN):
        keep_ref[i:i + RUN, :] = dot(half(rows_s[i:i + RUN, :]), basis_ref[...])
        send_ref[i:i + RUN, :] = half(dot(half(rows_s[HALF + i:HALF + i + RUN, :]), basis_ref[...]))


def rotate_out_kernel(core_ref, *refs):
    blocks, (own_ref, other_ref, out_ref, rows_s) = refs[:6], refs[6:]
    at = 0
    for block in blocks:
        rows_s[at:at + block.shape[0], :] = block[...]
        at += block.shape[0]
    for i, basis in enumerate((own_ref, other_ref)):
        product = half(dot(rows_s[...], basis[...], 1, 1))
        out_ref[pl.ds((core_ref[0] ^ i) * HALF, HALF), :] = product


def stack_kernel(*refs):
    at = 0
    for block in refs[:-1]:
        refs[-1][at:at + block.shape[0], :] = block[...]
        at += block.shape[0]


def padding_sum(block):
    row = lax.rem(lax.broadcasted_iota(jnp.int32, block.shape, 0), ROWS)
    column = lax.broadcasted_iota(jnp.int32, block.shape, 1)
    return jnp.sum(jnp.where((row == OWN) & (column < 3), f32(block), 0.0), keepdims=True)


def with_terms(block, value):
    row = lax.broadcasted_iota(jnp.int32, block.shape, 0)
    column = lax.broadcasted_iota(jnp.int32, block.shape, 1)
    first = f32(half(value))
    second = f32(half(value - first))
    third = value - first - second
    terms = jnp.where(column == 0, first, jnp.where(column == 1, second, jnp.where(column == 2, third, 0.0)))
    return jnp.where(row == OWN, terms, block)


def share_kernel(parts_ref, ri0_ref, ri1_ref, out_ref):
    wide_sum = padding_sum(ri0_ref[:, :128]) + padding_sum(ri1_ref[:, :128])
    shares = []
    for c in range(C):
        total = f32(parts_ref[c * N])
        for n in range(1, N):
            total += f32(parts_ref[c * N + n])
        shares.append(with_terms(total, wide_sum) if c == 0 else total)
    share = half(jnp.concatenate(shares, 1))
    for n in range(N):
        out_ref[n] = share


def query_spans(q):
    spans = []
    for x in range(X):
        lo, hi = max(q * QTOK, x * 448), min((q + 1) * QTOK, (x + 1) * 448)
        if lo < hi:
            spans.append((x, (lo - x * 448) // 28, (hi - 1 - x * 448) // 28 + 1))
    return spans


def score_kernel(to_out_ref, to_in_ref, ro_ref, ri0_ref, ri1_ref, eig_ref, out_ref, ro_s, ri_s):
    def place(scratch, at_ref, i, block):
        scratch[pl.ds(pl.multiple_of(at_ref[i] * ROWS, ROWS), ROWS), :] = block

    overall = jnp.zeros((1, 1), jnp.float32)
    width = ro_ref.shape[2] // C
    for i in range(PIECES):
        n, c, at = i // (C * PER), i // PER % C, i % PER * ROWS
        place(ro_s, to_out_ref, i, ro_ref[n, at:at + ROWS, c * width:(c + 1) * width])
        source = (ri0_ref, ri1_ref)[i // (PIECES // C)]
        at = i % (PIECES // C) * ROWS
        place(ri_s, to_in_ref, i, source[at:at + ROWS, :])
    for n in range(N):
        overall += padding_sum(ro_ref[n, :ROWS, :128])

    def rows(ref, x, c, first, last):
        base = (x * C + c) * RUN
        return ref[base + first * ROWS:base + last * ROWS, :]

    def tokens(x, c, first, last, axis):
        shape = [1, 1]
        shape[axis] = (last - first) * ROWS
        at = lax.broadcasted_iota(jnp.int32, tuple(shape), axis)
        own = lax.rem(at, ROWS)
        return jnp.where(own < OWN, x * 448 + (first + at // ROWS) * 28 + c * OWN + own, -1)

    recip = 1.0 / (f32(eig_ref[...]) + overall * (0.1 / (FF * D)))
    scored = lax.broadcasted_iota(jnp.int32, (SCORED, 1), 0) + QUERIES * QTOK
    pick = jnp.concatenate([tokens(1, c, TRAIN_Z, Z, 1) for c in range(C)], 1) == scored
    pick = half(jnp.where(pick, 1.0, 0.0))
    train_out = dot(pick, cat(*[rows(ro_s, 1, c, TRAIN_Z, Z) for c in range(C)]))
    train_in = half(dot(pick, cat(*[rows(ri_s, 1, c, TRAIN_Z, Z) for c in range(C)])))
    scale = 1.0 / math.sqrt(QTOK * FF * D)
    for q in range(QUERIES):
        outs, ins = [], []
        for x, first, last in query_spans(q):
            for c in range(C):
                token = tokens(x, c, first, last, 0)
                keep = (token >= q * QTOK) & (token < (q + 1) * QTOK)
                outs.append(half(jnp.where(keep, f32(rows(ro_s, x, c, first, last)), 0.0)))
                ins.append(rows(ri_s, x, c, first, last))
        precond = half(dot(cat(*outs), cat(*ins), 0, 0) * recip)
        projected = dot(train_in, precond, 1, 1)
        score = jnp.sum(train_out * projected, axis=1) * scale
        for n in range(N):
            out_ref[n, q, :] = score


def stack(*blocks):
    rows = sum(b.shape[0] for b in blocks)
    shape = jax.ShapeDtypeStruct((rows,) + blocks[0].shape[1:], jnp.bfloat16)
    return pl.pallas_call(
        stack_kernel,
        out_shape=shape,
        in_specs=[VMEM] * len(blocks),
        out_specs=VMEM,
        compiler_params=params(),
        cost_estimate=pl.CostEstimate(flops=0, bytes_accessed=4 * shape.size, transcendentals=0),
    )(*blocks)


def gather_z(own):
    above = from_z(own, 5)
    near = stack(own, above, from_z(own, -5))
    up, down, across = from_z(near, 1), from_z(near, -1), from_z(above, 3)
    return near, (up, down, across), (from_z(up, 1), from_z(down, -1))


def on_device(grad_out, inputs, out_basis, in_basis, eigen_values):
    x_me, c_me = lax.axis_index("x_lo"), lax.axis_index("core")
    z_me = lax.axis_index(ZZ)
    n_out, n_in = out_basis.shape[1], in_basis.shape[1]

    def places(order, core, z):
        return ((x_me ^ order[:, 1]) * C + (core ^ order[:, 0])) * Z + lax.rem(z + order[:, 2] + Z, Z)

    own_basis = out_basis.T
    other_basis = shift(own_basis, "core", 1)

    near, mid, far = gather_z(lax.optimization_barrier(jnp.pad(grad_out, ((0, ROWS - OWN), (0, 0)))))
    *mid, near_x = lax.optimization_barrier((*mid, shift(near, "x_lo", 1)))
    mid, far = stack(*mid), stack(*far)
    blocks = [near, mid, near_x, far, shift(mid, "x_lo", 1), shift(far, "x_lo", 1)]

    to_rows = ((c_me ^ OWNERS[:, 0]) * X + (x_me ^ OWNERS[:, 1])) * Z + OWNERS[:, 2]
    keep, send = pl.pallas_call(
        rotate_in_kernel,
        out_shape=(jax.ShapeDtypeStruct((HALF, n_in), jnp.float32), jax.ShapeDtypeStruct((HALF, n_in), jnp.bfloat16)),
        in_specs=[SMEM, VMEM, VMEM],
        out_specs=(VMEM, VMEM),
        scratch_shapes=[
            pltpu.VMEM((TOKENS + 8, inputs.shape[1]), jnp.float32),
            pltpu.VMEM((ALL, inputs.shape[1]), jnp.float32),
        ],
        compiler_params=params(),
        cost_estimate=pl.CostEstimate(flops=3 * 10**8, bytes_accessed=3 * 10**6, transcendentals=0),
    )(to_rows, inputs, in_basis)
    part = keep + f32(shift(send, "core", 1))
    part = part[:RUN] + f32(shift(half(part[RUN:]), "x_lo", 1))
    pieces = lax.all_to_all(half(part), ZZ, 0, 0, tiled=True)
    own_in = jnp.sum(f32(pieces.reshape(Z, ROWS, n_in)), 0)
    own_in = half(with_terms(own_in, jnp.sum(eigen_values, dtype=jnp.float32)))
    near, mid, far = gather_z(cat(own_in, shift(own_in, "x_lo", 1)))
    ri0 = stack(near, *mid, *far)
    ri1 = shift(ri0, "core", 1)

    partial_out = pl.pallas_call(
        rotate_out_kernel,
        out_shape=jax.ShapeDtypeStruct((ALL, n_out), jnp.bfloat16),
        in_specs=[SMEM] + [VMEM] * 8,
        out_specs=VMEM,
        scratch_shapes=[pltpu.VMEM((HALF, grad_out.shape[1]), jnp.bfloat16)],
        compiler_params=params(),
        cost_estimate=pl.CostEstimate(flops=33 * 10**8, bytes_accessed=10**7, transcendentals=0),
    )(c_me.astype(jnp.int32).reshape(1), *blocks, own_basis, other_basis)
    parts = lax.all_to_all(partial_out, ("core",) + NARROW, 0, 0, tiled=True)
    shares = pl.pallas_call(
        share_kernel,
        out_shape=jax.ShapeDtypeStruct((N, SHARE, C * n_out), jnp.bfloat16),
        in_specs=[VMEM] * 3,
        out_specs=VMEM,
        compiler_params=params(),
        cost_estimate=pl.CostEstimate(flops=10**6, bytes_accessed=2 * 10**6, transcendentals=0),
    )(parts.reshape(C * N, SHARE, n_out), ri0, ri1)
    rotated_out = lax.all_to_all(shares, NARROW, 0, 0, tiled=True)

    scores = pl.pallas_call(
        score_kernel,
        out_shape=jax.ShapeDtypeStruct((N, QUERIES, SCORED), jnp.float32),
        in_specs=[SMEM] * 2 + [VMEM] * 4,
        out_specs=VMEM,
        scratch_shapes=[pltpu.VMEM((ALL, n_out), jnp.bfloat16), pltpu.VMEM((ALL, n_in), jnp.bfloat16)],
        compiler_params=params(),
        cost_estimate=pl.CostEstimate(flops=3 * 10**9, bytes_accessed=5 * 10**6, transcendentals=0),
    )(places(OUT_ORDER, 0, z_me), places(IN_ORDER, c_me, z_me), rotated_out, ri0, ri1, eigen_values)
    scores = jnp.sum(lax.all_to_all(scores, NARROW, 0, 0, tiled=True), 0)
    for axes in (("zl", "core"), ("x_lo", "zh")):
        scores = jnp.sum(lax.all_to_all(jnp.broadcast_to(scores, (8,) + scores.shape), axes, 0, 0, tiled=True), 0)
    return scores


def solution(mesh):
    fine = Mesh(mesh.devices.reshape(tuple(AXES.values())), tuple(AXES))
    return jax.shard_map(
        on_device,
        mesh=fine,
        in_specs=(
            P(WIDE, NARROW),
            P(None, WIDE),
            P(NARROW, WIDE),
            P(WIDE, NARROW),
            P(WIDE, NARROW),
        ),
        out_specs=P(),
        check_vma=False,
    )
```

time: 535 us -> 289 us (0.54)
  blocking collectives: 346 us -> 62.9 us
  starting transfers between devices: 31.6 us -> 107 us
  local copies, waits for them, and re-layouts: 29.5 us -> 3.92 us
  Pallas kernels: 0 us -> 16.5 us
  matrix products: 15.8 us -> 0 us
  between operations: 14.6 us -> 1.73 us
    psum x2 -> x0, blocking collectives: 210 us -> none  [the longest x1 108 us: on_device(): return lax.psum(partial_scores, ('wide', 'narrow'))]
    unnamed x1 -> x0, blocking collectives: 136 us -> none
    ppermute x0 -> x22, starting transfers between devices: none -> 93.9 us  [shift(): return lax.ppermute(x, axis, [(i, (i + by) % size) for i in range(size)])]
    psum x1 -> x0, waiting for transfers between devices: 87.4 us -> none  [on_device(): summed = lax.psum(partial_out.astype(jnp.bfloat16), 'narrow')]
    ppermute x0 -> x22, waiting for transfers between devices: none -> 76.9 us  [shift(): return lax.ppermute(x, axis, [(i, (i + by) % size) for i in range(size)])]
    all_to_all x0 -> x4, blocking collectives: none -> 62.9 us  [the longest x2 29.8 us: on_device(): lax.all_to_all(jnp.broadcast_to(scores, (8,) + scores.shape), axes, 0, 0,...]
    unnamed x8 -> x0, starting transfers between devices: 31.5 us -> none
    unnamed x8 -> x20, local copies, waits for them, and re-layouts: 27.3 us -> 3.82 us
  transfers between devices with their start and end apart: 11 -> 24, of which waited for: 1 -> 10; matrix products, arithmetic and copies ran while one was open for 34% -> 1% of each run, Pallas kernels for 0% -> 3%
where the time goes in v1:
time: 289 us; the launch traced here: 288 us
  starting transfers between devices  107 us (37%)
  waiting for transfers between devices  90.9 us (31%)
  blocking collectives  62.9 us (22%)
  Pallas kernels  16.5 us (6%)
  other arithmetic  5.05 us (2%)
  local copies, waits for them, and re-layouts  3.92 us (1%)
    ppermute x22, starting transfers between devices, shift(): return lax.ppermute(x, axis, [(i, (i + by) % size) for i in range(size)])  93.9 us
    ppermute x22, waiting for transfers between devices, shift(): return lax.ppermute(x, axis, [(i, (i + by) % size) for i in range(size)])  76.9 us
    all_to_all x2, blocking collectives, on_device(): lax.all_to_all(jnp.broadcast_to(scores, (8,) + scores.shape), axes, 0, 0,...  29.8 us
    all_to_all x1, blocking collectives, on_device(): parts = lax.all_to_all(partial_out, ('core',) + NARROW, 0, 0, tiled=True)  22.7 us
    all_to_all x1, waiting for transfers between devices, on_device(): rotated_out = lax.all_to_all(shares, NARROW, 0, 0, tiled=True)  14 us
    all_to_all x1, blocking collectives, on_device(): scores = jnp.sum(lax.all_to_all(scores, NARROW, 0, 0, tiled=True), 0)  10.5 us
    all_to_all x1, starting transfers between devices, on_device(): pieces = lax.all_to_all(half(part), ZZ, 0, 0, tiled=True)  9.59 us
    pallas_call x1, Pallas kernels, on_device(): pl.pallas_call(rotate_out_kernel, out_shape=jax.ShapeDtypeStruct((ALL, n_...  7.52 us
  transfers between devices with their start and end apart: 24, of which 10 were waited for; matrix products, arithmetic and copies ran while one was open for 1% of the time, Pallas kernels for 3%

profile of v1, /device:TPU:1, one launch (start us, length us, event | category | flops | bytes accessed | tf_op | source)
XLA Modules:
  0.0 288.3 jit_solution(14324578916389251407)
XLA Ops:
  3.9 8.8 %collective-permute-start.11 = (bf16[512,1024]{1,0:T(8,128)(2,1)S(1)}, bf16[512,1024]{1,0:T(8,128)(2,1)S(1)}, u32[]{:S(2)}, u32[]{:S(2)}) collective-permute-start(bf16[512,1024]{1,0:T(8,128)(2,1)S(1)} %get-tuple-element.16), channel_id=1, source_target_pairs={{0,8},{8,0},{1,9},{9,1},{2,10},{10,2},{3,11},{11,3},{4,12},{12,4},... | collective-permute-start | bytes 3145736 | tf_op jit(solution)/shard_map/ppermute | solution.py:49
  19.8 10.8 %collective-permute-done.12 = bf16[256,1024]{1,0:T(8,128)(2,1)S(1)} collective-permute-done((bf16[256,1024]{1,0:T(8,128)(2,1)S(1)}, bf16[256,1024]{1,0:T(8,128)(2,1)S(1)}, u32[]{:S(2)}, u32[]{:S(2)}) %collective-permute-start.12) | collective-permute-done | bytes 524320 | tf_op jit(solution)/shard_map/ppermute | solution.py:49
  31.5 9.6 %all-to-all-start.1 = ((bf16[16,16,1024]{2,1,0:T(8,128)(2,1)}), bf16[16,16,1024]{2,1,0:T(8,128)(2,1)}, u32[]{:S(2)}, u32[]{:S(2)}) async-start(bf16[16,16,1024]{2,1,0:T(8,128)(2,1)} %bitcast.3), calls=%async_computation.1 | async-start | bytes 1048576 | tf_op jit(solution)/shard_map/all_to_all | solution.py:239
  41.2 9.2 %collective-permute-start = (bf16[16,3584]{1,0:T(8,128)(2,1)S(1)}, bf16[16,3584]{1,0:T(8,128)(2,1)S(1)}, u32[]{:S(2)}, u32[]{:S(2)}) collective-permute-start(bf16[16,3584]{1,0:T(8,128)(2,1)S(1)} %pad.4.refs_0_), channel_id=1, source_target_pairs={{0,176},{16,192},{32,208},{48,224},{64,240},{80,0},{96,16},{112,32... | collective-permute-start | bytes 344072 | tf_op jit(solution)/shard_map/ppermute | solution.py:49
  52.4 27.5 %collective-permute-done.refs_1_ = bf16[16,3584]{1,0:T(8,128)(2,1)S(1)} collective-permute-done((bf16[16,3584]{1,0:T(8,128)(2,1)S(1)}, bf16[16,3584]{1,0:T(8,128)(2,1)S(1)}, u32[]{:S(2)}, u32[]{:S(2)}) %collective-permute-start) | collective-permute-done | bytes 114720 | tf_op jit(solution)/shard_map/ppermute | solution.py:49
  81.8 3.4 %collective-permute-start.3 = (bf16[48,3584]{1,0:T(8,128)(2,1)S(1)}, bf16[48,3584]{1,0:T(8,128)(2,1)S(1)}, u32[]{:S(2)}, u32[]{:S(2)}) collective-permute-start(bf16[48,3584]{1,0:T(8,128)(2,1)S(1)} %shard_map.136.refs_0_), channel_id=1, source_target_pairs={{0,16},{16,32},{32,48},{48,64},{64,80},{80,96},{96,112},{112,128},... | collective-permute-start | bytes 1032200 | tf_op jit(solution)/shard_map/ppermute | solution.py:49
  94.8 9.6 %collective-permute-start.4 = (bf16[16,3584]{1,0:T(8,128)(2,1)S(1)}, bf16[16,3584]{1,0:T(8,128)(2,1)S(1)}, u32[]{:S(2)}, u32[]{:S(2)}) collective-permute-start(bf16[16,3584]{1,0:T(8,128)(2,1)S(1)} %collective-permute-done.refs_1_), channel_id=1, source_target_pairs={{0,208},{16,224},{32,240},{48,0},{64,16},{80,32},{96,48},{112,64},... | collective-permute-start | bytes 344072 | tf_op jit(solution)/shard_map/ppermute | solution.py:49
  105.7 4.8 %collective-permute-done.4.refs_2_ = bf16[16,3584]{1,0:T(8,128)(2,1)S(1)} collective-permute-done((bf16[16,3584]{1,0:T(8,128)(2,1)S(1)}, bf16[16,3584]{1,0:T(8,128)(2,1)S(1)}, u32[]{:S(2)}, u32[]{:S(2)}) %collective-permute-start.4) | collective-permute-done | bytes 114720 | tf_op jit(solution)/shard_map/ppermute | solution.py:49
  111.3 3.1 %collective-permute-start.8 = (bf16[112,3584]{1,0:T(8,128)(2,1)S(1)}, bf16[112,3584]{1,0:T(8,128)(2,1)}, u32[]{:S(2)}, u32[]{:S(2)}) collective-permute-start(bf16[112,3584]{1,0:T(8,128)(2,1)S(1)} %shard_map.137.refs_1_), channel_id=1, source_target_pairs={{0,256},{256,0},{1,257},{257,1},{2,258},{258,2},{3,259},{259,3},{4... | collective-permute-start | bytes 2408456 | tf_op jit(solution)/shard_map/ppermute | solution.py:49
  122.9 23.1 %collective-permute-done.13 = bf16[16,1024]{1,0:T(8,128)(2,1)S(1)} collective-permute-done((bf16[16,1024]{1,0:T(8,128)(2,1)S(1)}, bf16[16,1024]{1,0:T(8,128)(2,1)S(1)}, u32[]{:S(2)}, u32[]{:S(2)}) %collective-permute-start.13) | collective-permute-done | bytes 32800 | tf_op jit(solution)/shard_map/ppermute | solution.py:49
  146.0 4.6 %collective-permute-start.14 = (bf16[32,1024]{1,0:T(8,128)(2,1)S(1)}, bf16[32,1024]{1,0:T(8,128)(2,1)S(1)}, u32[]{:S(2)}, u32[]{:S(2)}) collective-permute-start(bf16[32,1024]{1,0:T(8,128)(2,1)S(1)} %pad_maximum_fusion.refs_0_), channel_id=1, source_target_pairs={{0,176},{16,192},{32,208},{48,224},{64,240},{80,0},{96,16},{112,32... | collective-permute-start | bytes 196616 | tf_op jit(solution)/shard_map/ppermute | solution.py:49
  150.6 5.5 %collective-permute-start.15 = (bf16[32,1024]{1,0:T(8,128)(2,1)S(1)}, bf16[32,1024]{1,0:T(8,128)(2,1)S(1)}, u32[]{:S(2)}, u32[]{:S(2)}) collective-permute-start(bf16[32,1024]{1,0:T(8,128)(2,1)S(1)} %pad_maximum_fusion.refs_0_), channel_id=1, source_target_pairs={{0,80},{16,96},{32,112},{48,128},{64,144},{80,160},{96,176},{112,1... | collective-permute-start | bytes 196616 | tf_op jit(solution)/shard_map/ppermute | solution.py:49
  156.1 8.0 %collective-permute-start.18 = (bf16[32,1024]{1,0:T(8,128)(2,1)S(1)}, bf16[32,1024]{1,0:T(8,128)(2,1)S(1)}, u32[]{:S(2)}, u32[]{:S(2)}) collective-permute-start(bf16[32,1024]{1,0:T(8,128)(2,1)S(1)} %collective-permute-done.14.refs_1_), channel_id=1, source_target_pairs={{0,208},{16,224},{32,240},{48,0},{64,16},{80,32},{96,48},{112,64},... | collective-permute-start | bytes 196616 | tf_op jit(solution)/shard_map/ppermute | solution.py:49
  166.1 3.4 %collective-permute-start.17 = (bf16[96,1024]{1,0:T(8,128)(2,1)S(1)}, bf16[96,1024]{1,0:T(8,128)(2,1)S(1)}, u32[]{:S(2)}, u32[]{:S(2)}) collective-permute-start(bf16[96,1024]{1,0:T(8,128)(2,1)S(1)} %shard_map.141.refs_0_), channel_id=1, source_target_pairs={{0,16},{16,32},{32,48},{48,64},{64,80},{80,96},{96,112},{112,128},... | collective-permute-start | bytes 589832 | tf_op jit(solution)/shard_map/ppermute | solution.py:49
  179.3 3.7 %collective-permute-done.20.refs_5_ = bf16[96,1024]{1,0:T(8,128)(2,1)S(1)} collective-permute-done((bf16[96,1024]{1,0:T(8,128)(2,1)S(1)}, bf16[96,1024]{1,0:T(8,128)(2,1)S(1)}, u32[]{:S(2)}, u32[]{:S(2)}) %collective-permute-start.20) | collective-permute-done | bytes 196640 | tf_op jit(solution)/shard_map/ppermute | solution.py:49
  183.1 9.3 %collective-permute-start.21 = (bf16[512,1024]{1,0:T(8,128)(2,1)S(1)}, bf16[512,1024]{1,0:T(8,128)(2,1)S(1)}, u32[]{:S(2)}, u32[]{:S(2)}) collective-permute-start(bf16[512,1024]{1,0:T(8,128)(2,1)S(1)} %shard_map.142.ri0_ref), channel_id=1, source_target_pairs={{0,8},{8,0},{1,9},{9,1},{2,10},{10,2},{3,11},{11,3},{4,12},{12,4},... | collective-permute-start | bytes 3145736 | tf_op jit(solution)/shard_map/ppermute | solution.py:49
  192.5 7.5 %shard_map.139 = bf16[1024,448]{1,0:T(8,128)(2,1)S(1)} custom-call(s32[1]{0:T(128)} %bitcast.core_ref, bf16[48,3584]{1,0:T(8,128)(2,1)S(1)} %shard_map.136.refs_0_, bf16[112,3584]{1,0:T(8,128)(2,1)S(1)} %shard_map.137.refs_1_, bf16[48,3584]{1,0:T(8,128)(2,1)S(1)} %copy-done.3, bf16[96,3584]{1,0:T(8,128)(2,1)} %shard_map.138.refs_3_, ...), custom_call_target="tpu_custom_call" | custom-call | flops 3300000000 | bytes 10000000 | tf_op jit(solution)/shard_map/pallas_call | solution.py:246
  200.0 22.7 %all_to_all.38.parts_ref = bf16[16,64,448]{2,1,0:T(8,128)(2,1)S(1)} all-to-all(bf16[16,64,448]{2,1,0:T(8,128)(2,1)S(1)} %bitcast.4), channel_id=1, replica_groups=mesh['x_lo'=2,'zh'=4,'zl'=4,'core'=2,'y'=4,'x_hi'=2] {'core','y','x_hi'}, dimensions={0} | all-to-all | bytes 1835008 | tf_op jit(solution)/shard_map/all_to_all | solution.py:255
  223.8 3.7 %all-to-all-start.2 = ((bf16[8,64,896]{2,1,0:T(8,128)(2,1)}), bf16[8,64,896]{2,1,0:T(8,128)(2,1)S(1)}, u32[]{:S(2)}, u32[]{:S(2)}) async-start(bf16[8,64,896]{2,1,0:T(8,128)(2,1)} %shard_map.143), calls=%async_computation.2 | async-start | bytes 1835008 | tf_op jit(solution)/shard_map/all_to_all | solution.py:264
  227.6 14.0 %all-to-all-done.2.ro_ref = bf16[8,64,896]{2,1,0:T(8,128)(2,1)S(1)} async-done(((bf16[8,64,896]{2,1,0:T(8,128)(2,1)}), bf16[8,64,896]{2,1,0:T(8,128)(2,1)S(1)}, u32[]{:S(2)}, u32[]{:S(2)}) %all-to-all-start.2) | async-done | bytes 917536 | tf_op jit(solution)/shard_map/all_to_all | solution.py:264
  242.8 4.5 %shard_map.144 = f32[8,4,384]{2,1,0:T(4,128)S(1)} custom-call(s32[64]{0:T(128)S(1)} %fusion.3.to_out_ref, s32[64]{0:T(128)S(1)} %get-tuple-element.18.to_in_ref, bf16[8,64,896]{2,1,0:T(8,128)(2,1)S(1)} %all-to-all-done.2.ro_ref, bf16[512,1024]{1,0:T(8,128)(2,1)S(1)} %shard_map.142.ri0_ref, bf16[512,1024]{1,0:T(8,128)(2,1)S(1)} %collective-permute-done.21.ri1_ref, ...), custom_call_target="tpu_custom_call" | custom-call | flops 3000000000 | bytes 5000000 | tf_op jit(solution)/shard_map/pallas_call | solution.py:266
  247.3 10.5 %all_to_all.39 = f32[8,4,384]{2,1,0:T(4,128)S(1)} all-to-all(f32[8,4,384]{2,1,0:T(4,128)S(1)} %shard_map.144), channel_id=1, replica_groups=mesh['x_lo'=2,'zh'=4,'zl'=4,'core'=2,'y'=4,'x_hi'=2] {'y','x_hi'}, dimensions={0} | all-to-all | bytes 98304 | tf_op jit(solution)/shard_map/all_to_all | solution.py:275
  257.8 11.0 %all_to_all.40 = f32[8,4,384]{2,1,0:T(4,128)S(1)} all-to-all(f32[8,4,384]{2,1,0:T(4,128)S(1)} %broadcast_in_dim.25), channel_id=1, replica_groups=mesh['x_lo'=2,'zh'=4,'zl'=4,'core'=2,'y'=4,'x_hi'=2] {'zl','core'}, dimensions={0} | all-to-all | bytes 98304 | tf_op jit(solution)/shard_map/all_to_all | solution.py:277
  268.8 18.9 %all_to_all.41 = f32[8,4,384]{2,1,0:T(4,128)S(1)} all-to-all(f32[8,4,384]{2,1,0:T(4,128)S(1)} %broadcast_in_dim.26), channel_id=1, replica_groups=mesh['x_lo'=2,'zh'=4,'zl'=4,'core'=2,'y'=4,'x_hi'=2] {'x_lo','zh'}, dimensions={0} | all-to-all | bytes 98304 | tf_op jit(solution)/shard_map/all_to_all | solution.py:277
  (75 shorter events, 49.5 us)
Async XLA Ops:
  3.9 11.1 %collective-permute-start.11 = (bf16[512,1024]{1,0:T(8,128)(2,1)S(1)}, bf16[512,1024]{1,0:T(8,128)(2,1)S(1)}, u32[]{:S(2)}, u32[]{:S(2)}) collective-permute-start(bf16[512,1024]{1,0:T(8,128)(2,1)S(1)} %get-tuple-element.16), channel_id=1, source_target_pairs={{0,8},{8,0},{1,9},{9,1},{2,10},{10,2},{3,11},{11,3},{4,12},{12,4},... | collective-permute-start | bytes 3145736 | tf_op jit(solution)/shard_map/ppermute | solution.py:49
  15.4 15.2 %collective-permute-start.12 = (bf16[256,1024]{1,0:T(8,128)(2,1)S(1)}, bf16[256,1024]{1,0:T(8,128)(2,1)S(1)}, u32[]{:S(2)}, u32[]{:S(2)}) collective-permute-start(bf16[256,1024]{1,0:T(8,128)(2,1)S(1)} %slice.15), channel_id=1, source_target_pairs={{0,256},{256,0},{1,257},{257,1},{2,258},{258,2},{3,259},{259,3},{4... | collective-permute-start | bytes 1572872 | tf_op jit(solution)/shard_map/ppermute | solution.py:49
  17.5 175.0 %collective-permute-start.10 = (bf16[448,3584]{1,0:T(8,128)(2,1)}, bf16[448,3584]{1,0:T(8,128)(2,1)}, u32[]{:S(2)}, u32[]{:S(2)}) collective-permute-start(bf16[448,3584]{1,0:T(8,128)(2,1)} %bitcast.1.refs_6_), channel_id=1, source_target_pairs={{0,8},{8,0},{1,9},{9,1},{2,10},{10,2},{3,11},{11,3},{4,12},{12,4},... | collective-permute-start | bytes 9633800 | tf_op jit(solution)/shard_map/ppermute | solution.py:49
  31.5 86.9 %all-to-all-start.1 = ((bf16[16,16,1024]{2,1,0:T(8,128)(2,1)}), bf16[16,16,1024]{2,1,0:T(8,128)(2,1)}, u32[]{:S(2)}, u32[]{:S(2)}) async-start(bf16[16,16,1024]{2,1,0:T(8,128)(2,1)} %bitcast.3), calls=%async_computation.1 | async-start | bytes 1048576 | tf_op jit(solution)/shard_map/all_to_all | solution.py:239
  41.2 38.7 %collective-permute-start = (bf16[16,3584]{1,0:T(8,128)(2,1)S(1)}, bf16[16,3584]{1,0:T(8,128)(2,1)S(1)}, u32[]{:S(2)}, u32[]{:S(2)}) collective-permute-start(bf16[16,3584]{1,0:T(8,128)(2,1)S(1)} %pad.4.refs_0_), channel_id=1, source_target_pairs={{0,176},{16,192},{32,208},{48,224},{64,240},{80,0},{96,16},{112,32... | collective-permute-start | bytes 344072 | tf_op jit(solution)/shard_map/ppermute | solution.py:49
  50.4 29.5 %collective-permute-start.1 = (bf16[16,3584]{1,0:T(8,128)(2,1)S(1)}, bf16[16,3584]{1,0:T(8,128)(2,1)S(1)}, u32[]{:S(2)}, u32[]{:S(2)}) collective-permute-start(bf16[16,3584]{1,0:T(8,128)(2,1)S(1)} %pad.4.refs_0_), channel_id=1, source_target_pairs={{0,80},{16,96},{32,112},{48,128},{64,144},{80,160},{96,176},{112,1... | collective-permute-start | bytes 344072 | tf_op jit(solution)/shard_map/ppermute | solution.py:49
  79.9 8.5 %collective-permute-start.2 = (bf16[48,3584]{1,0:T(8,128)(2,1)S(1)}, bf16[48,3584]{1,0:T(8,128)(2,1)S(1)}, u32[]{:S(2)}, u32[]{:S(2)}) collective-permute-start(bf16[48,3584]{1,0:T(8,128)(2,1)S(1)} %shard_map.136.refs_0_), channel_id=1, source_target_pairs={{0,240},{16,0},{32,16},{48,32},{64,48},{80,64},{96,80},{112,96},{1... | collective-permute-start | bytes 1032200 | tf_op jit(solution)/shard_map/ppermute | solution.py:49
  81.8 9.6 %collective-permute-start.3 = (bf16[48,3584]{1,0:T(8,128)(2,1)S(1)}, bf16[48,3584]{1,0:T(8,128)(2,1)S(1)}, u32[]{:S(2)}, u32[]{:S(2)}) collective-permute-start(bf16[48,3584]{1,0:T(8,128)(2,1)S(1)} %shard_map.136.refs_0_), channel_id=1, source_target_pairs={{0,16},{16,32},{32,48},{48,64},{64,80},{80,96},{96,112},{112,128},... | collective-permute-start | bytes 1032200 | tf_op jit(solution)/shard_map/ppermute | solution.py:49
  85.2 25.3 %collective-permute-start.5 = (bf16[48,3584]{1,0:T(8,128)(2,1)S(1)}, bf16[48,3584]{1,0:T(8,128)(2,1)S(1)}, u32[]{:S(2)}, u32[]{:S(2)}) collective-permute-start(bf16[48,3584]{1,0:T(8,128)(2,1)S(1)} %shard_map.136.refs_0_), channel_id=1, source_target_pairs={{0,256},{256,0},{1,257},{257,1},{2,258},{258,2},{3,259},{259,3},{4... | collective-permute-start | bytes 1032200 | tf_op jit(solution)/shard_map/ppermute | solution.py:49
  88.4 26.1 %collective-permute-start.6 = (bf16[48,3584]{1,0:T(8,128)(2,1)S(1)}, bf16[48,3584]{1,0:T(8,128)(2,1)S(1)}, u32[]{:S(2)}, u32[]{:S(2)}) collective-permute-start(bf16[48,3584]{1,0:T(8,128)(2,1)S(1)} %collective-permute-done.2.refs_0_), channel_id=1, source_target_pairs={{0,240},{16,0},{32,16},{48,32},{64,48},{80,64},{96,80},{112,96},{1... | collective-permute-start | bytes 1032200 | tf_op jit(solution)/shard_map/ppermute | solution.py:49
  91.5 22.9 %collective-permute-start.7 = (bf16[48,3584]{1,0:T(8,128)(2,1)S(1)}, bf16[48,3584]{1,0:T(8,128)(2,1)}, u32[]{:S(2)}, u32[]{:S(2)}) collective-permute-start(bf16[48,3584]{1,0:T(8,128)(2,1)S(1)} %collective-permute-done.3.refs_1_), channel_id=1, source_target_pairs={{0,16},{16,32},{32,48},{48,64},{64,80},{80,96},{96,112},{112,128},... | collective-permute-start | bytes 1032200 | tf_op jit(solution)/shard_map/ppermute | solution.py:49
  94.8 15.7 %collective-permute-start.4 = (bf16[16,3584]{1,0:T(8,128)(2,1)S(1)}, bf16[16,3584]{1,0:T(8,128)(2,1)S(1)}, u32[]{:S(2)}, u32[]{:S(2)}) collective-permute-start(bf16[16,3584]{1,0:T(8,128)(2,1)S(1)} %collective-permute-done.refs_1_), channel_id=1, source_target_pairs={{0,208},{16,224},{32,240},{48,0},{64,16},{80,32},{96,48},{112,64},... | collective-permute-start | bytes 344072 | tf_op jit(solution)/shard_map/ppermute | solution.py:49
  111.3 81.1 %collective-permute-start.8 = (bf16[112,3584]{1,0:T(8,128)(2,1)S(1)}, bf16[112,3584]{1,0:T(8,128)(2,1)}, u32[]{:S(2)}, u32[]{:S(2)}) collective-permute-start(bf16[112,3584]{1,0:T(8,128)(2,1)S(1)} %shard_map.137.refs_1_), channel_id=1, source_target_pairs={{0,256},{256,0},{1,257},{257,1},{2,258},{258,2},{3,259},{259,3},{4... | collective-permute-start | bytes 2408456 | tf_op jit(solution)/shard_map/ppermute | solution.py:49
  116.3 76.1 %collective-permute-start.9 = (bf16[96,3584]{1,0:T(8,128)(2,1)}, bf16[96,3584]{1,0:T(8,128)(2,1)}, u32[]{:S(2)}, u32[]{:S(2)}) collective-permute-start(bf16[96,3584]{1,0:T(8,128)(2,1)} %shard_map.138.refs_3_), channel_id=1, source_target_pairs={{0,256},{256,0},{1,257},{257,1},{2,258},{258,2},{3,259},{259,3},{4... | collective-permute-start | bytes 2064392 | tf_op jit(solution)/shard_map/ppermute | solution.py:49
  119.8 26.3 %collective-permute-start.13 = (bf16[16,1024]{1,0:T(8,128)(2,1)S(1)}, bf16[16,1024]{1,0:T(8,128)(2,1)S(1)}, u32[]{:S(2)}, u32[]{:S(2)}) collective-permute-start(bf16[16,1024]{1,0:T(8,128)(2,1)S(1)} %select_convert_fusion), channel_id=1, source_target_pairs={{0,256},{256,0},{1,257},{257,1},{2,258},{258,2},{3,259},{259,3},{4... | collective-permute-start | bytes 98312 | tf_op jit(solution)/shard_map/ppermute | solution.py:49
  146.0 10.1 %collective-permute-start.14 = (bf16[32,1024]{1,0:T(8,128)(2,1)S(1)}, bf16[32,1024]{1,0:T(8,128)(2,1)S(1)}, u32[]{:S(2)}, u32[]{:S(2)}) collective-permute-start(bf16[32,1024]{1,0:T(8,128)(2,1)S(1)} %pad_maximum_fusion.refs_0_), channel_id=1, source_target_pairs={{0,176},{16,192},{32,208},{48,224},{64,240},{80,0},{96,16},{112,32... | collective-permute-start | bytes 196616 | tf_op jit(solution)/shard_map/ppermute | solution.py:49
  150.6 13.6 %collective-permute-start.15 = (bf16[32,1024]{1,0:T(8,128)(2,1)S(1)}, bf16[32,1024]{1,0:T(8,128)(2,1)S(1)}, u32[]{:S(2)}, u32[]{:S(2)}) collective-permute-start(bf16[32,1024]{1,0:T(8,128)(2,1)S(1)} %pad_maximum_fusion.refs_0_), channel_id=1, source_target_pairs={{0,80},{16,96},{32,112},{48,128},{64,144},{80,160},{96,176},{112,1... | collective-permute-start | bytes 196616 | tf_op jit(solution)/shard_map/ppermute | solution.py:49
  156.1 10.0 %collective-permute-start.18 = (bf16[32,1024]{1,0:T(8,128)(2,1)S(1)}, bf16[32,1024]{1,0:T(8,128)(2,1)S(1)}, u32[]{:S(2)}, u32[]{:S(2)}) collective-permute-start(bf16[32,1024]{1,0:T(8,128)(2,1)S(1)} %collective-permute-done.14.refs_1_), channel_id=1, source_target_pairs={{0,208},{16,224},{32,240},{48,0},{64,16},{80,32},{96,48},{112,64},... | collective-permute-start | bytes 196616 | tf_op jit(solution)/shard_map/ppermute | solution.py:49
  164.2 8.4 %collective-permute-start.16 = (bf16[96,1024]{1,0:T(8,128)(2,1)S(1)}, bf16[96,1024]{1,0:T(8,128)(2,1)S(1)}, u32[]{:S(2)}, u32[]{:S(2)}) collective-permute-start(bf16[96,1024]{1,0:T(8,128)(2,1)S(1)} %shard_map.141.refs_0_), channel_id=1, source_target_pairs={{0,240},{16,0},{32,16},{48,32},{64,48},{80,64},{96,80},{112,96},{1... | collective-permute-start | bytes 589832 | tf_op jit(solution)/shard_map/ppermute | solution.py:49
  166.1 9.2 %collective-permute-start.17 = (bf16[96,1024]{1,0:T(8,128)(2,1)S(1)}, bf16[96,1024]{1,0:T(8,128)(2,1)S(1)}, u32[]{:S(2)}, u32[]{:S(2)}) collective-permute-start(bf16[96,1024]{1,0:T(8,128)(2,1)S(1)} %shard_map.141.refs_0_), channel_id=1, source_target_pairs={{0,16},{16,32},{32,48},{48,64},{64,80},{80,96},{96,112},{112,128},... | collective-permute-start | bytes 589832 | tf_op jit(solution)/shard_map/ppermute | solution.py:49
  172.6 6.7 %collective-permute-start.19 = (bf16[96,1024]{1,0:T(8,128)(2,1)S(1)}, bf16[96,1024]{1,0:T(8,128)(2,1)S(1)}, u32[]{:S(2)}, u32[]{:S(2)}) collective-permute-start(bf16[96,1024]{1,0:T(8,128)(2,1)S(1)} %collective-permute-done.16.refs_1_), channel_id=1, source_target_pairs={{0,240},{16,0},{32,16},{48,32},{64,48},{80,64},{96,80},{112,96},{1... | collective-permute-start | bytes 589832 | tf_op jit(solution)/shard_map/ppermute | solution.py:49
  175.4 7.6 %collective-permute-start.20 = (bf16[96,1024]{1,0:T(8,128)(2,1)S(1)}, bf16[96,1024]{1,0:T(8,128)(2,1)S(1)}, u32[]{:S(2)}, u32[]{:S(2)}) collective-permute-start(bf16[96,1024]{1,0:T(8,128)(2,1)S(1)} %collective-permute-done.17.refs_2_), channel_id=1, source_target_pairs={{0,16},{16,32},{32,48},{48,64},{64,80},{80,96},{96,112},{112,128},... | collective-permute-start | bytes 589832 | tf_op jit(solution)/shard_map/ppermute | solution.py:49
  183.1 39.6 %collective-permute-start.21 = (bf16[512,1024]{1,0:T(8,128)(2,1)S(1)}, bf16[512,1024]{1,0:T(8,128)(2,1)S(1)}, u32[]{:S(2)}, u32[]{:S(2)}) collective-permute-start(bf16[512,1024]{1,0:T(8,128)(2,1)S(1)} %shard_map.142.ri0_ref), channel_id=1, source_target_pairs={{0,8},{8,0},{1,9},{9,1},{2,10},{10,2},{3,11},{11,3},{4,12},{12,4},... | collective-permute-start | bytes 3145736 | tf_op jit(solution)/shard_map/ppermute | solution.py:49
  223.8 17.8 %all-to-all-start.2 = ((bf16[8,64,896]{2,1,0:T(8,128)(2,1)}), bf16[8,64,896]{2,1,0:T(8,128)(2,1)S(1)}, u32[]{:S(2)}, u32[]{:S(2)}) async-start(bf16[8,64,896]{2,1,0:T(8,128)(2,1)} %shard_map.143), calls=%async_computation.2 | async-start | bytes 1835008 | tf_op jit(solution)/shard_map/all_to_all | solution.py:264
  (10 other events, 196.5 us)

commit v2 on v1

--- a/solution.py
+++ b/solution.py
@@ -27,13 +27,13 @@
 WIDE = ("x_lo", "zh", "zl", "core")
 NARROW = ("y", "x_hi")
 
-NEAR, MID, FAR = [0, 5, -5], [1, 6, -4, -1, 4, -6, 8], [2, 7, -3, -2, 3, -7]
+NEAR, MID, FAR = [0, 5, -5], [1, 6, -4, -1, 4, -6], [8, 2, 7, -3, -2, 3, -7]
 OUT_HALF = [(0, z) for z in NEAR + MID] + [(1, z) for z in NEAR]
 OUT_HALF += [(0, z) for z in FAR] + [(1, z) for z in MID + FAR]
 SHARE = HALF // N
 PER = SHARE // ROWS
 OUT_ORDER = np.array([(c,) + OUT_HALF[n * PER + i] for n in range(N) for c in range(C) for i in range(PER)], np.int32)
-IN_ORDER = np.array([(c, x, z) for c in range(C) for z in NEAR + MID + FAR for x in range(X)], np.int32)
+IN_ORDER = np.array([(c, x, z) for c in range(C) for x in range(X) for z in range(Z)], np.int32)
 OWNERS = np.array([(c, x, z) for x in range(X) for z in range(Z) for c in range(C)], np.int32)
 
 VMEM = pl.BlockSpec(memory_space=pltpu.VMEM)
@@ -115,14 +115,13 @@
     return jnp.where(row == OWN, terms, block)
 
 
-def share_kernel(parts_ref, ri0_ref, ri1_ref, out_ref):
-    wide_sum = padding_sum(ri0_ref[:, :128]) + padding_sum(ri1_ref[:, :128])
+def share_kernel(parts_ref, out_ref):
     shares = []
     for c in range(C):
         total = f32(parts_ref[c * N])
         for n in range(1, N):
             total += f32(parts_ref[c * N + n])
-        shares.append(with_terms(total, wide_sum) if c == 0 else total)
+        shares.append(total)
     share = half(jnp.concatenate(shares, 1))
     for n in range(N):
         out_ref[n] = share
@@ -137,20 +136,19 @@
     return spans
 
 
-def score_kernel(to_out_ref, to_in_ref, ro_ref, ri0_ref, ri1_ref, eig_ref, out_ref, ro_s, ri_s):
+def score_kernel(to_out_ref, to_in_ref, ro_ref, *refs):
+    in_refs, (eig_ref, out_ref, ro_s, ri_s) = refs[:4], refs[4:]
+
     def place(scratch, at_ref, i, block):
         scratch[pl.ds(pl.multiple_of(at_ref[i] * ROWS, ROWS), ROWS), :] = block
 
-    overall = jnp.zeros((1, 1), jnp.float32)
+    overall = sum(padding_sum(ref[:, :128]) for ref in in_refs)
     width = ro_ref.shape[2] // C
     for i in range(PIECES):
         n, c, at = i // (C * PER), i // PER % C, i % PER * ROWS
         place(ro_s, to_out_ref, i, ro_ref[n, at:at + ROWS, c * width:(c + 1) * width])
-        source = (ri0_ref, ri1_ref)[i // (PIECES // C)]
-        at = i % (PIECES // C) * ROWS
-        place(ri_s, to_in_ref, i, source[at:at + ROWS, :])
-    for n in range(N):
-        overall += padding_sum(ro_ref[n, :ROWS, :128])
+        at = i % Z * ROWS
+        place(ri_s, to_in_ref, i, in_refs[i // Z][at:at + ROWS, :])
 
     def rows(ref, x, c, first, last):
         base = (x * C + c) * RUN
@@ -198,13 +196,6 @@
     )(*blocks)
 
 
-def gather_z(own):
-    above = from_z(own, 5)
-    near = stack(own, above, from_z(own, -5))
-    up, down, across = from_z(near, 1), from_z(near, -1), from_z(above, 3)
-    return near, (up, down, across), (from_z(up, 1), from_z(down, -1))
-
-
 def on_device(grad_out, inputs, out_basis, in_basis, eigen_values):
     x_me, c_me = lax.axis_index("x_lo"), lax.axis_index("core")
     z_me = lax.axis_index(ZZ)
@@ -214,13 +205,8 @@
         return ((x_me ^ order[:, 1]) * C + (core ^ order[:, 0])) * Z + lax.rem(z + order[:, 2] + Z, Z)
 
     own_basis = out_basis.T
-    other_basis = shift(own_basis, "core", 1)
-
-    near, mid, far = gather_z(lax.optimization_barrier(jnp.pad(grad_out, ((0, ROWS - OWN), (0, 0)))))
-    *mid, near_x = lax.optimization_barrier((*mid, shift(near, "x_lo", 1)))
-    mid, far = stack(*mid), stack(*far)
-    blocks = [near, mid, near_x, far, shift(mid, "x_lo", 1), shift(far, "x_lo", 1)]
-
+    own, inputs = lax.optimization_barrier((jnp.pad(grad_out, ((0, ROWS - OWN), (0, 0))), inputs))
+    above, below = from_z(own, 5), from_z(own, -5)
     to_rows = ((c_me ^ OWNERS[:, 0]) * X + (x_me ^ OWNERS[:, 1])) * Z + OWNERS[:, 2]
     keep, send = pl.pallas_call(
         rotate_in_kernel,
@@ -232,16 +218,30 @@
             pltpu.VMEM((ALL, inputs.shape[1]), jnp.float32),
         ],
         compiler_params=params(),
-        cost_estimate=pl.CostEstimate(flops=3 * 10**8, bytes_accessed=3 * 10**6, transcendentals=0),
+        cost_estimate=pl.CostEstimate(flops=3 * 10**10, bytes_accessed=3 * 10**6, transcendentals=0),
     )(to_rows, inputs, in_basis)
     part = keep + f32(shift(send, "core", 1))
-    part = part[:RUN] + f32(shift(half(part[RUN:]), "x_lo", 1))
-    pieces = lax.all_to_all(half(part), ZZ, 0, 0, tiled=True)
+    part_x = shift(half(part[RUN:]), "x_lo", 1)
+    local_sum = jnp.full((N, 128), jnp.sum(eigen_values, dtype=jnp.float32))
+    narrow_sum = jnp.sum(lax.all_to_all(local_sum, NARROW, 0, 0, tiled=True)[:, 0])
+    above, below, part, part_x, narrow_sum = lax.optimization_barrier((above, below, part, part_x, narrow_sum))
+
+    near = stack(own, above, below)
+    up, down, near_x = from_z(near, 1), from_z(near, -1), shift(near, "x_lo", 1)
+    across = from_z(above, 3)
+    other_basis = shift(own_basis, "core", 1)
+    part = half(part[:RUN] + f32(part_x))
+    up, down, near_x, part = lax.optimization_barrier((up, down, near_x, part))
+    pieces = lax.all_to_all(part, ZZ, 0, 0, tiled=True)
+    mid = stack(up, down)
+    *far, mid_x = lax.optimization_barrier((from_z(up, 1), from_z(down, -1), shift(mid, "x_lo", 1)))
+    far = stack(across, *far)
+    far_x = shift(far, "x_lo", 1)
+    blocks = [near, mid, near_x, far, mid_x, far_x]
+
     own_in = jnp.sum(f32(pieces.reshape(Z, ROWS, n_in)), 0)
-    own_in = half(with_terms(own_in, jnp.sum(eigen_values, dtype=jnp.float32)))
-    near, mid, far = gather_z(cat(own_in, shift(own_in, "x_lo", 1)))
-    ri0 = stack(near, *mid, *far)
-    ri1 = shift(ri0, "core", 1)
+    own_in = half(with_terms(own_in, narrow_sum))
+    column = lax.all_to_all(jnp.broadcast_to(own_in, (Z,) + own_in.shape), ZZ, 0, 0, tiled=True)
 
     partial_out = pl.pallas_call(
         rotate_out_kernel,
@@ -252,26 +252,30 @@
         compiler_params=params(),
         cost_estimate=pl.CostEstimate(flops=33 * 10**8, bytes_accessed=10**7, transcendentals=0),
     )(c_me.astype(jnp.int32).reshape(1), *blocks, own_basis, other_basis)
+    column, partial_out = lax.optimization_barrier((column.reshape(RUN, n_in), partial_out))
+    column_x = shift(column, "x_lo", 1)
+    rotated_in = [column, column_x, shift(column, "core", 1), shift(column_x, "core", 1)]
+
     parts = lax.all_to_all(partial_out, ("core",) + NARROW, 0, 0, tiled=True)
     shares = pl.pallas_call(
         share_kernel,
         out_shape=jax.ShapeDtypeStruct((N, SHARE, C * n_out), jnp.bfloat16),
-        in_specs=[VMEM] * 3,
+        in_specs=[VMEM],
         out_specs=VMEM,
         compiler_params=params(),
         cost_estimate=pl.CostEstimate(flops=10**6, bytes_accessed=2 * 10**6, transcendentals=0),
-    )(parts.reshape(C * N, SHARE, n_out), ri0, ri1)
+    )(parts.reshape(C * N, SHARE, n_out))
     rotated_out = lax.all_to_all(shares, NARROW, 0, 0, tiled=True)
 
     scores = pl.pallas_call(
         score_kernel,
         out_shape=jax.ShapeDtypeStruct((N, QUERIES, SCORED), jnp.float32),
-        in_specs=[SMEM] * 2 + [VMEM] * 4,
+        in_specs=[SMEM] * 2 + [VMEM] * 6,
         out_specs=VMEM,
         scratch_shapes=[pltpu.VMEM((ALL, n_out), jnp.bfloat16), pltpu.VMEM((ALL, n_in), jnp.bfloat16)],
         compiler_params=params(),
         cost_estimate=pl.CostEstimate(flops=3 * 10**9, bytes_accessed=5 * 10**6, transcendentals=0),
-    )(places(OUT_ORDER, 0, z_me), places(IN_ORDER, c_me, z_me), rotated_out, ri0, ri1, eigen_values)
+    )(places(OUT_ORDER, 0, z_me), places(IN_ORDER, c_me, 0), rotated_out, *rotated_in, eigen_values)
     scores = jnp.sum(lax.all_to_all(scores, NARROW, 0, 0, tiled=True), 0)
     for axes in (("zl", "core"), ("x_lo", "zh")):
         scores = jnp.sum(lax.all_to_all(jnp.broadcast_to(scores, (8,) + scores.shape), axes, 0, 0, tiled=True), 0)

time: 289 us -> 280 us (0.969)
  blocking collectives: 62.9 us -> 45.7 us
  starting transfers between devices: 107 us -> 115 us
    all_to_all x1 -> x4, starting transfers between devices: 9.59 us -> 40.4 us  [the longest x1 12.5 us: on_device(): lax.all_to_all(jnp.broadcast_to(own_in, (Z,) + own_in.shape), ZZ, 0, 0, t...]
    all_to_all x1 -> x4, waiting for transfers between devices: 0.01 us -> 29.8 us  [the longest x1 17.1 us: on_device(): pieces = lax.all_to_all(part, ZZ, 0, 0, tiled=True)]
    ppermute x22 -> x16, waiting for transfers between devices: 76.9 us -> 49 us  [shift(): return lax.ppermute(x, axis, [(i, (i + by) % size) for i in range(size)])]
    ppermute x22 -> x16, starting transfers between devices: 93.9 us -> 70 us  [shift(): return lax.ppermute(x, axis, [(i, (i + by) % size) for i in range(size)])]
    all_to_all x1 -> x0, blocking collectives: 22.7 us -> none  [on_device(): parts = lax.all_to_all(partial_out, ('core',) + NARROW, 0, 0, tiled=True)]
    all_to_all x2, blocking collectives: 29.8 us -> 36.7 us  [on_device(): lax.all_to_all(jnp.broadcast_to(scores, (8,) + scores.shape), axes, 0, 0,...]
    all_to_all x1, waiting for transfers between devices: 14 us -> 9.8 us  [on_device(): rotated_out = lax.all_to_all(shares, NARROW, 0, 0, tiled=True)]
  transfers between devices with their start and end apart: 24 -> 21, of which waited for: 10 -> 13; matrix products, arithmetic and copies ran while one was open for 1% -> 2% of each run, Pallas kernels for 3% -> 3%
where the time goes in v2:
time: 280 us; the launch traced here: 279 us
  starting transfers between devices  115 us (41%)
  waiting for transfers between devices  88.6 us (32%)
  blocking collectives  45.7 us (16%)
  Pallas kernels  15.5 us (6%)
  local copies, waits for them, and re-layouts  6.26 us (2%)
  other arithmetic  5.85 us (2%)
    ppermute x16, starting transfers between devices, shift(): return lax.ppermute(x, axis, [(i, (i + by) % size) for i in range(size)])  70 us
    ppermute x16, waiting for transfers between devices, shift(): return lax.ppermute(x, axis, [(i, (i + by) % size) for i in range(size)])  49 us
    all_to_all x2, blocking collectives, on_device(): lax.all_to_all(jnp.broadcast_to(scores, (8,) + scores.shape), axes, 0, 0,...  36.7 us
    all_to_all x1, waiting for transfers between devices, on_device(): pieces = lax.all_to_all(part, ZZ, 0, 0, tiled=True)  17.1 us
    all_to_all x1, waiting for transfers between devices, on_device(): parts = lax.all_to_all(partial_out, ('core',) + NARROW, 0, 0, tiled=True)  12.7 us
    all_to_all x1, starting transfers between devices, on_device(): lax.all_to_all(jnp.broadcast_to(own_in, (Z,) + own_in.shape), ZZ, 0, 0, t...  12.5 us
    all_to_all x1, starting transfers between devices, on_device(): parts = lax.all_to_all(partial_out, ('core',) + NARROW, 0, 0, tiled=True)  12.4 us
    all_to_all x1, starting transfers between devices, on_device(): pieces = lax.all_to_all(part, ZZ, 0, 0, tiled=True)  12.2 us
  transfers between devices with their start and end apart: 21, of which 13 were waited for; matrix products, arithmetic and copies ran while one was open for 2% of the time, Pallas kernels for 3%

profile of v2, /device:TPU:1, one launch (start us, length us, event | category | flops | bytes accessed | tf_op | source)
XLA Modules:
  0.0 278.8 jit_solution(3105351990422373049)
XLA Ops:
  4.8 8.8 %collective-permute-start.2 = (bf16[512,1024]{1,0:T(8,128)(2,1)S(1)}, bf16[512,1024]{1,0:T(8,128)(2,1)S(1)}, u32[]{:S(2)}, u32[]{:S(2)}) collective-permute-start(bf16[512,1024]{1,0:T(8,128)(2,1)S(1)} %get-tuple-element.26), channel_id=1, source_target_pairs={{0,8},{8,0},{1,9},{9,1},{2,10},{10,2},{3,11},{11,3},{4,12},{12,4},... | collective-permute-start | bytes 3145736 | tf_op jit(solution)/shard_map/ppermute | solution.py:49
  21.9 3.3 %all-to-all-start = ((f32[8,1,128]{2,1,0:T(1,128)}), f32[8,1,128]{2,1,0:T(1,128)S(1)}, u32[]{:S(2)}, u32[]{:S(2)}) async-start(f32[8,1,128]{2,1,0:T(1,128)} %broadcast_in_dim.27), calls=%async_computation | async-start | bytes 8192 | tf_op jit(solution)/shard_map/all_to_all | solution.py:226
  25.2 9.0 %collective-permute-start.1 = (bf16[16,3584]{1,0:T(8,128)(2,1)S(1)}, bf16[16,3584]{1,0:T(8,128)(2,1)S(1)}, u32[]{:S(2)}, u32[]{:S(2)}) collective-permute-start(bf16[16,3584]{1,0:T(8,128)(2,1)S(1)} %pad.4.refs_0_), channel_id=1, source_target_pairs={{0,80},{16,96},{32,112},{48,128},{64,144},{80,160},{96,176},{112,1... | collective-permute-start | bytes 344072 | tf_op jit(solution)/shard_map/ppermute | solution.py:49
  34.3 5.9 %collective-permute-start = (bf16[16,3584]{1,0:T(8,128)(2,1)S(1)}, bf16[16,3584]{1,0:T(8,128)(2,1)S(1)}, u32[]{:S(2)}, u32[]{:S(2)}) collective-permute-start(bf16[16,3584]{1,0:T(8,128)(2,1)S(1)} %pad.4.refs_0_), channel_id=1, source_target_pairs={{0,176},{16,192},{32,208},{48,224},{64,240},{80,0},{96,16},{112,32... | collective-permute-start | bytes 344072 | tf_op jit(solution)/shard_map/ppermute | solution.py:49
  40.8 7.3 %collective-permute-done.refs_1_ = bf16[16,3584]{1,0:T(8,128)(2,1)S(1)} collective-permute-done((bf16[16,3584]{1,0:T(8,128)(2,1)S(1)}, bf16[16,3584]{1,0:T(8,128)(2,1)S(1)}, u32[]{:S(2)}, u32[]{:S(2)}) %collective-permute-start) | collective-permute-done | bytes 114720 | tf_op jit(solution)/shard_map/ppermute | solution.py:49
  52.0 10.4 %collective-permute-start.4 = (bf16[48,3584]{1,0:T(8,128)(2,1)S(1)}, bf16[48,3584]{1,0:T(8,128)(2,1)S(1)}, u32[]{:S(2)}, u32[]{:S(2)}) collective-permute-start(bf16[48,3584]{1,0:T(8,128)(2,1)S(1)} %shard_map.137.refs_0_), channel_id=1, source_target_pairs={{0,240},{16,0},{32,16},{48,32},{64,48},{80,64},{96,80},{112,96},{1... | collective-permute-start | bytes 1032200 | tf_op jit(solution)/shard_map/ppermute | solution.py:49
  68.7 12.2 %all-to-all-start.1 = ((bf16[16,16,1024]{2,1,0:T(8,128)(2,1)}), bf16[16,16,1024]{2,1,0:T(8,128)(2,1)S(1)}, u32[]{:S(2)}, u32[]{:S(2)}) async-start(bf16[16,16,1024]{2,1,0:T(8,128)(2,1)} %bitcast.1), calls=%async_computation.1 | async-start | bytes 1048576 | tf_op jit(solution)/shard_map/all_to_all | solution.py:235
  80.8 3.9 %collective-permute-start.12 = (bf16[448,3584]{1,0:T(8,128)(2,1)}, bf16[448,3584]{1,0:T(8,128)(2,1)}, u32[]{:S(2)}, u32[]{:S(2)}) collective-permute-start(bf16[448,3584]{1,0:T(8,128)(2,1)} %bitcast.10), channel_id=1, source_target_pairs={{0,8},{8,0},{1,9},{9,1},{2,10},{10,2},{3,11},{11,3},{4,12},{12,4},... | collective-permute-start | bytes 9633800 | tf_op jit(solution)/shard_map/ppermute | solution.py:49
  86.1 17.1 %all-to-all-done.1 = bf16[16,16,1024]{2,1,0:T(8,128)(2,1)S(1)} async-done(((bf16[16,16,1024]{2,1,0:T(8,128)(2,1)}), bf16[16,16,1024]{2,1,0:T(8,128)(2,1)S(1)}, u32[]{:S(2)}, u32[]{:S(2)}) %all-to-all-start.1) | async-done | bytes 524320 | tf_op jit(solution)/shard_map/all_to_all | solution.py:235
  104.3 12.5 %all-to-all-start.2 = ((bf16[16,16,1024]{2,1,0:T(8,128)(2,1)}), bf16[16,16,1024]{2,1,0:T(8,128)(2,1)S(1)}, u32[]{:S(2)}, u32[]{:S(2)}) async-start(bf16[16,16,1024]{2,1,0:T(8,128)(2,1)} %broadcast_in_dim.32), calls=%async_computation.2 | async-start | bytes 1048576 | tf_op jit(solution)/shard_map/all_to_all | solution.py:244
  120.1 4.5 %collective-permute-start.8 = (bf16[48,3584]{1,0:T(8,128)(2,1)S(1)}, bf16[48,3584]{1,0:T(8,128)(2,1)S(1)}, u32[]{:S(2)}, u32[]{:S(2)}) collective-permute-start(bf16[48,3584]{1,0:T(8,128)(2,1)S(1)} %collective-permute-done.4.refs_0_), channel_id=1, source_target_pairs={{0,240},{16,0},{32,16},{48,32},{64,48},{80,64},{96,80},{112,96},{1... | collective-permute-start | bytes 1032200 | tf_op jit(solution)/shard_map/ppermute | solution.py:49
  126.6 5.2 %collective-permute-start.7 = (bf16[16,3584]{1,0:T(8,128)(2,1)S(1)}, bf16[16,3584]{1,0:T(8,128)(2,1)S(1)}, u32[]{:S(2)}, u32[]{:S(2)}) collective-permute-start(bf16[16,3584]{1,0:T(8,128)(2,1)S(1)} %collective-permute-done.refs_1_), channel_id=1, source_target_pairs={{0,208},{16,224},{32,240},{48,0},{64,16},{80,32},{96,48},{112,64},... | collective-permute-start | bytes 344072 | tf_op jit(solution)/shard_map/ppermute | solution.py:49
  131.7 16.7 %collective-permute-done.8.refs_1_ = bf16[48,3584]{1,0:T(8,128)(2,1)S(1)} collective-permute-done((bf16[48,3584]{1,0:T(8,128)(2,1)S(1)}, bf16[48,3584]{1,0:T(8,128)(2,1)S(1)}, u32[]{:S(2)}, u32[]{:S(2)}) %collective-permute-start.8) | collective-permute-done | bytes 344096 | tf_op jit(solution)/shard_map/ppermute | solution.py:49
  155.1 13.7 %collective-permute-done.11.refs_5_ = bf16[112,3584]{1,0:T(8,128)(2,1)S(1)} collective-permute-done((bf16[112,3584]{1,0:T(8,128)(2,1)S(1)}, bf16[112,3584]{1,0:T(8,128)(2,1)S(1)}, u32[]{:S(2)}, u32[]{:S(2)}) %collective-permute-start.11) | collective-permute-done | bytes 802848 | tf_op jit(solution)/shard_map/ppermute | solution.py:49
  168.8 7.8 %shard_map.140 = bf16[1024,448]{1,0:T(8,128)(2,1)} custom-call(s32[1]{0:T(128)} %bitcast.3.core_ref, bf16[48,3584]{1,0:T(8,128)(2,1)S(1)} %shard_map.137.refs_0_, bf16[96,3584]{1,0:T(8,128)(2,1)S(1)} %shard_map.138.refs_1_, bf16[48,3584]{1,0:T(8,128)(2,1)S(1)} %collective-permute-done.6.refs_2_, bf16[112,3584]{1,0:T(8,128)(2,1)S(1)} %shard_map.139.refs_3_, ...), custom_call_target="tpu_custom_call" | custom-call | flops 3300000000 | bytes 10000000 | tf_op jit(solution)/shard_map/pallas_call | solution.py:246
  176.6 12.4 %all-to-all-start.3 = ((bf16[16,64,448]{2,1,0:T(8,128)(2,1)}), bf16[16,64,448]{2,1,0:T(8,128)(2,1)S(1)}, u32[]{:S(2)}, u32[]{:S(2)}) async-start(bf16[16,64,448]{2,1,0:T(8,128)(2,1)} %bitcast.5), calls=%async_computation.3 | async-start | bytes 2097152 | tf_op jit(solution)/shard_map/all_to_all | solution.py:259
  191.4 12.7 %all-to-all-done.3.parts_ref = bf16[16,64,448]{2,1,0:T(8,128)(2,1)S(1)} async-done(((bf16[16,64,448]{2,1,0:T(8,128)(2,1)}), bf16[16,64,448]{2,1,0:T(8,128)(2,1)S(1)}, u32[]{:S(2)}, u32[]{:S(2)}) %all-to-all-start.3) | async-done | bytes 917536 | tf_op jit(solution)/shard_map/all_to_all | solution.py:259
  205.2 4.7 %all-to-all-start.4 = ((bf16[8,64,896]{2,1,0:T(8,128)(2,1)}), bf16[8,64,896]{2,1,0:T(8,128)(2,1)S(1)}, u32[]{:S(2)}, u32[]{:S(2)}) async-start(bf16[8,64,896]{2,1,0:T(8,128)(2,1)} %shard_map.141), calls=%async_computation.4 | async-start | bytes 1835008 | tf_op jit(solution)/shard_map/all_to_all | solution.py:268
  209.9 3.4 %collective-permute-start.14 = (bf16[256,1024]{1,0:T(8,128)(2,1)S(1)}, bf16[256,1024]{1,0:T(8,128)(2,1)}, u32[]{:S(2)}, u32[]{:S(2)}) collective-permute-start(bf16[256,1024]{1,0:T(8,128)(2,1)S(1)} %bitcast.7), channel_id=1, source_target_pairs={{0,8},{8,0},{1,9},{9,1},{2,10},{10,2},{3,11},{11,3},{4,12},{12,4},... | collective-permute-start | bytes 1572872 | tf_op jit(solution)/shard_map/ppermute | solution.py:49
  217.4 9.8 %all-to-all-done.4.ro_ref = bf16[8,64,896]{2,1,0:T(8,128)(2,1)S(1)} async-done(((bf16[8,64,896]{2,1,0:T(8,128)(2,1)}), bf16[8,64,896]{2,1,0:T(8,128)(2,1)S(1)}, u32[]{:S(2)}, u32[]{:S(2)}) %all-to-all-start.4) | async-done | bytes 917536 | tf_op jit(solution)/shard_map/all_to_all | solution.py:268
  227.2 5.2 %shard_map.142 = f32[8,4,384]{2,1,0:T(4,128)S(1)} custom-call(s32[64]{0:T(128)S(1)} %fusion.2.to_out_ref, s32[64]{0:T(128)S(1)} %get-tuple-element.42.to_in_ref, bf16[8,64,896]{2,1,0:T(8,128)(2,1)S(1)} %all-to-all-done.4.ro_ref, bf16[256,1024]{1,0:T(8,128)(2,1)S(1)} %bitcast.8, bf16[256,1024]{1,0:T(8,128)(2,1)S(1)} %collective-permute-done.13.refs_1_, ...), custom_call_target="tpu_custom_call" | custom-call | flops 3000000000 | bytes 5000000 | tf_op jit(solution)/shard_map/pallas_call | solution.py:270
  232.4 9.0 %all_to_all.52 = f32[8,4,384]{2,1,0:T(4,128)S(1)} all-to-all(f32[8,4,384]{2,1,0:T(4,128)S(1)} %shard_map.142), channel_id=1, replica_groups=mesh['x_lo'=2,'zh'=4,'zl'=4,'core'=2,'y'=4,'x_hi'=2] {'y','x_hi'}, dimensions={0} | all-to-all | bytes 98304 | tf_op jit(solution)/shard_map/all_to_all | solution.py:279
  241.5 17.2 %all_to_all.53 = f32[8,4,384]{2,1,0:T(4,128)S(1)} all-to-all(f32[8,4,384]{2,1,0:T(4,128)S(1)} %broadcast_in_dim.33), channel_id=1, replica_groups=mesh['x_lo'=2,'zh'=4,'zl'=4,'core'=2,'y'=4,'x_hi'=2] {'zl','core'}, dimensions={0} | all-to-all | bytes 98304 | tf_op jit(solution)/shard_map/all_to_all | solution.py:281
  258.7 19.5 %all_to_all.54 = f32[8,4,384]{2,1,0:T(4,128)S(1)} all-to-all(f32[8,4,384]{2,1,0:T(4,128)S(1)} %broadcast_in_dim.34), channel_id=1, replica_groups=mesh['x_lo'=2,'zh'=4,'zl'=4,'core'=2,'y'=4,'x_hi'=2] {'x_lo','zh'}, dimensions={0} | all-to-all | bytes 98304 | tf_op jit(solution)/shard_map/all_to_all | solution.py:281
  (62 shorter events, 44.9 us)
Async XLA Ops:
  4.8 11.1 %collective-permute-start.2 = (bf16[512,1024]{1,0:T(8,128)(2,1)S(1)}, bf16[512,1024]{1,0:T(8,128)(2,1)S(1)}, u32[]{:S(2)}, u32[]{:S(2)}) collective-permute-start(bf16[512,1024]{1,0:T(8,128)(2,1)S(1)} %get-tuple-element.26), channel_id=1, source_target_pairs={{0,8},{8,0},{1,9},{9,1},{2,10},{10,2},{3,11},{11,3},{4,12},{12,4},... | collective-permute-start | bytes 3145736 | tf_op jit(solution)/shard_map/ppermute | solution.py:49
  17.8 30.4 %collective-permute-start.3 = (bf16[256,1024]{1,0:T(8,128)(2,1)S(1)}, bf16[256,1024]{1,0:T(8,128)(2,1)S(1)}, u32[]{:S(2)}, u32[]{:S(2)}) collective-permute-start(bf16[256,1024]{1,0:T(8,128)(2,1)S(1)} %slice.17), channel_id=1, source_target_pairs={{0,256},{256,0},{1,257},{257,1},{2,258},{258,2},{3,259},{259,3},{4... | collective-permute-start | bytes 1572872 | tf_op jit(solution)/shard_map/ppermute | solution.py:49
  21.9 18.2 %all-to-all-start = ((f32[8,1,128]{2,1,0:T(1,128)}), f32[8,1,128]{2,1,0:T(1,128)S(1)}, u32[]{:S(2)}, u32[]{:S(2)}) async-start(f32[8,1,128]{2,1,0:T(1,128)} %broadcast_in_dim.27), calls=%async_computation | async-start | bytes 8192 | tf_op jit(solution)/shard_map/all_to_all | solution.py:226
  25.2 15.6 %collective-permute-start.1 = (bf16[16,3584]{1,0:T(8,128)(2,1)S(1)}, bf16[16,3584]{1,0:T(8,128)(2,1)S(1)}, u32[]{:S(2)}, u32[]{:S(2)}) collective-permute-start(bf16[16,3584]{1,0:T(8,128)(2,1)S(1)} %pad.4.refs_0_), channel_id=1, source_target_pairs={{0,80},{16,96},{32,112},{48,128},{64,144},{80,160},{96,176},{112,1... | collective-permute-start | bytes 344072 | tf_op jit(solution)/shard_map/ppermute | solution.py:49
  34.3 13.8 %collective-permute-start = (bf16[16,3584]{1,0:T(8,128)(2,1)S(1)}, bf16[16,3584]{1,0:T(8,128)(2,1)S(1)}, u32[]{:S(2)}, u32[]{:S(2)}) collective-permute-start(bf16[16,3584]{1,0:T(8,128)(2,1)S(1)} %pad.4.refs_0_), channel_id=1, source_target_pairs={{0,176},{16,192},{32,208},{48,224},{64,240},{80,0},{96,16},{112,32... | collective-permute-start | bytes 344072 | tf_op jit(solution)/shard_map/ppermute | solution.py:49
  48.2 16.5 %collective-permute-start.6 = (bf16[48,3584]{1,0:T(8,128)(2,1)S(1)}, bf16[48,3584]{1,0:T(8,128)(2,1)S(1)}, u32[]{:S(2)}, u32[]{:S(2)}) collective-permute-start(bf16[48,3584]{1,0:T(8,128)(2,1)S(1)} %shard_map.137.refs_0_), channel_id=1, source_target_pairs={{0,256},{256,0},{1,257},{257,1},{2,258},{258,2},{3,259},{259,3},{4... | collective-permute-start | bytes 1032200 | tf_op jit(solution)/shard_map/ppermute | solution.py:49
  50.1 17.7 %collective-permute-start.5 = (bf16[48,3584]{1,0:T(8,128)(2,1)S(1)}, bf16[48,3584]{1,0:T(8,128)(2,1)S(1)}, u32[]{:S(2)}, u32[]{:S(2)}) collective-permute-start(bf16[48,3584]{1,0:T(8,128)(2,1)S(1)} %shard_map.137.refs_0_), channel_id=1, source_target_pairs={{0,16},{16,32},{32,48},{48,64},{64,80},{80,96},{96,112},{112,128},... | collective-permute-start | bytes 1032200 | tf_op jit(solution)/shard_map/ppermute | solution.py:49
  52.0 16.7 %collective-permute-start.4 = (bf16[48,3584]{1,0:T(8,128)(2,1)S(1)}, bf16[48,3584]{1,0:T(8,128)(2,1)S(1)}, u32[]{:S(2)}, u32[]{:S(2)}) collective-permute-start(bf16[48,3584]{1,0:T(8,128)(2,1)S(1)} %shard_map.137.refs_0_), channel_id=1, source_target_pairs={{0,240},{16,0},{32,16},{48,32},{64,48},{80,64},{96,80},{112,96},{1... | collective-permute-start | bytes 1032200 | tf_op jit(solution)/shard_map/ppermute | solution.py:49
  68.7 34.6 %all-to-all-start.1 = ((bf16[16,16,1024]{2,1,0:T(8,128)(2,1)}), bf16[16,16,1024]{2,1,0:T(8,128)(2,1)S(1)}, u32[]{:S(2)}, u32[]{:S(2)}) async-start(bf16[16,16,1024]{2,1,0:T(8,128)(2,1)} %bitcast.1), calls=%async_computation.1 | async-start | bytes 1048576 | tf_op jit(solution)/shard_map/all_to_all | solution.py:235
  80.8 74.3 %collective-permute-start.12 = (bf16[448,3584]{1,0:T(8,128)(2,1)}, bf16[448,3584]{1,0:T(8,128)(2,1)}, u32[]{:S(2)}, u32[]{:S(2)}) collective-permute-start(bf16[448,3584]{1,0:T(8,128)(2,1)} %bitcast.10), channel_id=1, source_target_pairs={{0,8},{8,0},{1,9},{9,1},{2,10},{10,2},{3,11},{11,3},{4,12},{12,4},... | collective-permute-start | bytes 9633800 | tf_op jit(solution)/shard_map/ppermute | solution.py:49
  104.3 72.3 %all-to-all-start.2 = ((bf16[16,16,1024]{2,1,0:T(8,128)(2,1)}), bf16[16,16,1024]{2,1,0:T(8,128)(2,1)S(1)}, u32[]{:S(2)}, u32[]{:S(2)}) async-start(bf16[16,16,1024]{2,1,0:T(8,128)(2,1)} %broadcast_in_dim.32), calls=%async_computation.2 | async-start | bytes 1048576 | tf_op jit(solution)/shard_map/all_to_all | solution.py:244
  116.9 32.8 %collective-permute-start.10 = (bf16[96,3584]{1,0:T(8,128)(2,1)S(1)}, bf16[96,3584]{1,0:T(8,128)(2,1)S(1)}, u32[]{:S(2)}, u32[]{:S(2)}) collective-permute-start(bf16[96,3584]{1,0:T(8,128)(2,1)S(1)} %shard_map.138.refs_1_), channel_id=1, source_target_pairs={{0,256},{256,0},{1,257},{257,1},{2,258},{258,2},{3,259},{259,3},{4... | collective-permute-start | bytes 2064392 | tf_op jit(solution)/shard_map/ppermute | solution.py:49
  120.1 28.3 %collective-permute-start.8 = (bf16[48,3584]{1,0:T(8,128)(2,1)S(1)}, bf16[48,3584]{1,0:T(8,128)(2,1)S(1)}, u32[]{:S(2)}, u32[]{:S(2)}) collective-permute-start(bf16[48,3584]{1,0:T(8,128)(2,1)S(1)} %collective-permute-done.4.refs_0_), channel_id=1, source_target_pairs={{0,240},{16,0},{32,16},{48,32},{64,48},{80,64},{96,80},{112,96},{1... | collective-permute-start | bytes 1032200 | tf_op jit(solution)/shard_map/ppermute | solution.py:49
  124.6 25.0 %collective-permute-start.9 = (bf16[48,3584]{1,0:T(8,128)(2,1)S(1)}, bf16[48,3584]{1,0:T(8,128)(2,1)S(1)}, u32[]{:S(2)}, u32[]{:S(2)}) collective-permute-start(bf16[48,3584]{1,0:T(8,128)(2,1)S(1)} %collective-permute-done.5.refs_1_), channel_id=1, source_target_pairs={{0,16},{16,32},{32,48},{48,64},{64,80},{80,96},{96,112},{112,128},... | collective-permute-start | bytes 1032200 | tf_op jit(solution)/shard_map/ppermute | solution.py:49
  126.6 25.2 %collective-permute-start.7 = (bf16[16,3584]{1,0:T(8,128)(2,1)S(1)}, bf16[16,3584]{1,0:T(8,128)(2,1)S(1)}, u32[]{:S(2)}, u32[]{:S(2)}) collective-permute-start(bf16[16,3584]{1,0:T(8,128)(2,1)S(1)} %collective-permute-done.refs_1_), channel_id=1, source_target_pairs={{0,208},{16,224},{32,240},{48,0},{64,16},{80,32},{96,48},{112,64},... | collective-permute-start | bytes 344072 | tf_op jit(solution)/shard_map/ppermute | solution.py:49
  151.8 16.9 %collective-permute-start.11 = (bf16[112,3584]{1,0:T(8,128)(2,1)S(1)}, bf16[112,3584]{1,0:T(8,128)(2,1)S(1)}, u32[]{:S(2)}, u32[]{:S(2)}) collective-permute-start(bf16[112,3584]{1,0:T(8,128)(2,1)S(1)} %shard_map.139.refs_3_), channel_id=1, source_target_pairs={{0,256},{256,0},{1,257},{257,1},{2,258},{258,2},{3,259},{259,3},{4... | collective-permute-start | bytes 2408456 | tf_op jit(solution)/shard_map/ppermute | solution.py:49
  176.6 27.5 %all-to-all-start.3 = ((bf16[16,64,448]{2,1,0:T(8,128)(2,1)}), bf16[16,64,448]{2,1,0:T(8,128)(2,1)S(1)}, u32[]{:S(2)}, u32[]{:S(2)}) async-start(bf16[16,64,448]{2,1,0:T(8,128)(2,1)} %bitcast.5), calls=%async_computation.3 | async-start | bytes 2097152 | tf_op jit(solution)/shard_map/all_to_all | solution.py:259
  189.0 26.8 %copy-start.4 = (s32[64]{0:T(128)S(1)}, s32[64]{0:T(128)}, u32[]{:S(2)}) copy-start(s32[64]{0:T(128)} %constant.63.clone) | copy-start | bytes 772
  189.0 26.8 %copy-start.5 = (s32[64]{0:T(128)S(1)}, s32[64]{0:T(128)}, u32[]{:S(2)}) copy-start(s32[64]{0:T(128)} %constant.62.clone) | copy-start | bytes 772
  189.1 26.8 %copy-start.6 = (s32[64]{0:T(128)S(1)}, s32[64]{0:T(128)}, u32[]{:S(2)}) copy-start(s32[64]{0:T(128)} %constant.61.clone) | copy-start | bytes 772
  189.1 24.3 %collective-permute-start.13 = (bf16[256,1024]{1,0:T(8,128)(2,1)S(1)}, bf16[256,1024]{1,0:T(8,128)(2,1)S(1)}, u32[]{:S(2)}, u32[]{:S(2)}) collective-permute-start(bf16[256,1024]{1,0:T(8,128)(2,1)S(1)} %bitcast.6), channel_id=1, source_target_pairs={{0,256},{256,0},{1,257},{257,1},{2,258},{258,2},{3,259},{259,3},{4... | collective-permute-start | bytes 1572872 | tf_op jit(solution)/shard_map/ppermute | solution.py:49
  205.2 22.0 %all-to-all-start.4 = ((bf16[8,64,896]{2,1,0:T(8,128)(2,1)}), bf16[8,64,896]{2,1,0:T(8,128)(2,1)S(1)}, u32[]{:S(2)}, u32[]{:S(2)}) async-start(bf16[8,64,896]{2,1,0:T(8,128)(2,1)} %shard_map.141), calls=%async_computation.4 | async-start | bytes 1835008 | tf_op jit(solution)/shard_map/all_to_all | solution.py:268
  209.9 5.9 %collective-permute-start.14 = (bf16[256,1024]{1,0:T(8,128)(2,1)S(1)}, bf16[256,1024]{1,0:T(8,128)(2,1)}, u32[]{:S(2)}, u32[]{:S(2)}) collective-permute-start(bf16[256,1024]{1,0:T(8,128)(2,1)S(1)} %bitcast.7), channel_id=1, source_target_pairs={{0,8},{8,0},{1,9},{9,1},{2,10},{10,2},{3,11},{11,3},{4,12},{12,4},... | collective-permute-start | bytes 1572872 | tf_op jit(solution)/shard_map/ppermute | solution.py:49
  213.4 4.1 %collective-permute-start.15 = (bf16[256,1024]{1,0:T(8,128)(2,1)S(1)}, bf16[256,1024]{1,0:T(8,128)(2,1)}, u32[]{:S(2)}, u32[]{:S(2)}) collective-permute-start(bf16[256,1024]{1,0:T(8,128)(2,1)S(1)} %collective-permute-done.13.refs_1_), channel_id=1, source_target_pairs={{0,8},{8,0},{1,9},{9,1},{2,10},{10,2},{3,11},{11,3},{4,12},{12,4},... | collective-permute-start | bytes 1572872 | tf_op jit(solution)/shard_map/ppermute | solution.py:49
  (4 other events, 7.0 us)

commit v3 on v2

--- a/solution.py
+++ b/solution.py
@@ -205,8 +205,9 @@
         return ((x_me ^ order[:, 1]) * C + (core ^ order[:, 0])) * Z + lax.rem(z + order[:, 2] + Z, Z)
 
     own_basis = out_basis.T
-    own, inputs = lax.optimization_barrier((jnp.pad(grad_out, ((0, ROWS - OWN), (0, 0))), inputs))
+    own = lax.optimization_barrier(jnp.pad(grad_out, ((0, ROWS - OWN), (0, 0))))
     above, below = from_z(own, 5), from_z(own, -5)
+    above, below, inputs, eigen_values = lax.optimization_barrier((above, below, inputs, eigen_values))
     to_rows = ((c_me ^ OWNERS[:, 0]) * X + (x_me ^ OWNERS[:, 1])) * Z + OWNERS[:, 2]
     keep, send = pl.pallas_call(
         rotate_in_kernel,
@@ -218,31 +219,25 @@
             pltpu.VMEM((ALL, inputs.shape[1]), jnp.float32),
         ],
         compiler_params=params(),
-        cost_estimate=pl.CostEstimate(flops=3 * 10**10, bytes_accessed=3 * 10**6, transcendentals=0),
+        cost_estimate=pl.CostEstimate(flops=3 * 10**8, bytes_accessed=3 * 10**6, transcendentals=0),
     )(to_rows, inputs, in_basis)
     part = keep + f32(shift(send, "core", 1))
-    part_x = shift(half(part[RUN:]), "x_lo", 1)
     local_sum = jnp.full((N, 128), jnp.sum(eigen_values, dtype=jnp.float32))
     narrow_sum = jnp.sum(lax.all_to_all(local_sum, NARROW, 0, 0, tiled=True)[:, 0])
-    above, below, part, part_x, narrow_sum = lax.optimization_barrier((above, below, part, part_x, narrow_sum))
 
     near = stack(own, above, below)
     up, down, near_x = from_z(near, 1), from_z(near, -1), shift(near, "x_lo", 1)
     across = from_z(above, 3)
     other_basis = shift(own_basis, "core", 1)
-    part = half(part[:RUN] + f32(part_x))
-    up, down, near_x, part = lax.optimization_barrier((up, down, near_x, part))
-    pieces = lax.all_to_all(part, ZZ, 0, 0, tiled=True)
+    part = half(part[:RUN] + f32(shift(half(part[RUN:]), "x_lo", 1)))
+    up, down, near_x, across, narrow_sum = lax.optimization_barrier((up, down, near_x, across, narrow_sum))
     mid = stack(up, down)
-    *far, mid_x = lax.optimization_barrier((from_z(up, 1), from_z(down, -1), shift(mid, "x_lo", 1)))
-    far = stack(across, *far)
+    *far, mid_x, part = lax.optimization_barrier((from_z(up, 1), from_z(down, -1), shift(mid, "x_lo", 1), part))
+    far, part = lax.optimization_barrier((stack(across, *far), part))
     far_x = shift(far, "x_lo", 1)
     blocks = [near, mid, near_x, far, mid_x, far_x]
 
-    own_in = jnp.sum(f32(pieces.reshape(Z, ROWS, n_in)), 0)
-    own_in = half(with_terms(own_in, narrow_sum))
-    column = lax.all_to_all(jnp.broadcast_to(own_in, (Z,) + own_in.shape), ZZ, 0, 0, tiled=True)
-
+    pieces = lax.all_to_all(part, ZZ, 0, 0, tiled=True)
     partial_out = pl.pallas_call(
         rotate_out_kernel,
         out_shape=jax.ShapeDtypeStruct((ALL, n_out), jnp.bfloat16),
@@ -252,7 +247,10 @@
         compiler_params=params(),
         cost_estimate=pl.CostEstimate(flops=33 * 10**8, bytes_accessed=10**7, transcendentals=0),
     )(c_me.astype(jnp.int32).reshape(1), *blocks, own_basis, other_basis)
-    column, partial_out = lax.optimization_barrier((column.reshape(RUN, n_in), partial_out))
+    pieces, partial_out = lax.optimization_barrier((pieces, partial_out))
+    own_in = jnp.sum(f32(pieces.reshape(Z, ROWS, n_in)), 0)
+    own_in = half(with_terms(own_in, narrow_sum))
+    column = lax.all_to_all(jnp.broadcast_to(own_in, (Z,) + own_in.shape), ZZ, 0, 0, tiled=True).reshape(RUN, n_in)
     column_x = shift(column, "x_lo", 1)
     rotated_in = [column, column_x, shift(column, "core", 1), shift(column_x, "core", 1)]
 

time: 280 us -> 274 us (0.979)
  starting transfers between devices: 115 us -> 86.8 us
  blocking collectives: 45.7 us -> 70.7 us
  waiting for transfers between devices: 88.6 us -> 77 us
  local copies, waits for them, and re-layouts: 6.26 us -> 9.83 us
    all_to_all x0 -> x1, blocking collectives: none -> 31.8 us  [on_device(): lax.all_to_all(jnp.broadcast_to(own_in, (Z,) + own_in.shape), ZZ, 0, 0, t...]
    all_to_all x1, waiting for transfers between devices: 17.1 us -> 0.01 us  [on_device(): pieces = lax.all_to_all(part, ZZ, 0, 0, tiled=True)]
    ppermute x16, starting transfers between devices: 70 us -> 57.2 us  [shift(): return lax.ppermute(x, axis, [(i, (i + by) % size) for i in range(size)])]
    all_to_all x1 -> x0, starting transfers between devices: 12.5 us -> none  [on_device(): lax.all_to_all(jnp.broadcast_to(own_in, (Z,) + own_in.shape), ZZ, 0, 0, t...]
    all_to_all x1, starting transfers between devices: 12.2 us -> 3.61 us  [on_device(): pieces = lax.all_to_all(part, ZZ, 0, 0, tiled=True)]
    all_to_all x2, blocking collectives: 36.7 us -> 29.9 us  [on_device(): lax.all_to_all(jnp.broadcast_to(scores, (8,) + scores.shape), axes, 0, 0,...]
    ppermute x16, waiting for transfers between devices: 49 us -> 52.2 us  [shift(): return lax.ppermute(x, axis, [(i, (i + by) % size) for i in range(size)])]
    all_to_all x1, starting transfers between devices: 3.31 us -> 6.35 us  [on_device(): lax.all_to_all(local_sum, NARROW, 0, 0, tiled=True)[:, 0]]
  transfers between devices with their start and end apart: 21 -> 20, of which waited for: 13 -> 10; matrix products, arithmetic and copies ran while one was open for 2% -> 4% of each run, Pallas kernels for 3% -> 4%
where the time goes in v3:
time: 274 us; the launch traced here: 272 us
  starting transfers between devices  86.8 us (32%)
  waiting for transfers between devices  77 us (28%)
  blocking collectives  70.7 us (26%)
  Pallas kernels  17.9 us (7%)
  local copies, waits for them, and re-layouts  9.83 us (4%)
  other arithmetic  8.45 us (3%)
    ppermute x16, starting transfers between devices, shift(): return lax.ppermute(x, axis, [(i, (i + by) % size) for i in range(size)])  57.2 us
    ppermute x16, waiting for transfers between devices, shift(): return lax.ppermute(x, axis, [(i, (i + by) % size) for i in range(size)])  52.2 us
    all_to_all x1, blocking collectives, on_device(): lax.all_to_all(jnp.broadcast_to(own_in, (Z,) + own_in.shape), ZZ, 0, 0, t...  31.8 us
    all_to_all x2, blocking collectives, on_device(): lax.all_to_all(jnp.broadcast_to(scores, (8,) + scores.shape), axes, 0, 0,...  29.9 us
    all_to_all x1, starting transfers between devices, on_device(): parts = lax.all_to_all(partial_out, ('core',) + NARROW, 0, 0, tiled=True)  14.9 us
    all_to_all x1, waiting for transfers between devices, on_device(): parts = lax.all_to_all(partial_out, ('core',) + NARROW, 0, 0, tiled=True)  13 us
    all_to_all x1, waiting for transfers between devices, on_device(): rotated_out = lax.all_to_all(shares, NARROW, 0, 0, tiled=True)  11.8 us
    all_to_all x1, blocking collectives, on_device(): scores = jnp.sum(lax.all_to_all(scores, NARROW, 0, 0, tiled=True), 0)  9.03 us
  transfers between devices with their start and end apart: 20, of which 10 were waited for; matrix products, arithmetic and copies ran while one was open for 4% of the time, Pallas kernels for 4%

profile of v3, /device:TPU:1, one launch (start us, length us, event | category | flops | bytes accessed | tf_op | source)
XLA Modules:
  0.0 272.2 jit_solution(5008152840336190243)
XLA Ops:
  1.0 14.9 %collective-permute-start = (bf16[16,3584]{1,0:T(8,128)(2,1)S(1)}, bf16[16,3584]{1,0:T(8,128)(2,1)S(1)}, u32[]{:S(2)}, u32[]{:S(2)}) collective-permute-start(bf16[16,3584]{1,0:T(8,128)(2,1)S(1)} %pad.4.refs_0_), channel_id=1, source_target_pairs={{0,176},{16,192},{32,208},{48,224},{64,240},{80,0},{96,16},{112,32... | collective-permute-start | bytes 344072 | tf_op jit(solution)/shard_map/ppermute | solution.py:49
  18.6 9.2 %collective-permute-done.refs_1_ = bf16[16,3584]{1,0:T(8,128)(2,1)S(1)} collective-permute-done((bf16[16,3584]{1,0:T(8,128)(2,1)S(1)}, bf16[16,3584]{1,0:T(8,128)(2,1)S(1)}, u32[]{:S(2)}, u32[]{:S(2)}) %collective-permute-start) | collective-permute-done | bytes 114720 | tf_op jit(solution)/shard_map/ppermute | solution.py:49
  27.9 4.6 %collective-permute-done.1.refs_2_ = bf16[16,3584]{1,0:T(8,128)(2,1)S(1)} collective-permute-done((bf16[16,3584]{1,0:T(8,128)(2,1)S(1)}, bf16[16,3584]{1,0:T(8,128)(2,1)S(1)}, u32[]{:S(2)}, u32[]{:S(2)}) %collective-permute-start.1) | collective-permute-done | bytes 114720 | tf_op jit(solution)/shard_map/ppermute | solution.py:49
  37.3 8.0 %collective-permute-start.9 = (bf16[512,1024]{1,0:T(8,128)(2,1)}, bf16[512,1024]{1,0:T(8,128)(2,1)}, u32[]{:S(2)}, u32[]{:S(2)}) collective-permute-start(bf16[512,1024]{1,0:T(8,128)(2,1)} %get-tuple-element.32), channel_id=1, source_target_pairs={{0,8},{8,0},{1,9},{9,1},{2,10},{10,2},{3,11},{11,3},{4,12},{12,4},... | collective-permute-start | bytes 3145736 | tf_op jit(solution)/shard_map/ppermute | solution.py:49
  51.2 3.2 %collective-permute-start.3 = (bf16[48,3584]{1,0:T(8,128)(2,1)S(1)}, bf16[48,3584]{1,0:T(8,128)(2,1)}, u32[]{:S(2)}, u32[]{:S(2)}) collective-permute-start(bf16[48,3584]{1,0:T(8,128)(2,1)S(1)} %shard_map.136.refs_0_), channel_id=1, source_target_pairs={{0,16},{16,32},{32,48},{48,64},{64,80},{80,96},{96,112},{112,128},... | collective-permute-start | bytes 1032200 | tf_op jit(solution)/shard_map/ppermute | solution.py:49
  54.3 3.1 %collective-permute-start.4 = (bf16[48,3584]{1,0:T(8,128)(2,1)S(1)}, bf16[48,3584]{1,0:T(8,128)(2,1)}, u32[]{:S(2)}, u32[]{:S(2)}) collective-permute-start(bf16[48,3584]{1,0:T(8,128)(2,1)S(1)} %shard_map.136.refs_0_), channel_id=1, source_target_pairs={{0,256},{256,0},{1,257},{257,1},{2,258},{258,2},{3,259},{259,3},{4... | collective-permute-start | bytes 1032200 | tf_op jit(solution)/shard_map/ppermute | solution.py:49
  59.8 6.4 %all-to-all-start = ((f32[8,1,128]{2,1,0:T(1,128)}), f32[8,1,128]{2,1,0:T(1,128)S(1)}, u32[]{:S(2)}, u32[]{:S(2)}) async-start(f32[8,1,128]{2,1,0:T(1,128)} %broadcast_in_dim.27), calls=%async_computation | async-start | bytes 8192 | tf_op jit(solution)/shard_map/all_to_all | solution.py:226
  72.2 7.1 %collective-permute-done.5.refs_0_ = bf16[16,3584]{1,0:T(8,128)(2,1)S(1)} collective-permute-done((bf16[16,3584]{1,0:T(8,128)(2,1)}, bf16[16,3584]{1,0:T(8,128)(2,1)S(1)}, u32[]{:S(2)}, u32[]{:S(2)}) %collective-permute-start.5) | collective-permute-done | bytes 114720 | tf_op jit(solution)/shard_map/ppermute | solution.py:49
  83.1 3.4 %collective-permute-start.8 = (bf16[96,3584]{1,0:T(8,128)(2,1)S(1)}, bf16[96,3584]{1,0:T(8,128)(2,1)S(1)}, u32[]{:S(2)}, u32[]{:S(2)}) collective-permute-start(bf16[96,3584]{1,0:T(8,128)(2,1)S(1)} %shard_map.137.refs_1_), channel_id=1, source_target_pairs={{0,256},{256,0},{1,257},{257,1},{2,258},{258,2},{3,259},{259,3},{4... | collective-permute-start | bytes 2064392 | tf_op jit(solution)/shard_map/ppermute | solution.py:49
  88.4 3.4 %collective-permute-start.7 = (bf16[48,3584]{1,0:T(8,128)(2,1)}, bf16[48,3584]{1,0:T(8,128)(2,1)S(1)}, u32[]{:S(2)}, u32[]{:S(2)}) collective-permute-start(bf16[48,3584]{1,0:T(8,128)(2,1)} %collective-permute-done.3.refs_1_), channel_id=1, source_target_pairs={{0,16},{16,32},{32,48},{48,64},{64,80},{80,96},{96,112},{112,128},... | collective-permute-start | bytes 1032200 | tf_op jit(solution)/shard_map/ppermute | solution.py:49
  97.8 11.1 %collective-permute-done.8.refs_4_ = bf16[96,3584]{1,0:T(8,128)(2,1)S(1)} collective-permute-done((bf16[96,3584]{1,0:T(8,128)(2,1)S(1)}, bf16[96,3584]{1,0:T(8,128)(2,1)S(1)}, u32[]{:S(2)}, u32[]{:S(2)}) %collective-permute-start.8) | collective-permute-done | bytes 688160 | tf_op jit(solution)/shard_map/ppermute | solution.py:49
  109.7 3.6 %all-to-all-start.1 = ((bf16[16,16,1024]{2,1,0:T(8,128)(2,1)}), bf16[16,16,1024]{2,1,0:T(8,128)(2,1)S(1)}, u32[]{:S(2)}, u32[]{:S(2)}) async-start(bf16[16,16,1024]{2,1,0:T(8,128)(2,1)} %bitcast.12), calls=%async_computation.1 | async-start | bytes 1048576 | tf_op jit(solution)/shard_map/all_to_all | solution.py:240
  116.7 16.3 %collective-permute-done.11.refs_5_ = bf16[112,3584]{1,0:T(8,128)(2,1)} collective-permute-done((bf16[112,3584]{1,0:T(8,128)(2,1)S(1)}, bf16[112,3584]{1,0:T(8,128)(2,1)}, u32[]{:S(2)}, u32[]{:S(2)}) %collective-permute-start.11) | collective-permute-done | bytes 802848 | tf_op jit(solution)/shard_map/ppermute | solution.py:49
  134.2 8.2 %shard_map.140 = bf16[1024,448]{1,0:T(8,128)(2,1)} custom-call(s32[1]{0:T(128)} %bitcast.3.core_ref, bf16[48,3584]{1,0:T(8,128)(2,1)S(1)} %shard_map.136.refs_0_, bf16[96,3584]{1,0:T(8,128)(2,1)S(1)} %shard_map.137.refs_1_, bf16[48,3584]{1,0:T(8,128)(2,1)} %collective-permute-done.4.refs_2_, bf16[112,3584]{1,0:T(8,128)(2,1)S(1)} %shard_map.139.refs_3_, ...), custom_call_target="tpu_custom_call" | custom-call | flops 3300000000 | bytes 10000000 | tf_op jit(solution)/shard_map/pallas_call | solution.py:241
  142.5 31.8 %all_to_all.55 = bf16[16,16,1024]{2,1,0:T(8,128)(2,1)S(1)} all-to-all(bf16[16,16,1024]{2,1,0:T(8,128)(2,1)S(1)} %broadcast_in_dim.32), channel_id=1, replica_groups=mesh['x_lo'=2,'zh'=4,'zl'=4,'core'=2,'y'=4,'x_hi'=2] {'zh','zl'}, dimensions={0} | all-to-all | bytes 1048576 | tf_op jit(solution)/shard_map/all_to_all | solution.py:253
  174.3 14.9 %all-to-all-start.2 = ((bf16[16,64,448]{2,1,0:T(8,128)(2,1)}), bf16[16,64,448]{2,1,0:T(8,128)(2,1)S(1)}, u32[]{:S(2)}, u32[]{:S(2)}) async-start(bf16[16,64,448]{2,1,0:T(8,128)(2,1)} %bitcast.5), calls=%async_computation.2 | async-start | bytes 2097152 | tf_op jit(solution)/shard_map/all_to_all | solution.py:257
  191.3 13.0 %all-to-all-done.2.parts_ref = bf16[16,64,448]{2,1,0:T(8,128)(2,1)S(1)} async-done(((bf16[16,64,448]{2,1,0:T(8,128)(2,1)}), bf16[16,64,448]{2,1,0:T(8,128)(2,1)S(1)}, u32[]{:S(2)}, u32[]{:S(2)}) %all-to-all-start.2) | async-done | bytes 917536 | tf_op jit(solution)/shard_map/all_to_all | solution.py:257
  205.4 4.7 %all-to-all-start.3 = ((bf16[8,64,896]{2,1,0:T(8,128)(2,1)}), bf16[8,64,896]{2,1,0:T(8,128)(2,1)S(1)}, u32[]{:S(2)}, u32[]{:S(2)}) async-start(bf16[8,64,896]{2,1,0:T(8,128)(2,1)} %shard_map.141), calls=%async_computation.3 | async-start | bytes 1835008 | tf_op jit(solution)/shard_map/all_to_all | solution.py:266
  210.1 3.4 %collective-permute-start.14 = (bf16[256,1024]{1,0:T(8,128)(2,1)S(1)}, bf16[256,1024]{1,0:T(8,128)(2,1)}, u32[]{:S(2)}, u32[]{:S(2)}) collective-permute-start(bf16[256,1024]{1,0:T(8,128)(2,1)S(1)} %bitcast.10), channel_id=1, source_target_pairs={{0,8},{8,0},{1,9},{9,1},{2,10},{10,2},{3,11},{11,3},{4,12},{12,4},... | collective-permute-start | bytes 1572872 | tf_op jit(solution)/shard_map/ppermute | solution.py:49
  215.7 11.8 %all-to-all-done.3.ro_ref = bf16[8,64,896]{2,1,0:T(8,128)(2,1)S(1)} async-done(((bf16[8,64,896]{2,1,0:T(8,128)(2,1)}), bf16[8,64,896]{2,1,0:T(8,128)(2,1)S(1)}, u32[]{:S(2)}, u32[]{:S(2)}) %all-to-all-start.3) | async-done | bytes 917536 | tf_op jit(solution)/shard_map/all_to_all | solution.py:266
  227.5 5.1 %shard_map.142 = f32[8,4,384]{2,1,0:T(4,128)S(1)} custom-call(s32[64]{0:T(128)S(1)} %fusion.3.to_out_ref, s32[64]{0:T(128)S(1)} %get-tuple-element.44.to_in_ref, bf16[8,64,896]{2,1,0:T(8,128)(2,1)S(1)} %all-to-all-done.3.ro_ref, bf16[256,1024]{1,0:T(8,128)(2,1)S(1)} %bitcast.11, bf16[256,1024]{1,0:T(8,128)(2,1)S(1)} %collective-permute-done.13.refs_1_, ...), custom_call_target="tpu_custom_call" | custom-call | flops 3000000000 | bytes 5000000 | tf_op jit(solution)/shard_map/pallas_call | solution.py:268
  232.7 9.0 %all_to_all.56 = f32[8,4,384]{2,1,0:T(4,128)S(1)} all-to-all(f32[8,4,384]{2,1,0:T(4,128)S(1)} %shard_map.142), channel_id=1, replica_groups=mesh['x_lo'=2,'zh'=4,'zl'=4,'core'=2,'y'=4,'x_hi'=2] {'y','x_hi'}, dimensions={0} | all-to-all | bytes 98304 | tf_op jit(solution)/shard_map/all_to_all | solution.py:277
  241.7 12.8 %all_to_all.57 = f32[8,4,384]{2,1,0:T(4,128)S(1)} all-to-all(f32[8,4,384]{2,1,0:T(4,128)S(1)} %broadcast_in_dim.33), channel_id=1, replica_groups=mesh['x_lo'=2,'zh'=4,'zl'=4,'core'=2,'y'=4,'x_hi'=2] {'zl','core'}, dimensions={0} | all-to-all | bytes 98304 | tf_op jit(solution)/shard_map/all_to_all | solution.py:279
  254.5 17.1 %all_to_all.58 = f32[8,4,384]{2,1,0:T(4,128)S(1)} all-to-all(f32[8,4,384]{2,1,0:T(4,128)S(1)} %broadcast_in_dim.34), channel_id=1, replica_groups=mesh['x_lo'=2,'zh'=4,'zl'=4,'core'=2,'y'=4,'x_hi'=2] {'x_lo','zh'}, dimensions={0} | all-to-all | bytes 98304 | tf_op jit(solution)/shard_map/all_to_all | solution.py:279
  (71 shorter events, 44.5 us)
Async XLA Ops:
  0.0 57.5 %copy-start = (bf16[448,1024]{1,0:T(8,128)(2,1)S(1)}, bf16[448,1024]{1,0:T(8,128)(2,1)}, u32[]{:S(2)}) copy-start(bf16[448,1024]{1,0:T(8,128)(2,1)} %refs_4_) | copy-start | bytes 2752516
  1.0 26.9 %collective-permute-start = (bf16[16,3584]{1,0:T(8,128)(2,1)S(1)}, bf16[16,3584]{1,0:T(8,128)(2,1)S(1)}, u32[]{:S(2)}, u32[]{:S(2)}) collective-permute-start(bf16[16,3584]{1,0:T(8,128)(2,1)S(1)} %pad.4.refs_0_), channel_id=1, source_target_pairs={{0,176},{16,192},{32,208},{48,224},{64,240},{80,0},{96,16},{112,32... | collective-permute-start | bytes 344072 | tf_op jit(solution)/shard_map/ppermute | solution.py:49
  15.9 16.5 %collective-permute-start.1 = (bf16[16,3584]{1,0:T(8,128)(2,1)S(1)}, bf16[16,3584]{1,0:T(8,128)(2,1)S(1)}, u32[]{:S(2)}, u32[]{:S(2)}) collective-permute-start(bf16[16,3584]{1,0:T(8,128)(2,1)S(1)} %pad.4.refs_0_), channel_id=1, source_target_pairs={{0,80},{16,96},{32,112},{48,128},{64,144},{80,160},{96,176},{112,1... | collective-permute-start | bytes 344072 | tf_op jit(solution)/shard_map/ppermute | solution.py:49
  37.3 28.9 %collective-permute-start.9 = (bf16[512,1024]{1,0:T(8,128)(2,1)}, bf16[512,1024]{1,0:T(8,128)(2,1)}, u32[]{:S(2)}, u32[]{:S(2)}) collective-permute-start(bf16[512,1024]{1,0:T(8,128)(2,1)} %get-tuple-element.32), channel_id=1, source_target_pairs={{0,8},{8,0},{1,9},{9,1},{2,10},{10,2},{3,11},{11,3},{4,12},{12,4},... | collective-permute-start | bytes 3145736 | tf_op jit(solution)/shard_map/ppermute | solution.py:49
  45.3 87.8 %collective-permute-start.12 = (bf16[448,3584]{1,0:T(8,128)(2,1)}, bf16[448,3584]{1,0:T(8,128)(2,1)}, u32[]{:S(2)}, u32[]{:S(2)}) collective-permute-start(bf16[448,3584]{1,0:T(8,128)(2,1)} %bitcast.14), channel_id=1, source_target_pairs={{0,8},{8,0},{1,9},{9,1},{2,10},{10,2},{3,11},{11,3},{4,12},{12,4},... | collective-permute-start | bytes 9633800 | tf_op jit(solution)/shard_map/ppermute | solution.py:49
  49.0 32.9 %collective-permute-start.2 = (bf16[48,3584]{1,0:T(8,128)(2,1)S(1)}, bf16[48,3584]{1,0:T(8,128)(2,1)}, u32[]{:S(2)}, u32[]{:S(2)}) collective-permute-start(bf16[48,3584]{1,0:T(8,128)(2,1)S(1)} %shard_map.136.refs_0_), channel_id=1, source_target_pairs={{0,240},{16,0},{32,16},{48,32},{64,48},{80,64},{96,80},{112,96},{1... | collective-permute-start | bytes 1032200 | tf_op jit(solution)/shard_map/ppermute | solution.py:49
  51.2 30.8 %collective-permute-start.3 = (bf16[48,3584]{1,0:T(8,128)(2,1)S(1)}, bf16[48,3584]{1,0:T(8,128)(2,1)}, u32[]{:S(2)}, u32[]{:S(2)}) collective-permute-start(bf16[48,3584]{1,0:T(8,128)(2,1)S(1)} %shard_map.136.refs_0_), channel_id=1, source_target_pairs={{0,16},{16,32},{32,48},{48,64},{64,80},{80,96},{96,112},{112,128},... | collective-permute-start | bytes 1032200 | tf_op jit(solution)/shard_map/ppermute | solution.py:49
  54.3 27.6 %collective-permute-start.4 = (bf16[48,3584]{1,0:T(8,128)(2,1)S(1)}, bf16[48,3584]{1,0:T(8,128)(2,1)}, u32[]{:S(2)}, u32[]{:S(2)}) collective-permute-start(bf16[48,3584]{1,0:T(8,128)(2,1)S(1)} %shard_map.136.refs_0_), channel_id=1, source_target_pairs={{0,256},{256,0},{1,257},{257,1},{2,258},{258,2},{3,259},{259,3},{4... | collective-permute-start | bytes 1032200 | tf_op jit(solution)/shard_map/ppermute | solution.py:49
  59.8 21.6 %all-to-all-start = ((f32[8,1,128]{2,1,0:T(1,128)}), f32[8,1,128]{2,1,0:T(1,128)S(1)}, u32[]{:S(2)}, u32[]{:S(2)}) async-start(f32[8,1,128]{2,1,0:T(1,128)} %broadcast_in_dim.27), calls=%async_computation | async-start | bytes 8192 | tf_op jit(solution)/shard_map/all_to_all | solution.py:226
  66.1 13.3 %collective-permute-start.5 = (bf16[16,3584]{1,0:T(8,128)(2,1)}, bf16[16,3584]{1,0:T(8,128)(2,1)S(1)}, u32[]{:S(2)}, u32[]{:S(2)}) collective-permute-start(bf16[16,3584]{1,0:T(8,128)(2,1)} %copy-done.1), channel_id=1, source_target_pairs={{0,208},{16,224},{32,240},{48,0},{64,16},{80,32},{96,48},{112,64},... | collective-permute-start | bytes 344072 | tf_op jit(solution)/shard_map/ppermute | solution.py:49
  79.4 14.9 %collective-permute-start.10 = (bf16[256,1024]{1,0:T(8,128)(2,1)S(1)}, bf16[256,1024]{1,0:T(8,128)(2,1)}, u32[]{:S(2)}, u32[]{:S(2)}) collective-permute-start(bf16[256,1024]{1,0:T(8,128)(2,1)S(1)} %slice.20), channel_id=1, source_target_pairs={{0,256},{256,0},{1,257},{257,1},{2,258},{258,2},{3,259},{259,3},{4... | collective-permute-start | bytes 1572872 | tf_op jit(solution)/shard_map/ppermute | solution.py:49
  83.1 25.8 %collective-permute-start.8 = (bf16[96,3584]{1,0:T(8,128)(2,1)S(1)}, bf16[96,3584]{1,0:T(8,128)(2,1)S(1)}, u32[]{:S(2)}, u32[]{:S(2)}) collective-permute-start(bf16[96,3584]{1,0:T(8,128)(2,1)S(1)} %shard_map.137.refs_1_), channel_id=1, source_target_pairs={{0,256},{256,0},{1,257},{257,1},{2,258},{258,2},{3,259},{259,3},{4... | collective-permute-start | bytes 2064392 | tf_op jit(solution)/shard_map/ppermute | solution.py:49
  86.4 10.5 %collective-permute-start.6 = (bf16[48,3584]{1,0:T(8,128)(2,1)}, bf16[48,3584]{1,0:T(8,128)(2,1)S(1)}, u32[]{:S(2)}, u32[]{:S(2)}) collective-permute-start(bf16[48,3584]{1,0:T(8,128)(2,1)} %collective-permute-done.2.refs_0_), channel_id=1, source_target_pairs={{0,240},{16,0},{32,16},{48,32},{64,48},{80,64},{96,80},{112,96},{1... | collective-permute-start | bytes 1032200 | tf_op jit(solution)/shard_map/ppermute | solution.py:49
  88.4 9.4 %collective-permute-start.7 = (bf16[48,3584]{1,0:T(8,128)(2,1)}, bf16[48,3584]{1,0:T(8,128)(2,1)S(1)}, u32[]{:S(2)}, u32[]{:S(2)}) collective-permute-start(bf16[48,3584]{1,0:T(8,128)(2,1)} %collective-permute-done.3.refs_1_), channel_id=1, source_target_pairs={{0,16},{16,32},{32,48},{48,64},{64,80},{80,96},{96,112},{112,128},... | collective-permute-start | bytes 1032200 | tf_op jit(solution)/shard_map/ppermute | solution.py:49
  109.7 32.6 %all-to-all-start.1 = ((bf16[16,16,1024]{2,1,0:T(8,128)(2,1)}), bf16[16,16,1024]{2,1,0:T(8,128)(2,1)S(1)}, u32[]{:S(2)}, u32[]{:S(2)}) async-start(bf16[16,16,1024]{2,1,0:T(8,128)(2,1)} %bitcast.12), calls=%async_computation.1 | async-start | bytes 1048576 | tf_op jit(solution)/shard_map/all_to_all | solution.py:240
  113.4 19.7 %collective-permute-start.11 = (bf16[112,3584]{1,0:T(8,128)(2,1)S(1)}, bf16[112,3584]{1,0:T(8,128)(2,1)}, u32[]{:S(2)}, u32[]{:S(2)}) collective-permute-start(bf16[112,3584]{1,0:T(8,128)(2,1)S(1)} %shard_map.139.refs_3_), channel_id=1, source_target_pairs={{0,256},{256,0},{1,257},{257,1},{2,258},{258,2},{3,259},{259,3},{4... | collective-permute-start | bytes 2408456 | tf_op jit(solution)/shard_map/ppermute | solution.py:49
  174.3 30.0 %all-to-all-start.2 = ((bf16[16,64,448]{2,1,0:T(8,128)(2,1)}), bf16[16,64,448]{2,1,0:T(8,128)(2,1)S(1)}, u32[]{:S(2)}, u32[]{:S(2)}) async-start(bf16[16,64,448]{2,1,0:T(8,128)(2,1)} %bitcast.5), calls=%async_computation.2 | async-start | bytes 2097152 | tf_op jit(solution)/shard_map/all_to_all | solution.py:257
  189.2 26.4 %copy-start.9 = (s32[64]{0:T(128)S(1)}, s32[64]{0:T(128)}, u32[]{:S(2)}) copy-start(s32[64]{0:T(128)} %constant.63.clone) | copy-start | bytes 772
  189.2 26.4 %copy-start.10 = (s32[64]{0:T(128)S(1)}, s32[64]{0:T(128)}, u32[]{:S(2)}) copy-start(s32[64]{0:T(128)} %constant.62.clone) | copy-start | bytes 772
  189.3 26.4 %copy-start.11 = (s32[64]{0:T(128)S(1)}, s32[64]{0:T(128)}, u32[]{:S(2)}) copy-start(s32[64]{0:T(128)} %constant.61.clone) | copy-start | bytes 772
  189.3 24.3 %collective-permute-start.13 = (bf16[256,1024]{1,0:T(8,128)(2,1)S(1)}, bf16[256,1024]{1,0:T(8,128)(2,1)S(1)}, u32[]{:S(2)}, u32[]{:S(2)}) collective-permute-start(bf16[256,1024]{1,0:T(8,128)(2,1)S(1)} %bitcast.9), channel_id=1, source_target_pairs={{0,256},{256,0},{1,257},{257,1},{2,258},{258,2},{3,259},{259,3},{4... | collective-permute-start | bytes 1572872 | tf_op jit(solution)/shard_map/ppermute | solution.py:49
  205.4 22.1 %all-to-all-start.3 = ((bf16[8,64,896]{2,1,0:T(8,128)(2,1)}), bf16[8,64,896]{2,1,0:T(8,128)(2,1)S(1)}, u32[]{:S(2)}, u32[]{:S(2)}) async-start(bf16[8,64,896]{2,1,0:T(8,128)(2,1)} %shard_map.141), calls=%async_computation.3 | async-start | bytes 1835008 | tf_op jit(solution)/shard_map/all_to_all | solution.py:266
  210.1 17.4 %collective-permute-start.14 = (bf16[256,1024]{1,0:T(8,128)(2,1)S(1)}, bf16[256,1024]{1,0:T(8,128)(2,1)}, u32[]{:S(2)}, u32[]{:S(2)}) collective-permute-start(bf16[256,1024]{1,0:T(8,128)(2,1)S(1)} %bitcast.10), channel_id=1, source_target_pairs={{0,8},{8,0},{1,9},{9,1},{2,10},{10,2},{3,11},{11,3},{4,12},{12,4},... | collective-permute-start | bytes 1572872 | tf_op jit(solution)/shard_map/ppermute | solution.py:49
  213.6 14.0 %collective-permute-start.15 = (bf16[256,1024]{1,0:T(8,128)(2,1)S(1)}, bf16[256,1024]{1,0:T(8,128)(2,1)}, u32[]{:S(2)}, u32[]{:S(2)}) collective-permute-start(bf16[256,1024]{1,0:T(8,128)(2,1)S(1)} %collective-permute-done.13.refs_1_), channel_id=1, source_target_pairs={{0,8},{8,0},{1,9},{9,1},{2,10},{10,2},{3,11},{11,3},{4,12},{12,4},... | collective-permute-start | bytes 1572872 | tf_op jit(solution)/shard_map/ppermute | solution.py:49
  (8 other events, 10.9 us)

commit v4 on v3

--- a/solution.py
+++ b/solution.py
@@ -207,7 +207,6 @@
     own_basis = out_basis.T
     own = lax.optimization_barrier(jnp.pad(grad_out, ((0, ROWS - OWN), (0, 0))))
     above, below = from_z(own, 5), from_z(own, -5)
-    above, below, inputs, eigen_values = lax.optimization_barrier((above, below, inputs, eigen_values))
     to_rows = ((c_me ^ OWNERS[:, 0]) * X + (x_me ^ OWNERS[:, 1])) * Z + OWNERS[:, 2]
     keep, send = pl.pallas_call(
         rotate_in_kernel,
@@ -221,7 +220,8 @@
         compiler_params=params(),
         cost_estimate=pl.CostEstimate(flops=3 * 10**8, bytes_accessed=3 * 10**6, transcendentals=0),
     )(to_rows, inputs, in_basis)
-    part = keep + f32(shift(send, "core", 1))
+    above, below, sent, eigen_values = lax.optimization_barrier((above, below, shift(send, "core", 1), eigen_values))
+    part = keep + f32(sent)
     local_sum = jnp.full((N, 128), jnp.sum(eigen_values, dtype=jnp.float32))
     narrow_sum = jnp.sum(lax.all_to_all(local_sum, NARROW, 0, 0, tiled=True)[:, 0])
 
@@ -230,14 +230,19 @@
     across = from_z(above, 3)
     other_basis = shift(own_basis, "core", 1)
     part = half(part[:RUN] + f32(shift(half(part[RUN:]), "x_lo", 1)))
-    up, down, near_x, across, narrow_sum = lax.optimization_barrier((up, down, near_x, across, narrow_sum))
+    up, down, near_x = lax.optimization_barrier((up, down, near_x))
+    part, _ = lax.optimization_barrier((part, up))
     mid = stack(up, down)
-    *far, mid_x, part = lax.optimization_barrier((from_z(up, 1), from_z(down, -1), shift(mid, "x_lo", 1), part))
-    far, part = lax.optimization_barrier((stack(across, *far), part))
+    *far, mid_x, narrow_sum = lax.optimization_barrier((from_z(up, 1), from_z(down, -1), shift(mid, "x_lo", 1), narrow_sum))
+    far = stack(across, *far)
     far_x = shift(far, "x_lo", 1)
     blocks = [near, mid, near_x, far, mid_x, far_x]
 
-    pieces = lax.all_to_all(part, ZZ, 0, 0, tiled=True)
+    pieces, far = lax.optimization_barrier((lax.all_to_all(part, ZZ, 0, 0, tiled=True), far))
+    blocks[3] = far
+    own_in = jnp.sum(f32(pieces.reshape(Z, ROWS, n_in)), 0)
+    own_in = half(with_terms(own_in, narrow_sum))
+    column = lax.all_gather(own_in, ZZ, axis=0, tiled=True)
     partial_out = pl.pallas_call(
         rotate_out_kernel,
         out_shape=jax.ShapeDtypeStruct((ALL, n_out), jnp.bfloat16),
@@ -247,13 +252,7 @@
         compiler_params=params(),
         cost_estimate=pl.CostEstimate(flops=33 * 10**8, bytes_accessed=10**7, transcendentals=0),
     )(c_me.astype(jnp.int32).reshape(1), *blocks, own_basis, other_basis)
-    pieces, partial_out = lax.optimization_barrier((pieces, partial_out))
-    own_in = jnp.sum(f32(pieces.reshape(Z, ROWS, n_in)), 0)
-    own_in = half(with_terms(own_in, narrow_sum))
-    column = lax.all_to_all(jnp.broadcast_to(own_in, (Z,) + own_in.shape), ZZ, 0, 0, tiled=True).reshape(RUN, n_in)
-    column_x = shift(column, "x_lo", 1)
-    rotated_in = [column, column_x, shift(column, "core", 1), shift(column_x, "core", 1)]
-
+    partial_out, column = lax.optimization_barrier((partial_out, column))
     parts = lax.all_to_all(partial_out, ("core",) + NARROW, 0, 0, tiled=True)
     shares = pl.pallas_call(
         share_kernel,
@@ -263,6 +262,8 @@
         compiler_params=params(),
         cost_estimate=pl.CostEstimate(flops=10**6, bytes_accessed=2 * 10**6, transcendentals=0),
     )(parts.reshape(C * N, SHARE, n_out))
+    column_x = shift(column, "x_lo", 1)
+    rotated_in = [column, column_x, shift(column, "core", 1), shift(column_x, "core", 1)]
     rotated_out = lax.all_to_all(shares, NARROW, 0, 0, tiled=True)
 
     scores = pl.pallas_call(

time: 274 us -> 260 us (0.949)
  waiting for transfers between devices: 77 us -> 57.9 us
  starting transfers between devices: 86.8 us -> 96.1 us
    all_gather x0 -> x1, blocking collectives: none -> 31.8 us  [on_device(): column = lax.all_gather(own_in, ZZ, axis=0, tiled=True)]
    all_to_all x1 -> x0, blocking collectives: 31.8 us -> none  [on_device(): lax.all_to_all(jnp.broadcast_to(own_in, (Z,) + own_in.shape), ZZ, 0, 0, t...]
    ppermute x16, waiting for transfers between devices: 52.2 us -> 33 us  [shift(): return lax.ppermute(x, axis, [(i, (i + by) % size) for i in range(size)])]
    all_to_all x1, starting transfers between devices: 3.61 us -> 10.3 us  [on_device(): lax.all_to_all(part, ZZ, 0, 0, tiled=True)]
    ppermute x16, starting transfers between devices: 57.2 us -> 62.9 us  [shift(): return lax.ppermute(x, axis, [(i, (i + by) % size) for i in range(size)])]
    all_to_all x1, waiting for transfers between devices: 0.01 us -> 3.96 us  [on_device(): lax.all_to_all(local_sum, NARROW, 0, 0, tiled=True)[:, 0]]
    all_to_all x1, starting transfers between devices: 14.9 us -> 11.6 us  [on_device(): parts = lax.all_to_all(partial_out, ('core',) + NARROW, 0, 0, tiled=True)]
    all_to_all x1, waiting for transfers between devices: 11.8 us -> 9.02 us  [on_device(): rotated_out = lax.all_to_all(shares, NARROW, 0, 0, tiled=True)]
  transfers between devices with their start and end apart: 20 -> 20, of which waited for: 10 -> 9; matrix products, arithmetic and copies ran while one was open for 4% -> 3% of each run, Pallas kernels for 4% -> 0%
where the time goes in v4:
time: 260 us; the launch traced here: 259 us
  starting transfers between devices  96.1 us (37%)
  blocking collectives  71.9 us (28%)
  waiting for transfers between devices  57.9 us (22%)
  Pallas kernels  15.7 us (6%)
  other arithmetic  8.39 us (3%)
  local copies, waits for them, and re-layouts  7.45 us (3%)
    ppermute x16, starting transfers between devices, shift(): return lax.ppermute(x, axis, [(i, (i + by) % size) for i in range(size)])  62.9 us
    ppermute x16, waiting for transfers between devices, shift(): return lax.ppermute(x, axis, [(i, (i + by) % size) for i in range(size)])  33 us
    all_gather x1, blocking collectives, on_device(): column = lax.all_gather(own_in, ZZ, axis=0, tiled=True)  31.8 us
    all_to_all x2, blocking collectives, on_device(): lax.all_to_all(jnp.broadcast_to(scores, (8,) + scores.shape), axes, 0, 0,...  31.1 us
    all_to_all x1, waiting for transfers between devices, on_device(): parts = lax.all_to_all(partial_out, ('core',) + NARROW, 0, 0, tiled=True)  11.9 us
    all_to_all x1, starting transfers between devices, on_device(): parts = lax.all_to_all(partial_out, ('core',) + NARROW, 0, 0, tiled=True)  11.6 us
    all_to_all x1, starting transfers between devices, on_device(): lax.all_to_all(part, ZZ, 0, 0, tiled=True)  10.3 us
    all_to_all x1, blocking collectives, on_device(): scores = jnp.sum(lax.all_to_all(scores, NARROW, 0, 0, tiled=True), 0)  9.03 us
  transfers between devices with their start and end apart: 20, of which 9 were waited for; matrix products, arithmetic and copies ran while one was open for 3% of the time, Pallas kernels for 0%

profile of v4, /device:TPU:1, one launch (start us, length us, event | category | flops | bytes accessed | tf_op | source)
XLA Modules:
  0.0 259.2 jit_solution(8185553550100474988)
XLA Ops:
  3.9 8.8 %collective-permute-start.2 = (bf16[512,1024]{1,0:T(8,128)(2,1)S(1)}, bf16[512,1024]{1,0:T(8,128)(2,1)S(1)}, u32[]{:S(2)}, u32[]{:S(2)}) collective-permute-start(bf16[512,1024]{1,0:T(8,128)(2,1)S(1)} %get-tuple-element.23), channel_id=1, source_target_pairs={{0,8},{8,0},{1,9},{9,1},{2,10},{10,2},{3,11},{11,3},{4,12},{12,4},... | collective-permute-start | bytes 3145736 | tf_op jit(solution)/shard_map/ppermute | solution.py:49
  13.6 4.8 %collective-permute-start.1 = (bf16[16,3584]{1,0:T(8,128)(2,1)S(1)}, bf16[16,3584]{1,0:T(8,128)(2,1)S(1)}, u32[]{:S(2)}, u32[]{:S(2)}) collective-permute-start(bf16[16,3584]{1,0:T(8,128)(2,1)S(1)} %pad.4.refs_0_), channel_id=1, source_target_pairs={{0,80},{16,96},{32,112},{48,128},{64,144},{80,160},{96,176},{112,1... | collective-permute-start | bytes 344072 | tf_op jit(solution)/shard_map/ppermute | solution.py:49
  18.4 6.5 %collective-permute-start = (bf16[16,3584]{1,0:T(8,128)(2,1)S(1)}, bf16[16,3584]{1,0:T(8,128)(2,1)S(1)}, u32[]{:S(2)}, u32[]{:S(2)}) collective-permute-start(bf16[16,3584]{1,0:T(8,128)(2,1)S(1)} %pad.4.refs_0_), channel_id=1, source_target_pairs={{0,176},{16,192},{32,208},{48,224},{64,240},{80,0},{96,16},{112,32... | collective-permute-start | bytes 344072 | tf_op jit(solution)/shard_map/ppermute | solution.py:49
  26.4 9.4 %collective-permute-done.refs_1_ = bf16[16,3584]{1,0:T(8,128)(2,1)S(1)} collective-permute-done((bf16[16,3584]{1,0:T(8,128)(2,1)S(1)}, bf16[16,3584]{1,0:T(8,128)(2,1)S(1)}, u32[]{:S(2)}, u32[]{:S(2)}) %collective-permute-start) | collective-permute-done | bytes 114720 | tf_op jit(solution)/shard_map/ppermute | solution.py:49
  42.0 5.2 %collective-permute-start.12 = (bf16[448,3584]{1,0:T(8,128)(2,1)}, bf16[448,3584]{1,0:T(8,128)(2,1)}, u32[]{:S(2)}, u32[]{:S(2)}) collective-permute-start(bf16[448,3584]{1,0:T(8,128)(2,1)} %bitcast.4.refs_6_), channel_id=1, source_target_pairs={{0,8},{8,0},{1,9},{9,1},{2,10},{10,2},{3,11},{11,3},{4,12},{12,4},... | collective-permute-start | bytes 9633800 | tf_op jit(solution)/shard_map/ppermute | solution.py:49
  51.3 5.1 %collective-permute-start.3 = (bf16[48,3584]{1,0:T(8,128)(2,1)S(1)}, bf16[48,3584]{1,0:T(8,128)(2,1)S(1)}, u32[]{:S(2)}, u32[]{:S(2)}) collective-permute-start(bf16[48,3584]{1,0:T(8,128)(2,1)S(1)} %shard_map.137.refs_0_), channel_id=1, source_target_pairs={{0,240},{16,0},{32,16},{48,32},{64,48},{80,64},{96,80},{112,96},{1... | collective-permute-start | bytes 1032200 | tf_op jit(solution)/shard_map/ppermute | solution.py:49
  58.7 6.7 %all-to-all-start.1 = ((f32[8,1,128]{2,1,0:T(1,128)}), f32[8,1,128]{2,1,0:T(1,128)S(1)}, u32[]{:S(2)}, u32[]{:S(2)}) async-start(f32[8,1,128]{2,1,0:T(1,128)} %broadcast_in_dim.24), calls=%async_computation.1 | async-start | bytes 8192 | tf_op jit(solution)/shard_map/all_to_all | solution.py:226
  67.8 4.0 %all-to-all-done.1 = f32[8,1,128]{2,1,0:T(1,128)S(1)} async-done(((f32[8,1,128]{2,1,0:T(1,128)}), f32[8,1,128]{2,1,0:T(1,128)S(1)}, u32[]{:S(2)}, u32[]{:S(2)}) %all-to-all-start.1) | async-done | bytes 4128 | tf_op jit(solution)/shard_map/all_to_all | solution.py:226
  71.7 10.3 %all-to-all-start = ((bf16[16,16,1024]{2,1,0:T(8,128)(2,1)}), bf16[16,16,1024]{2,1,0:T(8,128)(2,1)}, u32[]{:S(2)}, u32[]{:S(2)}) async-start(bf16[16,16,1024]{2,1,0:T(8,128)(2,1)} %bitcast.1), calls=%async_computation | async-start | bytes 1048576 | tf_op jit(solution)/shard_map/all_to_all | solution.py:241
  84.3 3.2 %collective-permute-start.9 = (bf16[48,3584]{1,0:T(8,128)(2,1)S(1)}, bf16[48,3584]{1,0:T(8,128)(2,1)S(1)}, u32[]{:S(2)}, u32[]{:S(2)}) collective-permute-start(bf16[48,3584]{1,0:T(8,128)(2,1)S(1)} %collective-permute-done.4.refs_1_), channel_id=1, source_target_pairs={{0,16},{16,32},{32,48},{48,64},{64,80},{80,96},{96,112},{112,128},... | collective-permute-start | bytes 1032200 | tf_op jit(solution)/shard_map/ppermute | solution.py:49
  87.5 3.3 %collective-permute-start.8 = (bf16[48,3584]{1,0:T(8,128)(2,1)S(1)}, bf16[48,3584]{1,0:T(8,128)(2,1)S(1)}, u32[]{:S(2)}, u32[]{:S(2)}) collective-permute-start(bf16[48,3584]{1,0:T(8,128)(2,1)S(1)} %collective-permute-done.3.refs_0_), channel_id=1, source_target_pairs={{0,240},{16,0},{32,16},{48,32},{64,48},{80,64},{96,80},{112,96},{1... | collective-permute-start | bytes 1032200 | tf_op jit(solution)/shard_map/ppermute | solution.py:49
  90.8 5.0 %collective-permute-start.7 = (bf16[16,3584]{1,0:T(8,128)(2,1)S(1)}, bf16[16,3584]{1,0:T(8,128)(2,1)S(1)}, u32[]{:S(2)}, u32[]{:S(2)}) collective-permute-start(bf16[16,3584]{1,0:T(8,128)(2,1)S(1)} %collective-permute-done.refs_1_), channel_id=1, source_target_pairs={{0,208},{16,224},{32,240},{48,0},{64,16},{80,32},{96,48},{112,64},... | collective-permute-start | bytes 344072 | tf_op jit(solution)/shard_map/ppermute | solution.py:49
  96.5 18.3 %collective-permute-done.9.refs_2_ = bf16[48,3584]{1,0:T(8,128)(2,1)S(1)} collective-permute-done((bf16[48,3584]{1,0:T(8,128)(2,1)S(1)}, bf16[48,3584]{1,0:T(8,128)(2,1)S(1)}, u32[]{:S(2)}, u32[]{:S(2)}) %collective-permute-start.9) | collective-permute-done | bytes 344096 | tf_op jit(solution)/shard_map/ppermute | solution.py:49
  121.4 31.8 %all_gather.3.refs_0_ = bf16[256,1024]{1,0:T(8,128)(2,1)S(1)} all-gather(bf16[16,1024]{1,0:T(8,128)(2,1)S(1)} %select_convert_fusion), channel_id=1, replica_groups=mesh['x_lo'=2,'zh'=4,'zl'=4,'core'=2,'y'=4,'x_hi'=2] {'zh','zl'}, dimensions={0}, use_global_device_ids=true | all-gather | bytes 557056 | tf_op jit(solution)/shard_map/all_gather | solution.py:245
  155.4 8.0 %shard_map.140 = bf16[1024,448]{1,0:T(8,128)(2,1)} custom-call(s32[1]{0:T(128)} %bitcast.core_ref, bf16[48,3584]{1,0:T(8,128)(2,1)S(1)} %shard_map.137.refs_0_, bf16[96,3584]{1,0:T(8,128)(2,1)S(1)} %shard_map.138.refs_1_, bf16[48,3584]{1,0:T(8,128)(2,1)S(1)} %copy-done.4, bf16[112,3584]{1,0:T(8,128)(2,1)S(1)} %shard_map.139.refs_3_, ...), custom_call_target="tpu_custom_call" | custom-call | flops 3300000000 | bytes 10000000 | tf_op jit(solution)/shard_map/pallas_call | solution.py:246
  163.4 11.6 %all-to-all-start.2 = ((bf16[16,64,448]{2,1,0:T(8,128)(2,1)}), bf16[16,64,448]{2,1,0:T(8,128)(2,1)S(1)}, u32[]{:S(2)}, u32[]{:S(2)}) async-start(bf16[16,64,448]{2,1,0:T(8,128)(2,1)} %bitcast.6), calls=%async_computation.2 | async-start | bytes 2097152 | tf_op jit(solution)/shard_map/all_to_all | solution.py:256
  178.1 11.9 %all-to-all-done.2.parts_ref = bf16[16,64,448]{2,1,0:T(8,128)(2,1)S(1)} async-done(((bf16[16,64,448]{2,1,0:T(8,128)(2,1)}), bf16[16,64,448]{2,1,0:T(8,128)(2,1)S(1)}, u32[]{:S(2)}, u32[]{:S(2)}) %all-to-all-start.2) | async-done | bytes 917536 | tf_op jit(solution)/shard_map/all_to_all | solution.py:256
  191.2 4.7 %all-to-all-start.3 = ((bf16[8,64,896]{2,1,0:T(8,128)(2,1)}), bf16[8,64,896]{2,1,0:T(8,128)(2,1)S(1)}, u32[]{:S(2)}, u32[]{:S(2)}) async-start(bf16[8,64,896]{2,1,0:T(8,128)(2,1)} %shard_map.141), calls=%async_computation.3 | async-start | bytes 1835008 | tf_op jit(solution)/shard_map/all_to_all | solution.py:267
  195.8 3.4 %collective-permute-start.14 = (bf16[256,1024]{1,0:T(8,128)(2,1)S(1)}, bf16[256,1024]{1,0:T(8,128)(2,1)}, u32[]{:S(2)}, u32[]{:S(2)}) collective-permute-start(bf16[256,1024]{1,0:T(8,128)(2,1)S(1)} %all_gather.3.refs_0_), channel_id=1, source_target_pairs={{0,8},{8,0},{1,9},{9,1},{2,10},{10,2},{3,11},{11,3},{4,12},{12,4},... | collective-permute-start | bytes 1572872 | tf_op jit(solution)/shard_map/ppermute | solution.py:49
  204.2 9.0 %all-to-all-done.3.ro_ref = bf16[8,64,896]{2,1,0:T(8,128)(2,1)S(1)} async-done(((bf16[8,64,896]{2,1,0:T(8,128)(2,1)}), bf16[8,64,896]{2,1,0:T(8,128)(2,1)S(1)}, u32[]{:S(2)}, u32[]{:S(2)}) %all-to-all-start.3) | async-done | bytes 917536 | tf_op jit(solution)/shard_map/all_to_all | solution.py:267
  213.2 5.1 %shard_map.142 = f32[8,4,384]{2,1,0:T(4,128)S(1)} custom-call(s32[64]{0:T(128)S(1)} %fusion.3.to_out_ref, s32[64]{0:T(128)S(1)} %get-tuple-element.42.to_in_ref, bf16[8,64,896]{2,1,0:T(8,128)(2,1)S(1)} %all-to-all-done.3.ro_ref, bf16[256,1024]{1,0:T(8,128)(2,1)S(1)} %all_gather.3.refs_0_, bf16[256,1024]{1,0:T(8,128)(2,1)S(1)} %collective-permute-done.13.refs_1_, ...), custom_call_target="tpu_custom_call" | custom-call | flops 3000000000 | bytes 5000000 | tf_op jit(solution)/shard_map/pallas_call | solution.py:269
  218.4 9.0 %all_to_all.50 = f32[8,4,384]{2,1,0:T(4,128)S(1)} all-to-all(f32[8,4,384]{2,1,0:T(4,128)S(1)} %shard_map.142), channel_id=1, replica_groups=mesh['x_lo'=2,'zh'=4,'zl'=4,'core'=2,'y'=4,'x_hi'=2] {'y','x_hi'}, dimensions={0} | all-to-all | bytes 98304 | tf_op jit(solution)/shard_map/all_to_all | solution.py:278
  227.4 9.9 %all_to_all.51 = f32[8,4,384]{2,1,0:T(4,128)S(1)} all-to-all(f32[8,4,384]{2,1,0:T(4,128)S(1)} %broadcast_in_dim.29), channel_id=1, replica_groups=mesh['x_lo'=2,'zh'=4,'zl'=4,'core'=2,'y'=4,'x_hi'=2] {'zl','core'}, dimensions={0} | all-to-all | bytes 98304 | tf_op jit(solution)/shard_map/all_to_all | solution.py:280
  237.4 21.2 %all_to_all.52 = f32[8,4,384]{2,1,0:T(4,128)S(1)} all-to-all(f32[8,4,384]{2,1,0:T(4,128)S(1)} %broadcast_in_dim.30), channel_id=1, replica_groups=mesh['x_lo'=2,'zh'=4,'zl'=4,'core'=2,'y'=4,'x_hi'=2] {'x_lo','zh'}, dimensions={0} | all-to-all | bytes 98304 | tf_op jit(solution)/shard_map/all_to_all | solution.py:280
  (66 shorter events, 41.2 us)
Async XLA Ops:
  3.9 31.9 %collective-permute-start.2 = (bf16[512,1024]{1,0:T(8,128)(2,1)S(1)}, bf16[512,1024]{1,0:T(8,128)(2,1)S(1)}, u32[]{:S(2)}, u32[]{:S(2)}) collective-permute-start(bf16[512,1024]{1,0:T(8,128)(2,1)S(1)} %get-tuple-element.23), channel_id=1, source_target_pairs={{0,8},{8,0},{1,9},{9,1},{2,10},{10,2},{3,11},{11,3},{4,12},{12,4},... | collective-permute-start | bytes 3145736 | tf_op jit(solution)/shard_map/ppermute | solution.py:49
  13.6 12.7 %collective-permute-start.1 = (bf16[16,3584]{1,0:T(8,128)(2,1)S(1)}, bf16[16,3584]{1,0:T(8,128)(2,1)S(1)}, u32[]{:S(2)}, u32[]{:S(2)}) collective-permute-start(bf16[16,3584]{1,0:T(8,128)(2,1)S(1)} %pad.4.refs_0_), channel_id=1, source_target_pairs={{0,80},{16,96},{32,112},{48,128},{64,144},{80,160},{96,176},{112,1... | collective-permute-start | bytes 344072 | tf_op jit(solution)/shard_map/ppermute | solution.py:49
  18.4 17.3 %collective-permute-start = (bf16[16,3584]{1,0:T(8,128)(2,1)S(1)}, bf16[16,3584]{1,0:T(8,128)(2,1)S(1)}, u32[]{:S(2)}, u32[]{:S(2)}) collective-permute-start(bf16[16,3584]{1,0:T(8,128)(2,1)S(1)} %pad.4.refs_0_), channel_id=1, source_target_pairs={{0,176},{16,192},{32,208},{48,224},{64,240},{80,0},{96,16},{112,32... | collective-permute-start | bytes 344072 | tf_op jit(solution)/shard_map/ppermute | solution.py:49
  37.5 19.0 %copy-start = (bf16[448,1024]{1,0:T(8,128)(2,1)S(1)}, bf16[448,1024]{1,0:T(8,128)(2,1)}, u32[]{:S(2)}) copy-start(bf16[448,1024]{1,0:T(8,128)(2,1)} %refs_4_) | copy-start | bytes 2752516
  38.8 26.5 %collective-permute-start.6 = (bf16[256,1024]{1,0:T(8,128)(2,1)S(1)}, bf16[256,1024]{1,0:T(8,128)(2,1)}, u32[]{:S(2)}, u32[]{:S(2)}) collective-permute-start(bf16[256,1024]{1,0:T(8,128)(2,1)S(1)} %slice.20), channel_id=1, source_target_pairs={{0,256},{256,0},{1,257},{257,1},{2,258},{258,2},{3,259},{259,3},{4... | collective-permute-start | bytes 1572872 | tf_op jit(solution)/shard_map/ppermute | solution.py:49
  42.0 111.3 %collective-permute-start.12 = (bf16[448,3584]{1,0:T(8,128)(2,1)}, bf16[448,3584]{1,0:T(8,128)(2,1)}, u32[]{:S(2)}, u32[]{:S(2)}) collective-permute-start(bf16[448,3584]{1,0:T(8,128)(2,1)} %bitcast.4.refs_6_), channel_id=1, source_target_pairs={{0,8},{8,0},{1,9},{9,1},{2,10},{10,2},{3,11},{11,3},{4,12},{12,4},... | collective-permute-start | bytes 9633800 | tf_op jit(solution)/shard_map/ppermute | solution.py:49
  47.2 18.1 %collective-permute-start.5 = (bf16[48,3584]{1,0:T(8,128)(2,1)S(1)}, bf16[48,3584]{1,0:T(8,128)(2,1)S(1)}, u32[]{:S(2)}, u32[]{:S(2)}) collective-permute-start(bf16[48,3584]{1,0:T(8,128)(2,1)S(1)} %shard_map.137.refs_0_), channel_id=1, source_target_pairs={{0,256},{256,0},{1,257},{257,1},{2,258},{258,2},{3,259},{259,3},{4... | collective-permute-start | bytes 1032200 | tf_op jit(solution)/shard_map/ppermute | solution.py:49
  49.4 15.9 %collective-permute-start.4 = (bf16[48,3584]{1,0:T(8,128)(2,1)S(1)}, bf16[48,3584]{1,0:T(8,128)(2,1)S(1)}, u32[]{:S(2)}, u32[]{:S(2)}) collective-permute-start(bf16[48,3584]{1,0:T(8,128)(2,1)S(1)} %shard_map.137.refs_0_), channel_id=1, source_target_pairs={{0,16},{16,32},{32,48},{48,64},{64,80},{80,96},{96,112},{112,128},... | collective-permute-start | bytes 1032200 | tf_op jit(solution)/shard_map/ppermute | solution.py:49
  51.3 14.0 %collective-permute-start.3 = (bf16[48,3584]{1,0:T(8,128)(2,1)S(1)}, bf16[48,3584]{1,0:T(8,128)(2,1)S(1)}, u32[]{:S(2)}, u32[]{:S(2)}) collective-permute-start(bf16[48,3584]{1,0:T(8,128)(2,1)S(1)} %shard_map.137.refs_0_), channel_id=1, source_target_pairs={{0,240},{16,0},{32,16},{48,32},{64,48},{80,64},{96,80},{112,96},{1... | collective-permute-start | bytes 1032200 | tf_op jit(solution)/shard_map/ppermute | solution.py:49
  58.7 13.1 %all-to-all-start.1 = ((f32[8,1,128]{2,1,0:T(1,128)}), f32[8,1,128]{2,1,0:T(1,128)S(1)}, u32[]{:S(2)}, u32[]{:S(2)}) async-start(f32[8,1,128]{2,1,0:T(1,128)} %broadcast_in_dim.24), calls=%async_computation.1 | async-start | bytes 8192 | tf_op jit(solution)/shard_map/all_to_all | solution.py:226
  71.7 48.5 %all-to-all-start = ((bf16[16,16,1024]{2,1,0:T(8,128)(2,1)}), bf16[16,16,1024]{2,1,0:T(8,128)(2,1)}, u32[]{:S(2)}, u32[]{:S(2)}) async-start(bf16[16,16,1024]{2,1,0:T(8,128)(2,1)} %bitcast.1), calls=%async_computation | async-start | bytes 1048576 | tf_op jit(solution)/shard_map/all_to_all | solution.py:241
  82.1 32.7 %collective-permute-start.10 = (bf16[96,3584]{1,0:T(8,128)(2,1)S(1)}, bf16[96,3584]{1,0:T(8,128)(2,1)S(1)}, u32[]{:S(2)}, u32[]{:S(2)}) collective-permute-start(bf16[96,3584]{1,0:T(8,128)(2,1)S(1)} %shard_map.138.refs_1_), channel_id=1, source_target_pairs={{0,256},{256,0},{1,257},{257,1},{2,258},{258,2},{3,259},{259,3},{4... | collective-permute-start | bytes 2064392 | tf_op jit(solution)/shard_map/ppermute | solution.py:49
  84.3 30.5 %collective-permute-start.9 = (bf16[48,3584]{1,0:T(8,128)(2,1)S(1)}, bf16[48,3584]{1,0:T(8,128)(2,1)S(1)}, u32[]{:S(2)}, u32[]{:S(2)}) collective-permute-start(bf16[48,3584]{1,0:T(8,128)(2,1)S(1)} %collective-permute-done.4.refs_1_), channel_id=1, source_target_pairs={{0,16},{16,32},{32,48},{48,64},{64,80},{80,96},{96,112},{112,128},... | collective-permute-start | bytes 1032200 | tf_op jit(solution)/shard_map/ppermute | solution.py:49
  87.5 27.2 %collective-permute-start.8 = (bf16[48,3584]{1,0:T(8,128)(2,1)S(1)}, bf16[48,3584]{1,0:T(8,128)(2,1)S(1)}, u32[]{:S(2)}, u32[]{:S(2)}) collective-permute-start(bf16[48,3584]{1,0:T(8,128)(2,1)S(1)} %collective-permute-done.3.refs_0_), channel_id=1, source_target_pairs={{0,240},{16,0},{32,16},{48,32},{64,48},{80,64},{96,80},{112,96},{1... | collective-permute-start | bytes 1032200 | tf_op jit(solution)/shard_map/ppermute | solution.py:49
  90.8 25.8 %collective-permute-start.7 = (bf16[16,3584]{1,0:T(8,128)(2,1)S(1)}, bf16[16,3584]{1,0:T(8,128)(2,1)S(1)}, u32[]{:S(2)}, u32[]{:S(2)}) collective-permute-start(bf16[16,3584]{1,0:T(8,128)(2,1)S(1)} %collective-permute-done.refs_1_), channel_id=1, source_target_pairs={{0,208},{16,224},{32,240},{48,0},{64,16},{80,32},{96,48},{112,64},... | collective-permute-start | bytes 344072 | tf_op jit(solution)/shard_map/ppermute | solution.py:49
  116.7 36.6 %collective-permute-start.11 = (bf16[112,3584]{1,0:T(8,128)(2,1)S(1)}, bf16[112,3584]{1,0:T(8,128)(2,1)}, u32[]{:S(2)}, u32[]{:S(2)}) collective-permute-start(bf16[112,3584]{1,0:T(8,128)(2,1)S(1)} %shard_map.139.refs_3_), channel_id=1, source_target_pairs={{0,256},{256,0},{1,257},{257,1},{2,258},{258,2},{3,259},{259,3},{4... | collective-permute-start | bytes 2408456 | tf_op jit(solution)/shard_map/ppermute | solution.py:49
  163.4 26.6 %all-to-all-start.2 = ((bf16[16,64,448]{2,1,0:T(8,128)(2,1)}), bf16[16,64,448]{2,1,0:T(8,128)(2,1)S(1)}, u32[]{:S(2)}, u32[]{:S(2)}) async-start(bf16[16,64,448]{2,1,0:T(8,128)(2,1)} %bitcast.6), calls=%async_computation.2 | async-start | bytes 2097152 | tf_op jit(solution)/shard_map/all_to_all | solution.py:256
  175.0 27.6 %copy-start.7 = (s32[64]{0:T(128)S(1)}, s32[64]{0:T(128)}, u32[]{:S(2)}) copy-start(s32[64]{0:T(128)} %constant.63.clone) | copy-start | bytes 772
  175.0 27.6 %copy-start.8 = (s32[64]{0:T(128)S(1)}, s32[64]{0:T(128)}, u32[]{:S(2)}) copy-start(s32[64]{0:T(128)} %constant.62.clone) | copy-start | bytes 772
  175.0 27.6 %copy-start.9 = (s32[64]{0:T(128)S(1)}, s32[64]{0:T(128)}, u32[]{:S(2)}) copy-start(s32[64]{0:T(128)} %constant.61.clone) | copy-start | bytes 772
  175.0 24.7 %collective-permute-start.13 = (bf16[256,1024]{1,0:T(8,128)(2,1)S(1)}, bf16[256,1024]{1,0:T(8,128)(2,1)S(1)}, u32[]{:S(2)}, u32[]{:S(2)}) collective-permute-start(bf16[256,1024]{1,0:T(8,128)(2,1)S(1)} %all_gather.3.refs_0_), channel_id=1, source_target_pairs={{0,256},{256,0},{1,257},{257,1},{2,258},{258,2},{3,259},{259,3},{4... | collective-permute-start | bytes 1572872 | tf_op jit(solution)/shard_map/ppermute | solution.py:49
  191.2 22.1 %all-to-all-start.3 = ((bf16[8,64,896]{2,1,0:T(8,128)(2,1)}), bf16[8,64,896]{2,1,0:T(8,128)(2,1)S(1)}, u32[]{:S(2)}, u32[]{:S(2)}) async-start(bf16[8,64,896]{2,1,0:T(8,128)(2,1)} %shard_map.141), calls=%async_computation.3 | async-start | bytes 1835008 | tf_op jit(solution)/shard_map/all_to_all | solution.py:267
  195.8 6.8 %collective-permute-start.14 = (bf16[256,1024]{1,0:T(8,128)(2,1)S(1)}, bf16[256,1024]{1,0:T(8,128)(2,1)}, u32[]{:S(2)}, u32[]{:S(2)}) collective-permute-start(bf16[256,1024]{1,0:T(8,128)(2,1)S(1)} %all_gather.3.refs_0_), channel_id=1, source_target_pairs={{0,8},{8,0},{1,9},{9,1},{2,10},{10,2},{3,11},{11,3},{4,12},{12,4},... | collective-permute-start | bytes 1572872 | tf_op jit(solution)/shard_map/ppermute | solution.py:49
  199.7 4.5 %collective-permute-start.15 = (bf16[256,1024]{1,0:T(8,128)(2,1)S(1)}, bf16[256,1024]{1,0:T(8,128)(2,1)}, u32[]{:S(2)}, u32[]{:S(2)}) collective-permute-start(bf16[256,1024]{1,0:T(8,128)(2,1)S(1)} %collective-permute-done.13.refs_1_), channel_id=1, source_target_pairs={{0,8},{8,0},{1,9},{9,1},{2,10},{10,2},{3,11},{11,3},{4,12},{12,4},... | collective-permute-start | bytes 1572872 | tf_op jit(solution)/shard_map/ppermute | solution.py:49
  (6 other events, 22.6 us)

commit v5 on v4

--- a/solution.py
+++ b/solution.py
@@ -231,18 +231,15 @@
     other_basis = shift(own_basis, "core", 1)
     part = half(part[:RUN] + f32(shift(half(part[RUN:]), "x_lo", 1)))
     up, down, near_x = lax.optimization_barrier((up, down, near_x))
-    part, _ = lax.optimization_barrier((part, up))
     mid = stack(up, down)
-    *far, mid_x, narrow_sum = lax.optimization_barrier((from_z(up, 1), from_z(down, -1), shift(mid, "x_lo", 1), narrow_sum))
+    up = from_z(up, 1)
+    part, up = lax.optimization_barrier((part, up))
+    *far, mid_x, narrow_sum = lax.optimization_barrier((up, from_z(down, -1), shift(mid, "x_lo", 1), narrow_sum))
     far = stack(across, *far)
     far_x = shift(far, "x_lo", 1)
     blocks = [near, mid, near_x, far, mid_x, far_x]
 
-    pieces, far = lax.optimization_barrier((lax.all_to_all(part, ZZ, 0, 0, tiled=True), far))
-    blocks[3] = far
-    own_in = jnp.sum(f32(pieces.reshape(Z, ROWS, n_in)), 0)
-    own_in = half(with_terms(own_in, narrow_sum))
-    column = lax.all_gather(own_in, ZZ, axis=0, tiled=True)
+    pieces = lax.all_to_all(part, ZZ, 0, 0, tiled=True)
     partial_out = pl.pallas_call(
         rotate_out_kernel,
         out_shape=jax.ShapeDtypeStruct((ALL, n_out), jnp.bfloat16),
@@ -252,8 +249,12 @@
         compiler_params=params(),
         cost_estimate=pl.CostEstimate(flops=33 * 10**8, bytes_accessed=10**7, transcendentals=0),
     )(c_me.astype(jnp.int32).reshape(1), *blocks, own_basis, other_basis)
-    partial_out, column = lax.optimization_barrier((partial_out, column))
+    pieces, partial_out = lax.optimization_barrier((pieces, partial_out))
+    own_in = jnp.sum(f32(pieces.reshape(Z, ROWS, n_in)), 0)
+    own_in = half(with_terms(own_in, narrow_sum))
+    column = lax.all_gather(own_in, ZZ, axis=0, tiled=True)
     parts = lax.all_to_all(partial_out, ("core",) + NARROW, 0, 0, tiled=True)
+    parts, column = lax.optimization_barrier((parts, column))
     shares = pl.pallas_call(
         share_kernel,
         out_shape=jax.ShapeDtypeStruct((N, SHARE, C * n_out), jnp.bfloat16),

time: 260 us -> 261 us (level)
  waiting for transfers between devices: 57.9 us -> 69.5 us
  blocking collectives: 71.9 us -> 68.4 us
  local copies, waits for them, and re-layouts: 7.45 us -> 4.07 us
    ppermute x16, waiting for transfers between devices: 33 us -> 63.3 us  [shift(): return lax.ppermute(x, axis, [(i, (i + by) % size) for i in range(size)])]
    all_to_all x1, waiting for transfers between devices: 11.9 us -> 0.01 us  [on_device(): parts = lax.all_to_all(partial_out, ('core',) + NARROW, 0, 0, tiled=True)]
    all_to_all x1, waiting for transfers between devices: 9.02 us -> 2.03 us  [on_device(): rotated_out = lax.all_to_all(shares, NARROW, 0, 0, tiled=True)]
    all_gather x1, blocking collectives: 31.8 us -> 25.3 us  [on_device(): column = lax.all_gather(own_in, ZZ, axis=0, tiled=True)]
    all_to_all x1, starting transfers between devices: 11.6 us -> 5.96 us  [on_device(): parts = lax.all_to_all(partial_out, ('core',) + NARROW, 0, 0, tiled=True)]
    all_to_all x1, blocking collectives: 9.03 us -> 12.4 us  [on_device(): scores = jnp.sum(lax.all_to_all(scores, NARROW, 0, 0, tiled=True), 0)]
  transfers between devices with their start and end apart: 20 -> 20, of which waited for: 9 -> 9; matrix products, arithmetic and copies ran while one was open for 3% -> 3% of each run, Pallas kernels for 0% -> 3%
where the time goes in v5:
time: 261 us; the launch traced here: 260 us
  starting transfers between devices  94.8 us (36%)
  waiting for transfers between devices  69.5 us (27%)
  blocking collectives  68.4 us (26%)
  Pallas kernels  15.4 us (6%)
  other arithmetic  6 us (2%)
  local copies, waits for them, and re-layouts  4.07 us (2%)
    ppermute x16, waiting for transfers between devices, shift(): return lax.ppermute(x, axis, [(i, (i + by) % size) for i in range(size)])  63.3 us
    ppermute x16, starting transfers between devices, shift(): return lax.ppermute(x, axis, [(i, (i + by) % size) for i in range(size)])  63.3 us
    all_to_all x2, blocking collectives, on_device(): lax.all_to_all(jnp.broadcast_to(scores, (8,) + scores.shape), axes, 0, 0,...  30.7 us
    all_gather x1, blocking collectives, on_device(): column = lax.all_gather(own_in, ZZ, axis=0, tiled=True)  25.3 us
    all_to_all x1, blocking collectives, on_device(): scores = jnp.sum(lax.all_to_all(scores, NARROW, 0, 0, tiled=True), 0)  12.4 us
    all_to_all x1, starting transfers between devices, on_device(): pieces = lax.all_to_all(part, ZZ, 0, 0, tiled=True)  11.7 us
    pallas_call x1, Pallas kernels, on_device(): pl.pallas_call(rotate_out_kernel, out_shape=jax.ShapeDtypeStruct((ALL, n_...  7.84 us
    all_to_all x1, starting transfers between devices, on_device(): rotated_out = lax.all_to_all(shares, NARROW, 0, 0, tiled=True)  7.14 us
  transfers between devices with their start and end apart: 20, of which 9 were waited for; matrix products, arithmetic and copies ran while one was open for 3% of the time, Pallas kernels for 3%

profile of v5, /device:TPU:1, one launch (start us, length us, event | category | flops | bytes accessed | tf_op | source)
XLA Modules:
  0.0 259.8 jit_solution(2762917501819947437)
XLA Ops:
  3.9 8.8 %collective-permute-start.2 = (bf16[512,1024]{1,0:T(8,128)(2,1)S(1)}, bf16[512,1024]{1,0:T(8,128)(2,1)S(1)}, u32[]{:S(2)}, u32[]{:S(2)}) collective-permute-start(bf16[512,1024]{1,0:T(8,128)(2,1)S(1)} %get-tuple-element.25), channel_id=1, source_target_pairs={{0,8},{8,0},{1,9},{9,1},{2,10},{10,2},{3,11},{11,3},{4,12},{12,4},... | collective-permute-start | bytes 3145736 | tf_op jit(solution)/shard_map/ppermute | solution.py:49
  15.6 8.7 %collective-permute-start = (bf16[16,3584]{1,0:T(8,128)(2,1)S(1)}, bf16[16,3584]{1,0:T(8,128)(2,1)S(1)}, u32[]{:S(2)}, u32[]{:S(2)}) collective-permute-start(bf16[16,3584]{1,0:T(8,128)(2,1)S(1)} %pad.4.refs_0_), channel_id=1, source_target_pairs={{0,176},{16,192},{32,208},{48,224},{64,240},{80,0},{96,16},{112,32... | collective-permute-start | bytes 344072 | tf_op jit(solution)/shard_map/ppermute | solution.py:49
  26.2 5.3 %collective-permute-done.refs_1_ = bf16[16,3584]{1,0:T(8,128)(2,1)S(1)} collective-permute-done((bf16[16,3584]{1,0:T(8,128)(2,1)S(1)}, bf16[16,3584]{1,0:T(8,128)(2,1)S(1)}, u32[]{:S(2)}, u32[]{:S(2)}) %collective-permute-start) | collective-permute-done | bytes 114720 | tf_op jit(solution)/shard_map/ppermute | solution.py:49
  31.5 9.4 %collective-permute-done.1.refs_2_ = bf16[16,3584]{1,0:T(8,128)(2,1)S(1)} collective-permute-done((bf16[16,3584]{1,0:T(8,128)(2,1)S(1)}, bf16[16,3584]{1,0:T(8,128)(2,1)S(1)}, u32[]{:S(2)}, u32[]{:S(2)}) %collective-permute-start.1) | collective-permute-done | bytes 114720 | tf_op jit(solution)/shard_map/ppermute | solution.py:49
  41.5 3.3 %collective-permute-start.3 = (bf16[256,1024]{1,0:T(8,128)(2,1)S(1)}, bf16[256,1024]{1,0:T(8,128)(2,1)}, u32[]{:S(2)}, u32[]{:S(2)}) collective-permute-start(bf16[256,1024]{1,0:T(8,128)(2,1)S(1)} %slice.20), channel_id=1, source_target_pairs={{0,256},{256,0},{1,257},{257,1},{2,258},{258,2},{3,259},{259,3},{4... | collective-permute-start | bytes 1572872 | tf_op jit(solution)/shard_map/ppermute | solution.py:49
  46.7 3.4 %collective-permute-start.5 = (bf16[48,3584]{1,0:T(8,128)(2,1)S(1)}, bf16[48,3584]{1,0:T(8,128)(2,1)S(1)}, u32[]{:S(2)}, u32[]{:S(2)}) collective-permute-start(bf16[48,3584]{1,0:T(8,128)(2,1)S(1)} %shard_map.137.refs_0_), channel_id=1, source_target_pairs={{0,16},{16,32},{32,48},{48,64},{64,80},{80,96},{96,112},{112,128},... | collective-permute-start | bytes 1032200 | tf_op jit(solution)/shard_map/ppermute | solution.py:49
  53.2 4.5 %collective-permute-done.5.refs_1_ = bf16[48,3584]{1,0:T(8,128)(2,1)S(1)} collective-permute-done((bf16[48,3584]{1,0:T(8,128)(2,1)S(1)}, bf16[48,3584]{1,0:T(8,128)(2,1)S(1)}, u32[]{:S(2)}, u32[]{:S(2)}) %collective-permute-start.5) | collective-permute-done | bytes 344096 | tf_op jit(solution)/shard_map/ppermute | solution.py:49
  57.7 4.5 %collective-permute-done.6.refs_2_ = bf16[48,3584]{1,0:T(8,128)(2,1)S(1)} collective-permute-done((bf16[48,3584]{1,0:T(8,128)(2,1)S(1)}, bf16[48,3584]{1,0:T(8,128)(2,1)S(1)}, u32[]{:S(2)}, u32[]{:S(2)}) %collective-permute-start.6) | collective-permute-done | bytes 344096 | tf_op jit(solution)/shard_map/ppermute | solution.py:49
  66.5 6.7 %all-to-all-start.1 = ((f32[8,1,128]{2,1,0:T(1,128)}), f32[8,1,128]{2,1,0:T(1,128)S(1)}, u32[]{:S(2)}, u32[]{:S(2)}) async-start(f32[8,1,128]{2,1,0:T(1,128)} %broadcast_in_dim.24), calls=%async_computation.1 | async-start | bytes 8192 | tf_op jit(solution)/shard_map/all_to_all | solution.py:226
  75.4 4.1 %all-to-all-done.1 = f32[8,1,128]{2,1,0:T(1,128)S(1)} async-done(((f32[8,1,128]{2,1,0:T(1,128)}), f32[8,1,128]{2,1,0:T(1,128)S(1)}, u32[]{:S(2)}, u32[]{:S(2)}) %all-to-all-start.1) | async-done | bytes 4128 | tf_op jit(solution)/shard_map/all_to_all | solution.py:226
  79.5 11.7 %all-to-all-start = ((bf16[16,16,1024]{2,1,0:T(8,128)(2,1)}), bf16[16,16,1024]{2,1,0:T(8,128)(2,1)S(1)}, u32[]{:S(2)}, u32[]{:S(2)}) async-start(bf16[16,16,1024]{2,1,0:T(8,128)(2,1)} %bitcast.10), calls=%async_computation | async-start | bytes 1048576 | tf_op jit(solution)/shard_map/all_to_all | solution.py:242
  96.8 5.2 %collective-permute-start.8 = (bf16[16,3584]{1,0:T(8,128)(2,1)S(1)}, bf16[16,3584]{1,0:T(8,128)(2,1)S(1)}, u32[]{:S(2)}, u32[]{:S(2)}) collective-permute-start(bf16[16,3584]{1,0:T(8,128)(2,1)S(1)} %collective-permute-done.refs_1_), channel_id=1, source_target_pairs={{0,208},{16,224},{32,240},{48,0},{64,16},{80,32},{96,48},{112,64},... | collective-permute-start | bytes 344072 | tf_op jit(solution)/shard_map/ppermute | solution.py:49
  102.6 21.3 %collective-permute-done.9.refs_2_ = bf16[48,3584]{1,0:T(8,128)(2,1)S(1)} collective-permute-done((bf16[48,3584]{1,0:T(8,128)(2,1)S(1)}, bf16[48,3584]{1,0:T(8,128)(2,1)S(1)}, u32[]{:S(2)}, u32[]{:S(2)}) %collective-permute-start.9) | collective-permute-done | bytes 344096 | tf_op jit(solution)/shard_map/ppermute | solution.py:49
  126.3 17.5 %collective-permute-done.11.refs_5_ = bf16[112,3584]{1,0:T(8,128)(2,1)S(1)} collective-permute-done((bf16[112,3584]{1,0:T(8,128)(2,1)S(1)}, bf16[112,3584]{1,0:T(8,128)(2,1)S(1)}, u32[]{:S(2)}, u32[]{:S(2)}) %collective-permute-start.11) | collective-permute-done | bytes 802848 | tf_op jit(solution)/shard_map/ppermute | solution.py:49
  143.8 7.8 %shard_map.140 = bf16[1024,448]{1,0:T(8,128)(2,1)} custom-call(s32[1]{0:T(128)} %bitcast.2.core_ref, bf16[48,3584]{1,0:T(8,128)(2,1)S(1)} %shard_map.137.refs_0_, bf16[96,3584]{1,0:T(8,128)(2,1)S(1)} %shard_map.138.refs_1_, bf16[48,3584]{1,0:T(8,128)(2,1)S(1)} %collective-permute-done.6.refs_2_, bf16[112,3584]{1,0:T(8,128)(2,1)S(1)} %shard_map.139.refs_3_, ...), custom_call_target="tpu_custom_call" | custom-call | flops 3300000000 | bytes 10000000 | tf_op jit(solution)/shard_map/pallas_call | solution.py:243
  151.6 6.0 %all-to-all-start.2 = ((bf16[16,64,448]{2,1,0:T(8,128)(2,1)}), bf16[16,64,448]{2,1,0:T(8,128)(2,1)S(1)}, u32[]{:S(2)}, u32[]{:S(2)}) async-start(bf16[16,64,448]{2,1,0:T(8,128)(2,1)} %bitcast.5), calls=%async_computation.2 | async-start | bytes 2097152 | tf_op jit(solution)/shard_map/all_to_all | solution.py:256
  159.1 25.3 %all_gather.3.refs_0_ = bf16[256,1024]{1,0:T(8,128)(2,1)S(1)} all-gather(bf16[16,1024]{1,0:T(8,128)(2,1)S(1)} %select_convert_fusion), channel_id=1, replica_groups=mesh['x_lo'=2,'zh'=4,'zl'=4,'core'=2,'y'=4,'x_hi'=2] {'zh','zl'}, dimensions={0}, use_global_device_ids=true | all-gather | bytes 557056 | tf_op jit(solution)/shard_map/all_gather | solution.py:255
  187.7 7.1 %all-to-all-start.3 = ((bf16[8,64,896]{2,1,0:T(8,128)(2,1)}), bf16[8,64,896]{2,1,0:T(8,128)(2,1)S(1)}, u32[]{:S(2)}, u32[]{:S(2)}) async-start(bf16[8,64,896]{2,1,0:T(8,128)(2,1)} %shard_map.141), calls=%async_computation.3 | async-start | bytes 1835008 | tf_op jit(solution)/shard_map/all_to_all | solution.py:268
  194.8 9.1 %collective-permute-start.14 = (bf16[256,1024]{1,0:T(8,128)(2,1)S(1)}, bf16[256,1024]{1,0:T(8,128)(2,1)S(1)}, u32[]{:S(2)}, u32[]{:S(2)}) collective-permute-start(bf16[256,1024]{1,0:T(8,128)(2,1)S(1)} %all_gather.3.refs_0_), channel_id=1, source_target_pairs={{0,8},{8,0},{1,9},{9,1},{2,10},{10,2},{3,11},{11,3},{4,12},{12,4},... | collective-permute-start | bytes 1572872 | tf_op jit(solution)/shard_map/ppermute | solution.py:49
  203.9 4.9 %collective-permute-start.15 = (bf16[256,1024]{1,0:T(8,128)(2,1)S(1)}, bf16[256,1024]{1,0:T(8,128)(2,1)}, u32[]{:S(2)}, u32[]{:S(2)}) collective-permute-start(bf16[256,1024]{1,0:T(8,128)(2,1)S(1)} %collective-permute-done.13.refs_1_), channel_id=1, source_target_pairs={{0,8},{8,0},{1,9},{9,1},{2,10},{10,2},{3,11},{11,3},{4,12},{12,4},... | collective-permute-start | bytes 1572872 | tf_op jit(solution)/shard_map/ppermute | solution.py:49
  210.9 5.0 %shard_map.142 = f32[8,4,384]{2,1,0:T(4,128)S(1)} custom-call(s32[64]{0:T(128)S(1)} %fusion.3.to_out_ref, s32[64]{0:T(128)S(1)} %get-tuple-element.44.to_in_ref, bf16[8,64,896]{2,1,0:T(8,128)(2,1)S(1)} %all-to-all-done.3.ro_ref, bf16[256,1024]{1,0:T(8,128)(2,1)S(1)} %all_gather.3.refs_0_, bf16[256,1024]{1,0:T(8,128)(2,1)S(1)} %collective-permute-done.13.refs_1_, ...), custom_call_target="tpu_custom_call" | custom-call | flops 3000000000 | bytes 5000000 | tf_op jit(solution)/shard_map/pallas_call | solution.py:270
  215.9 12.4 %all_to_all.53 = f32[8,4,384]{2,1,0:T(4,128)S(1)} all-to-all(f32[8,4,384]{2,1,0:T(4,128)S(1)} %shard_map.142), channel_id=1, replica_groups=mesh['x_lo'=2,'zh'=4,'zl'=4,'core'=2,'y'=4,'x_hi'=2] {'y','x_hi'}, dimensions={0} | all-to-all | bytes 98304 | tf_op jit(solution)/shard_map/all_to_all | solution.py:279
  228.4 11.6 %all_to_all.54 = f32[8,4,384]{2,1,0:T(4,128)S(1)} all-to-all(f32[8,4,384]{2,1,0:T(4,128)S(1)} %broadcast_in_dim.29), channel_id=1, replica_groups=mesh['x_lo'=2,'zh'=4,'zl'=4,'core'=2,'y'=4,'x_hi'=2] {'zl','core'}, dimensions={0} | all-to-all | bytes 98304 | tf_op jit(solution)/shard_map/all_to_all | solution.py:281
  240.1 19.1 %all_to_all.55 = f32[8,4,384]{2,1,0:T(4,128)S(1)} all-to-all(f32[8,4,384]{2,1,0:T(4,128)S(1)} %broadcast_in_dim.30), channel_id=1, replica_groups=mesh['x_lo'=2,'zh'=4,'zl'=4,'core'=2,'y'=4,'x_hi'=2] {'x_lo','zh'}, dimensions={0} | all-to-all | bytes 98304 | tf_op jit(solution)/shard_map/all_to_all | solution.py:281
  (60 shorter events, 35.5 us)
Async XLA Ops:
  3.9 37.0 %collective-permute-start.2 = (bf16[512,1024]{1,0:T(8,128)(2,1)S(1)}, bf16[512,1024]{1,0:T(8,128)(2,1)S(1)}, u32[]{:S(2)}, u32[]{:S(2)}) collective-permute-start(bf16[512,1024]{1,0:T(8,128)(2,1)S(1)} %get-tuple-element.25), channel_id=1, source_target_pairs={{0,8},{8,0},{1,9},{9,1},{2,10},{10,2},{3,11},{11,3},{4,12},{12,4},... | collective-permute-start | bytes 3145736 | tf_op jit(solution)/shard_map/ppermute | solution.py:49
  12.7 131.1 %collective-permute-start.12 = (bf16[448,3584]{1,0:T(8,128)(2,1)}, bf16[448,3584]{1,0:T(8,128)(2,1)}, u32[]{:S(2)}, u32[]{:S(2)}) collective-permute-start(bf16[448,3584]{1,0:T(8,128)(2,1)} %bitcast.12), channel_id=1, source_target_pairs={{0,8},{8,0},{1,9},{9,1},{2,10},{10,2},{3,11},{11,3},{4,12},{12,4},... | collective-permute-start | bytes 9633800 | tf_op jit(solution)/shard_map/ppermute | solution.py:49
  15.6 15.9 %collective-permute-start = (bf16[16,3584]{1,0:T(8,128)(2,1)S(1)}, bf16[16,3584]{1,0:T(8,128)(2,1)S(1)}, u32[]{:S(2)}, u32[]{:S(2)}) collective-permute-start(bf16[16,3584]{1,0:T(8,128)(2,1)S(1)} %pad.4.refs_0_), channel_id=1, source_target_pairs={{0,176},{16,192},{32,208},{48,224},{64,240},{80,0},{96,16},{112,32... | collective-permute-start | bytes 344072 | tf_op jit(solution)/shard_map/ppermute | solution.py:49
  24.3 16.6 %collective-permute-start.1 = (bf16[16,3584]{1,0:T(8,128)(2,1)S(1)}, bf16[16,3584]{1,0:T(8,128)(2,1)S(1)}, u32[]{:S(2)}, u32[]{:S(2)}) collective-permute-start(bf16[16,3584]{1,0:T(8,128)(2,1)S(1)} %pad.4.refs_0_), channel_id=1, source_target_pairs={{0,80},{16,96},{32,112},{48,128},{64,144},{80,160},{96,176},{112,1... | collective-permute-start | bytes 344072 | tf_op jit(solution)/shard_map/ppermute | solution.py:49
  41.4 22.8 %copy-start = (bf16[448,1024]{1,0:T(8,128)(2,1)S(1)}, bf16[448,1024]{1,0:T(8,128)(2,1)}, u32[]{:S(2)}) copy-start(bf16[448,1024]{1,0:T(8,128)(2,1)} %refs_4_) | copy-start | bytes 2752516
  41.5 31.6 %collective-permute-start.3 = (bf16[256,1024]{1,0:T(8,128)(2,1)S(1)}, bf16[256,1024]{1,0:T(8,128)(2,1)}, u32[]{:S(2)}, u32[]{:S(2)}) collective-permute-start(bf16[256,1024]{1,0:T(8,128)(2,1)S(1)} %slice.20), channel_id=1, source_target_pairs={{0,256},{256,0},{1,257},{257,1},{2,258},{258,2},{3,259},{259,3},{4... | collective-permute-start | bytes 1572872 | tf_op jit(solution)/shard_map/ppermute | solution.py:49
  44.8 8.4 %collective-permute-start.4 = (bf16[48,3584]{1,0:T(8,128)(2,1)S(1)}, bf16[48,3584]{1,0:T(8,128)(2,1)S(1)}, u32[]{:S(2)}, u32[]{:S(2)}) collective-permute-start(bf16[48,3584]{1,0:T(8,128)(2,1)S(1)} %shard_map.137.refs_0_), channel_id=1, source_target_pairs={{0,240},{16,0},{32,16},{48,32},{64,48},{80,64},{96,80},{112,96},{1... | collective-permute-start | bytes 1032200 | tf_op jit(solution)/shard_map/ppermute | solution.py:49
  46.7 11.0 %collective-permute-start.5 = (bf16[48,3584]{1,0:T(8,128)(2,1)S(1)}, bf16[48,3584]{1,0:T(8,128)(2,1)S(1)}, u32[]{:S(2)}, u32[]{:S(2)}) collective-permute-start(bf16[48,3584]{1,0:T(8,128)(2,1)S(1)} %shard_map.137.refs_0_), channel_id=1, source_target_pairs={{0,16},{16,32},{32,48},{48,64},{64,80},{80,96},{96,112},{112,128},... | collective-permute-start | bytes 1032200 | tf_op jit(solution)/shard_map/ppermute | solution.py:49
  50.1 12.1 %collective-permute-start.6 = (bf16[48,3584]{1,0:T(8,128)(2,1)S(1)}, bf16[48,3584]{1,0:T(8,128)(2,1)S(1)}, u32[]{:S(2)}, u32[]{:S(2)}) collective-permute-start(bf16[48,3584]{1,0:T(8,128)(2,1)S(1)} %shard_map.137.refs_0_), channel_id=1, source_target_pairs={{0,256},{256,0},{1,257},{257,1},{2,258},{258,2},{3,259},{259,3},{4... | collective-permute-start | bytes 1032200 | tf_op jit(solution)/shard_map/ppermute | solution.py:49
  62.2 13.3 %collective-permute-start.7 = (bf16[48,3584]{1,0:T(8,128)(2,1)S(1)}, bf16[48,3584]{1,0:T(8,128)(2,1)S(1)}, u32[]{:S(2)}, u32[]{:S(2)}) collective-permute-start(bf16[48,3584]{1,0:T(8,128)(2,1)S(1)} %collective-permute-done.4.refs_0_), channel_id=1, source_target_pairs={{0,240},{16,0},{32,16},{48,32},{64,48},{80,64},{96,80},{112,96},{1... | collective-permute-start | bytes 1032200 | tf_op jit(solution)/shard_map/ppermute | solution.py:49
  66.5 13.1 %all-to-all-start.1 = ((f32[8,1,128]{2,1,0:T(1,128)}), f32[8,1,128]{2,1,0:T(1,128)S(1)}, u32[]{:S(2)}, u32[]{:S(2)}) async-start(f32[8,1,128]{2,1,0:T(1,128)} %broadcast_in_dim.24), calls=%async_computation.1 | async-start | bytes 8192 | tf_op jit(solution)/shard_map/all_to_all | solution.py:226
  79.5 72.1 %all-to-all-start = ((bf16[16,16,1024]{2,1,0:T(8,128)(2,1)}), bf16[16,16,1024]{2,1,0:T(8,128)(2,1)S(1)}, u32[]{:S(2)}, u32[]{:S(2)}) async-start(bf16[16,16,1024]{2,1,0:T(8,128)(2,1)} %bitcast.10), calls=%async_computation | async-start | bytes 1048576 | tf_op jit(solution)/shard_map/all_to_all | solution.py:242
  91.3 32.7 %collective-permute-start.10 = (bf16[96,3584]{1,0:T(8,128)(2,1)S(1)}, bf16[96,3584]{1,0:T(8,128)(2,1)S(1)}, u32[]{:S(2)}, u32[]{:S(2)}) collective-permute-start(bf16[96,3584]{1,0:T(8,128)(2,1)S(1)} %shard_map.138.refs_1_), channel_id=1, source_target_pairs={{0,256},{256,0},{1,257},{257,1},{2,258},{258,2},{3,259},{259,3},{4... | collective-permute-start | bytes 2064392 | tf_op jit(solution)/shard_map/ppermute | solution.py:49
  93.6 30.4 %collective-permute-start.9 = (bf16[48,3584]{1,0:T(8,128)(2,1)S(1)}, bf16[48,3584]{1,0:T(8,128)(2,1)S(1)}, u32[]{:S(2)}, u32[]{:S(2)}) collective-permute-start(bf16[48,3584]{1,0:T(8,128)(2,1)S(1)} %collective-permute-done.5.refs_1_), channel_id=1, source_target_pairs={{0,16},{16,32},{32,48},{48,64},{64,80},{80,96},{96,112},{112,128},... | collective-permute-start | bytes 1032200 | tf_op jit(solution)/shard_map/ppermute | solution.py:49
  96.8 27.2 %collective-permute-start.8 = (bf16[16,3584]{1,0:T(8,128)(2,1)S(1)}, bf16[16,3584]{1,0:T(8,128)(2,1)S(1)}, u32[]{:S(2)}, u32[]{:S(2)}) collective-permute-start(bf16[16,3584]{1,0:T(8,128)(2,1)S(1)} %collective-permute-done.refs_1_), channel_id=1, source_target_pairs={{0,208},{16,224},{32,240},{48,0},{64,16},{80,32},{96,48},{112,64},... | collective-permute-start | bytes 344072 | tf_op jit(solution)/shard_map/ppermute | solution.py:49
  124.0 19.7 %collective-permute-start.11 = (bf16[112,3584]{1,0:T(8,128)(2,1)S(1)}, bf16[112,3584]{1,0:T(8,128)(2,1)S(1)}, u32[]{:S(2)}, u32[]{:S(2)}) collective-permute-start(bf16[112,3584]{1,0:T(8,128)(2,1)S(1)} %shard_map.139.refs_3_), channel_id=1, source_target_pairs={{0,256},{256,0},{1,257},{257,1},{2,258},{258,2},{3,259},{259,3},{4... | collective-permute-start | bytes 2408456 | tf_op jit(solution)/shard_map/ppermute | solution.py:49
  151.6 32.8 %all-to-all-start.2 = ((bf16[16,64,448]{2,1,0:T(8,128)(2,1)}), bf16[16,64,448]{2,1,0:T(8,128)(2,1)S(1)}, u32[]{:S(2)}, u32[]{:S(2)}) async-start(bf16[16,64,448]{2,1,0:T(8,128)(2,1)} %bitcast.5), calls=%async_computation.2 | async-start | bytes 2097152 | tf_op jit(solution)/shard_map/all_to_all | solution.py:256
  159.1 49.7 %copy-start.4 = (s32[64]{0:T(128)S(1)}, s32[64]{0:T(128)}, u32[]{:S(2)}) copy-start(s32[64]{0:T(128)} %constant.63.clone) | copy-start | bytes 772
  159.1 49.7 %copy-start.5 = (s32[64]{0:T(128)S(1)}, s32[64]{0:T(128)}, u32[]{:S(2)}) copy-start(s32[64]{0:T(128)} %constant.62.clone) | copy-start | bytes 772
  159.1 49.7 %copy-start.6 = (s32[64]{0:T(128)S(1)}, s32[64]{0:T(128)}, u32[]{:S(2)}) copy-start(s32[64]{0:T(128)} %constant.61.clone) | copy-start | bytes 772
  184.4 19.5 %collective-permute-start.13 = (bf16[256,1024]{1,0:T(8,128)(2,1)S(1)}, bf16[256,1024]{1,0:T(8,128)(2,1)S(1)}, u32[]{:S(2)}, u32[]{:S(2)}) collective-permute-start(bf16[256,1024]{1,0:T(8,128)(2,1)S(1)} %all_gather.3.refs_0_), channel_id=1, source_target_pairs={{0,256},{256,0},{1,257},{257,1},{2,258},{258,2},{3,259},{259,3},{4... | collective-permute-start | bytes 1572872 | tf_op jit(solution)/shard_map/ppermute | solution.py:49
  187.7 23.2 %all-to-all-start.3 = ((bf16[8,64,896]{2,1,0:T(8,128)(2,1)}), bf16[8,64,896]{2,1,0:T(8,128)(2,1)S(1)}, u32[]{:S(2)}, u32[]{:S(2)}) async-start(bf16[8,64,896]{2,1,0:T(8,128)(2,1)} %shard_map.141), calls=%async_computation.3 | async-start | bytes 1835008 | tf_op jit(solution)/shard_map/all_to_all | solution.py:268
  194.8 14.0 %collective-permute-start.14 = (bf16[256,1024]{1,0:T(8,128)(2,1)S(1)}, bf16[256,1024]{1,0:T(8,128)(2,1)S(1)}, u32[]{:S(2)}, u32[]{:S(2)}) collective-permute-start(bf16[256,1024]{1,0:T(8,128)(2,1)S(1)} %all_gather.3.refs_0_), channel_id=1, source_target_pairs={{0,8},{8,0},{1,9},{9,1},{2,10},{10,2},{3,11},{11,3},{4,12},{12,4},... | collective-permute-start | bytes 1572872 | tf_op jit(solution)/shard_map/ppermute | solution.py:49
  203.9 7.0 %collective-permute-start.15 = (bf16[256,1024]{1,0:T(8,128)(2,1)S(1)}, bf16[256,1024]{1,0:T(8,128)(2,1)}, u32[]{:S(2)}, u32[]{:S(2)}) collective-permute-start(bf16[256,1024]{1,0:T(8,128)(2,1)S(1)} %collective-permute-done.13.refs_1_), channel_id=1, source_target_pairs={{0,8},{8,0},{1,9},{9,1},{2,10},{10,2},{3,11},{11,3},{4,12},{12,4},... | collective-permute-start | bytes 1572872 | tf_op jit(solution)/shard_map/ppermute | solution.py:49
  (3 other events, 22.7 us)

commit v6 on v5

--- a/solution.py
+++ b/solution.py
@@ -228,13 +228,13 @@
     near = stack(own, above, below)
     up, down, near_x = from_z(near, 1), from_z(near, -1), shift(near, "x_lo", 1)
     across = from_z(above, 3)
+    part = half(part[:RUN] + f32(shift(half(part[RUN:]), "x_lo", 1)))
+    up, down, near_x, narrow_sum, own_basis = lax.optimization_barrier((up, down, near_x, narrow_sum, own_basis))
     other_basis = shift(own_basis, "core", 1)
-    part = half(part[:RUN] + f32(shift(half(part[RUN:]), "x_lo", 1)))
-    up, down, near_x = lax.optimization_barrier((up, down, near_x))
     mid = stack(up, down)
-    up = from_z(up, 1)
-    part, up = lax.optimization_barrier((part, up))
-    *far, mid_x, narrow_sum = lax.optimization_barrier((up, from_z(down, -1), shift(mid, "x_lo", 1), narrow_sum))
+    across, *far, mid_x, part = lax.optimization_barrier(
+        (across, from_z(up, 1), from_z(down, -1), shift(mid, "x_lo", 1), part)
+    )
     far = stack(across, *far)
     far_x = shift(far, "x_lo", 1)
     blocks = [near, mid, near_x, far, mid_x, far_x]

time: 261 us -> 248 us (0.950)
  waiting for transfers between devices: 69.5 us -> 51.8 us
  blocking collectives: 68.4 us -> 82.9 us
  starting transfers between devices: 94.8 us -> 84.8 us
    ppermute x16, waiting for transfers between devices: 63.3 us -> 50 us  [shift(): return lax.ppermute(x, axis, [(i, (i + by) % size) for i in range(size)])]
    all_to_all x0 -> x1, blocking collectives: none -> 12.7 us  [on_device(): lax.all_to_all(local_sum, NARROW, 0, 0, tiled=True)[:, 0]]
    all_to_all x1, starting transfers between devices: 11.7 us -> 4.23 us  [on_device(): pieces = lax.all_to_all(part, ZZ, 0, 0, tiled=True)]
    all_to_all x1 -> x0, starting transfers between devices: 6.65 us -> none  [on_device(): lax.all_to_all(local_sum, NARROW, 0, 0, tiled=True)[:, 0]]
    ppermute x16, starting transfers between devices: 63.3 us -> 68.6 us  [shift(): return lax.ppermute(x, axis, [(i, (i + by) % size) for i in range(size)])]
    all_to_all x1 -> x0, waiting for transfers between devices: 4.1 us -> none  [on_device(): lax.all_to_all(local_sum, NARROW, 0, 0, tiled=True)[:, 0]]
  transfers between devices with their start and end apart: 20 -> 19, of which waited for: 9 -> 7; matrix products, arithmetic and copies ran while one was open for 3% -> 2% of each run, Pallas kernels for 3% -> 4%
where the time goes in v6:
time: 248 us; the launch traced here: 247 us
  starting transfers between devices  84.8 us (34%)
  blocking collectives  82.9 us (33%)
  waiting for transfers between devices  51.8 us (21%)
  Pallas kernels  15.5 us (6%)
  other arithmetic  5.74 us (2%)
  local copies, waits for them, and re-layouts  4.51 us (2%)
    ppermute x16, starting transfers between devices, shift(): return lax.ppermute(x, axis, [(i, (i + by) % size) for i in range(size)])  68.6 us
    ppermute x16, waiting for transfers between devices, shift(): return lax.ppermute(x, axis, [(i, (i + by) % size) for i in range(size)])  50 us
    all_to_all x2, blocking collectives, on_device(): lax.all_to_all(jnp.broadcast_to(scores, (8,) + scores.shape), axes, 0, 0,...  30.9 us
    all_gather x1, blocking collectives, on_device(): column = lax.all_gather(own_in, ZZ, axis=0, tiled=True)  26.3 us
    all_to_all x1, blocking collectives, on_device(): scores = jnp.sum(lax.all_to_all(scores, NARROW, 0, 0, tiled=True), 0)  12.9 us
    all_to_all x1, blocking collectives, on_device(): lax.all_to_all(local_sum, NARROW, 0, 0, tiled=True)[:, 0]  12.7 us
    pallas_call x1, Pallas kernels, on_device(): pl.pallas_call(rotate_out_kernel, out_shape=jax.ShapeDtypeStruct((ALL, n_...  7.84 us
    all_to_all x1, starting transfers between devices, on_device(): rotated_out = lax.all_to_all(shares, NARROW, 0, 0, tiled=True)  6.98 us
  transfers between devices with their start and end apart: 19, of which 7 were waited for; matrix products, arithmetic and copies ran while one was open for 2% of the time, Pallas kernels for 4%

profile of v6, /device:TPU:1, one launch (start us, length us, event | category | flops | bytes accessed | tf_op | source)
XLA Modules:
  0.0 247.0 jit_solution(10310490271314602652)
XLA Ops:
  4.0 8.8 %collective-permute-start.2 = (bf16[512,1024]{1,0:T(8,128)(2,1)S(1)}, bf16[512,1024]{1,0:T(8,128)(2,1)S(1)}, u32[]{:S(2)}, u32[]{:S(2)}) collective-permute-start(bf16[512,1024]{1,0:T(8,128)(2,1)S(1)} %get-tuple-element.25), channel_id=1, source_target_pairs={{0,8},{8,0},{1,9},{9,1},{2,10},{10,2},{3,11},{11,3},{4,12},{12,4},... | collective-permute-start | bytes 3145736 | tf_op jit(solution)/shard_map/ppermute | solution.py:49
  13.7 8.7 %collective-permute-start = (bf16[16,3584]{1,0:T(8,128)(2,1)S(1)}, bf16[16,3584]{1,0:T(8,128)(2,1)S(1)}, u32[]{:S(2)}, u32[]{:S(2)}) collective-permute-start(bf16[16,3584]{1,0:T(8,128)(2,1)S(1)} %pad.4.refs_0_), channel_id=1, source_target_pairs={{0,176},{16,192},{32,208},{48,224},{64,240},{80,0},{96,16},{112,32... | collective-permute-start | bytes 344072 | tf_op jit(solution)/shard_map/ppermute | solution.py:49
  24.4 5.3 %collective-permute-done.refs_1_ = bf16[16,3584]{1,0:T(8,128)(2,1)S(1)} collective-permute-done((bf16[16,3584]{1,0:T(8,128)(2,1)S(1)}, bf16[16,3584]{1,0:T(8,128)(2,1)S(1)}, u32[]{:S(2)}, u32[]{:S(2)}) %collective-permute-start) | collective-permute-done | bytes 114720 | tf_op jit(solution)/shard_map/ppermute | solution.py:49
  29.7 9.4 %collective-permute-done.1.refs_2_ = bf16[16,3584]{1,0:T(8,128)(2,1)S(1)} collective-permute-done((bf16[16,3584]{1,0:T(8,128)(2,1)S(1)}, bf16[16,3584]{1,0:T(8,128)(2,1)S(1)}, u32[]{:S(2)}, u32[]{:S(2)}) %collective-permute-start.1) | collective-permute-done | bytes 114720 | tf_op jit(solution)/shard_map/ppermute | solution.py:49
  41.1 3.4 %collective-permute-start.5 = (bf16[48,3584]{1,0:T(8,128)(2,1)S(1)}, bf16[48,3584]{1,0:T(8,128)(2,1)S(1)}, u32[]{:S(2)}, u32[]{:S(2)}) collective-permute-start(bf16[48,3584]{1,0:T(8,128)(2,1)S(1)} %shard_map.137.refs_0_), channel_id=1, source_target_pairs={{0,16},{16,32},{32,48},{48,64},{64,80},{80,96},{96,112},{112,128},... | collective-permute-start | bytes 1032200 | tf_op jit(solution)/shard_map/ppermute | solution.py:49
  44.4 3.1 %collective-permute-start.6 = (bf16[48,3584]{1,0:T(8,128)(2,1)S(1)}, bf16[48,3584]{1,0:T(8,128)(2,1)S(1)}, u32[]{:S(2)}, u32[]{:S(2)}) collective-permute-start(bf16[48,3584]{1,0:T(8,128)(2,1)S(1)} %shard_map.137.refs_0_), channel_id=1, source_target_pairs={{0,256},{256,0},{1,257},{257,1},{2,258},{258,2},{3,259},{259,3},{4... | collective-permute-start | bytes 1032200 | tf_op jit(solution)/shard_map/ppermute | solution.py:49
  49.4 12.7 %all_to_all.53 = f32[8,1,128]{2,1,0:T(1,128)S(1)} all-to-all(f32[8,1,128]{2,1,0:T(1,128)S(1)} %broadcast_in_dim.24), channel_id=1, replica_groups=mesh['x_lo'=2,'zh'=4,'zl'=4,'core'=2,'y'=4,'x_hi'=2] {'y','x_hi'}, dimensions={0} | all-to-all | bytes 8192 | tf_op jit(solution)/shard_map/all_to_all | solution.py:226
  62.8 10.1 %collective-permute-start.12 = (bf16[448,3584]{1,0:T(8,128)(2,1)}, bf16[448,3584]{1,0:T(8,128)(2,1)}, u32[]{:S(2)}, u32[]{:S(2)}) collective-permute-start(bf16[448,3584]{1,0:T(8,128)(2,1)} %bitcast.12), channel_id=1, source_target_pairs={{0,8},{8,0},{1,9},{9,1},{2,10},{10,2},{3,11},{11,3},{4,12},{12,4},... | collective-permute-start | bytes 9633800 | tf_op jit(solution)/shard_map/ppermute | solution.py:49
  75.2 3.4 %collective-permute-start.9 = (bf16[96,3584]{1,0:T(8,128)(2,1)S(1)}, bf16[96,3584]{1,0:T(8,128)(2,1)S(1)}, u32[]{:S(2)}, u32[]{:S(2)}) collective-permute-start(bf16[96,3584]{1,0:T(8,128)(2,1)S(1)} %shard_map.138.refs_1_), channel_id=1, source_target_pairs={{0,256},{256,0},{1,257},{257,1},{2,258},{258,2},{3,259},{259,3},{4... | collective-permute-start | bytes 2064392 | tf_op jit(solution)/shard_map/ppermute | solution.py:49
  78.6 3.3 %collective-permute-start.7 = (bf16[48,3584]{1,0:T(8,128)(2,1)S(1)}, bf16[48,3584]{1,0:T(8,128)(2,1)S(1)}, u32[]{:S(2)}, u32[]{:S(2)}) collective-permute-start(bf16[48,3584]{1,0:T(8,128)(2,1)S(1)} %collective-permute-done.4.refs_0_), channel_id=1, source_target_pairs={{0,240},{16,0},{32,16},{48,32},{64,48},{80,64},{96,80},{112,96},{1... | collective-permute-start | bytes 1032200 | tf_op jit(solution)/shard_map/ppermute | solution.py:49
  83.9 4.8 %collective-permute-done.10 = bf16[256,1024]{1,0:T(8,128)(2,1)S(1)} collective-permute-done((bf16[256,1024]{1,0:T(8,128)(2,1)S(1)}, bf16[256,1024]{1,0:T(8,128)(2,1)S(1)}, u32[]{:S(2)}, u32[]{:S(2)}) %collective-permute-start.10) | collective-permute-done | bytes 524320 | tf_op jit(solution)/shard_map/ppermute | solution.py:49
  91.5 10.1 %collective-permute-done.3.refs_0_ = bf16[16,3584]{1,0:T(8,128)(2,1)S(1)} collective-permute-done((bf16[16,3584]{1,0:T(8,128)(2,1)S(1)}, bf16[16,3584]{1,0:T(8,128)(2,1)S(1)}, u32[]{:S(2)}, u32[]{:S(2)}) %collective-permute-start.3) | collective-permute-done | bytes 114720 | tf_op jit(solution)/shard_map/ppermute | solution.py:49
  103.4 4.2 %all-to-all-start.1 = ((bf16[16,16,1024]{2,1,0:T(8,128)(2,1)}), bf16[16,16,1024]{2,1,0:T(8,128)(2,1)}, u32[]{:S(2)}, u32[]{:S(2)}) async-start(bf16[16,16,1024]{2,1,0:T(8,128)(2,1)} %bitcast.10), calls=%async_computation.1 | async-start | bytes 1048576 | tf_op jit(solution)/shard_map/all_to_all | solution.py:242
  109.7 18.6 %collective-permute-done.11.refs_5_ = bf16[112,3584]{1,0:T(8,128)(2,1)S(1)} collective-permute-done((bf16[112,3584]{1,0:T(8,128)(2,1)S(1)}, bf16[112,3584]{1,0:T(8,128)(2,1)S(1)}, u32[]{:S(2)}, u32[]{:S(2)}) %collective-permute-start.11) | collective-permute-done | bytes 802848 | tf_op jit(solution)/shard_map/ppermute | solution.py:49
  129.3 7.8 %shard_map.140 = bf16[1024,448]{1,0:T(8,128)(2,1)} custom-call(s32[1]{0:T(128)} %bitcast.4.core_ref, bf16[48,3584]{1,0:T(8,128)(2,1)S(1)} %shard_map.137.refs_0_, bf16[96,3584]{1,0:T(8,128)(2,1)S(1)} %shard_map.138.refs_1_, bf16[48,3584]{1,0:T(8,128)(2,1)S(1)} %copy-done.2, bf16[112,3584]{1,0:T(8,128)(2,1)S(1)} %shard_map.139.refs_3_, ...), custom_call_target="tpu_custom_call" | custom-call | flops 3300000000 | bytes 10000000 | tf_op jit(solution)/shard_map/pallas_call | solution.py:243
  137.2 5.1 %all-to-all-start.2 = ((bf16[16,64,448]{2,1,0:T(8,128)(2,1)}), bf16[16,64,448]{2,1,0:T(8,128)(2,1)S(1)}, u32[]{:S(2)}, u32[]{:S(2)}) async-start(bf16[16,64,448]{2,1,0:T(8,128)(2,1)} %bitcast.5), calls=%async_computation.2 | async-start | bytes 2097152 | tf_op jit(solution)/shard_map/all_to_all | solution.py:256
  144.9 26.3 %all_gather.3.refs_0_ = bf16[256,1024]{1,0:T(8,128)(2,1)S(1)} all-gather(bf16[16,1024]{1,0:T(8,128)(2,1)S(1)} %select_convert_fusion), channel_id=1, replica_groups=mesh['x_lo'=2,'zh'=4,'zl'=4,'core'=2,'y'=4,'x_hi'=2] {'zh','zl'}, dimensions={0}, use_global_device_ids=true | all-gather | bytes 557056 | tf_op jit(solution)/shard_map/all_gather | solution.py:255
  174.3 7.0 %all-to-all-start.3 = ((bf16[8,64,896]{2,1,0:T(8,128)(2,1)}), bf16[8,64,896]{2,1,0:T(8,128)(2,1)S(1)}, u32[]{:S(2)}, u32[]{:S(2)}) async-start(bf16[8,64,896]{2,1,0:T(8,128)(2,1)} %shard_map.141), calls=%async_computation.3 | async-start | bytes 1835008 | tf_op jit(solution)/shard_map/all_to_all | solution.py:268
  181.3 9.1 %collective-permute-start.14 = (bf16[256,1024]{1,0:T(8,128)(2,1)S(1)}, bf16[256,1024]{1,0:T(8,128)(2,1)}, u32[]{:S(2)}, u32[]{:S(2)}) collective-permute-start(bf16[256,1024]{1,0:T(8,128)(2,1)S(1)} %all_gather.3.refs_0_), channel_id=1, source_target_pairs={{0,8},{8,0},{1,9},{9,1},{2,10},{10,2},{3,11},{11,3},{4,12},{12,4},... | collective-permute-start | bytes 1572872 | tf_op jit(solution)/shard_map/ppermute | solution.py:49
  190.5 5.0 %collective-permute-start.15 = (bf16[256,1024]{1,0:T(8,128)(2,1)S(1)}, bf16[256,1024]{1,0:T(8,128)(2,1)}, u32[]{:S(2)}, u32[]{:S(2)}) collective-permute-start(bf16[256,1024]{1,0:T(8,128)(2,1)S(1)} %collective-permute-done.13.refs_1_), channel_id=1, source_target_pairs={{0,8},{8,0},{1,9},{9,1},{2,10},{10,2},{3,11},{11,3},{4,12},{12,4},... | collective-permute-start | bytes 1572872 | tf_op jit(solution)/shard_map/ppermute | solution.py:49
  197.4 5.1 %shard_map.142 = f32[8,4,384]{2,1,0:T(4,128)S(1)} custom-call(s32[64]{0:T(128)S(1)} %fusion.3.to_out_ref, s32[64]{0:T(128)S(1)} %get-tuple-element.46.to_in_ref, bf16[8,64,896]{2,1,0:T(8,128)(2,1)S(1)} %all-to-all-done.3.ro_ref, bf16[256,1024]{1,0:T(8,128)(2,1)S(1)} %all_gather.3.refs_0_, bf16[256,1024]{1,0:T(8,128)(2,1)S(1)} %collective-permute-done.13.refs_1_, ...), custom_call_target="tpu_custom_call" | custom-call | flops 3000000000 | bytes 5000000 | tf_op jit(solution)/shard_map/pallas_call | solution.py:270
  202.5 12.9 %all_to_all.54 = f32[8,4,384]{2,1,0:T(4,128)S(1)} all-to-all(f32[8,4,384]{2,1,0:T(4,128)S(1)} %shard_map.142), channel_id=1, replica_groups=mesh['x_lo'=2,'zh'=4,'zl'=4,'core'=2,'y'=4,'x_hi'=2] {'y','x_hi'}, dimensions={0} | all-to-all | bytes 98304 | tf_op jit(solution)/shard_map/all_to_all | solution.py:279
  215.4 10.8 %all_to_all.55 = f32[8,4,384]{2,1,0:T(4,128)S(1)} all-to-all(f32[8,4,384]{2,1,0:T(4,128)S(1)} %broadcast_in_dim.29), channel_id=1, replica_groups=mesh['x_lo'=2,'zh'=4,'zl'=4,'core'=2,'y'=4,'x_hi'=2] {'zl','core'}, dimensions={0} | all-to-all | bytes 98304 | tf_op jit(solution)/shard_map/all_to_all | solution.py:281
  226.3 20.1 %all_to_all.56 = f32[8,4,384]{2,1,0:T(4,128)S(1)} all-to-all(f32[8,4,384]{2,1,0:T(4,128)S(1)} %broadcast_in_dim.30), channel_id=1, replica_groups=mesh['x_lo'=2,'zh'=4,'zl'=4,'core'=2,'y'=4,'x_hi'=2] {'x_lo','zh'}, dimensions={0} | all-to-all | bytes 98304 | tf_op jit(solution)/shard_map/all_to_all | solution.py:281
  (61 shorter events, 30.0 us)
Async XLA Ops:
  0.0 47.6 %copy-start = (bf16[448,1024]{1,0:T(8,128)(2,1)S(1)}, bf16[448,1024]{1,0:T(8,128)(2,1)}, u32[]{:S(2)}) copy-start(bf16[448,1024]{1,0:T(8,128)(2,1)} %refs_4_) | copy-start | bytes 2752516
  4.0 35.1 %collective-permute-start.2 = (bf16[512,1024]{1,0:T(8,128)(2,1)S(1)}, bf16[512,1024]{1,0:T(8,128)(2,1)S(1)}, u32[]{:S(2)}, u32[]{:S(2)}) collective-permute-start(bf16[512,1024]{1,0:T(8,128)(2,1)S(1)} %get-tuple-element.25), channel_id=1, source_target_pairs={{0,8},{8,0},{1,9},{9,1},{2,10},{10,2},{3,11},{11,3},{4,12},{12,4},... | collective-permute-start | bytes 3145736 | tf_op jit(solution)/shard_map/ppermute | solution.py:49
  13.7 16.0 %collective-permute-start = (bf16[16,3584]{1,0:T(8,128)(2,1)S(1)}, bf16[16,3584]{1,0:T(8,128)(2,1)S(1)}, u32[]{:S(2)}, u32[]{:S(2)}) collective-permute-start(bf16[16,3584]{1,0:T(8,128)(2,1)S(1)} %pad.4.refs_0_), channel_id=1, source_target_pairs={{0,176},{16,192},{32,208},{48,224},{64,240},{80,0},{96,16},{112,32... | collective-permute-start | bytes 344072 | tf_op jit(solution)/shard_map/ppermute | solution.py:49
  22.5 16.6 %collective-permute-start.1 = (bf16[16,3584]{1,0:T(8,128)(2,1)S(1)}, bf16[16,3584]{1,0:T(8,128)(2,1)S(1)}, u32[]{:S(2)}, u32[]{:S(2)}) collective-permute-start(bf16[16,3584]{1,0:T(8,128)(2,1)S(1)} %pad.4.refs_0_), channel_id=1, source_target_pairs={{0,80},{16,96},{32,112},{48,128},{64,144},{80,160},{96,176},{112,1... | collective-permute-start | bytes 344072 | tf_op jit(solution)/shard_map/ppermute | solution.py:49
  39.1 23.6 %collective-permute-start.4 = (bf16[48,3584]{1,0:T(8,128)(2,1)S(1)}, bf16[48,3584]{1,0:T(8,128)(2,1)S(1)}, u32[]{:S(2)}, u32[]{:S(2)}) collective-permute-start(bf16[48,3584]{1,0:T(8,128)(2,1)S(1)} %shard_map.137.refs_0_), channel_id=1, source_target_pairs={{0,240},{16,0},{32,16},{48,32},{64,48},{80,64},{96,80},{112,96},{1... | collective-permute-start | bytes 1032200 | tf_op jit(solution)/shard_map/ppermute | solution.py:49
  41.1 21.7 %collective-permute-start.5 = (bf16[48,3584]{1,0:T(8,128)(2,1)S(1)}, bf16[48,3584]{1,0:T(8,128)(2,1)S(1)}, u32[]{:S(2)}, u32[]{:S(2)}) collective-permute-start(bf16[48,3584]{1,0:T(8,128)(2,1)S(1)} %shard_map.137.refs_0_), channel_id=1, source_target_pairs={{0,16},{16,32},{32,48},{48,64},{64,80},{80,96},{96,112},{112,128},... | collective-permute-start | bytes 1032200 | tf_op jit(solution)/shard_map/ppermute | solution.py:49
  44.4 18.3 %collective-permute-start.6 = (bf16[48,3584]{1,0:T(8,128)(2,1)S(1)}, bf16[48,3584]{1,0:T(8,128)(2,1)S(1)}, u32[]{:S(2)}, u32[]{:S(2)}) collective-permute-start(bf16[48,3584]{1,0:T(8,128)(2,1)S(1)} %shard_map.137.refs_0_), channel_id=1, source_target_pairs={{0,256},{256,0},{1,257},{257,1},{2,258},{258,2},{3,259},{259,3},{4... | collective-permute-start | bytes 1032200 | tf_op jit(solution)/shard_map/ppermute | solution.py:49
  62.8 10.4 %copy-start.1 = (bf16[48,3584]{1,0:T(8,128)(2,1)}, bf16[48,3584]{1,0:T(8,128)(2,1)S(1)}, u32[]{:S(2)}) copy-start(bf16[48,3584]{1,0:T(8,128)(2,1)S(1)} %collective-permute-done.6.refs_2_) | copy-start | bytes 1032196
  62.8 65.6 %collective-permute-start.12 = (bf16[448,3584]{1,0:T(8,128)(2,1)}, bf16[448,3584]{1,0:T(8,128)(2,1)}, u32[]{:S(2)}, u32[]{:S(2)}) collective-permute-start(bf16[448,3584]{1,0:T(8,128)(2,1)} %bitcast.12), channel_id=1, source_target_pairs={{0,8},{8,0},{1,9},{9,1},{2,10},{10,2},{3,11},{11,3},{4,12},{12,4},... | collective-permute-start | bytes 9633800 | tf_op jit(solution)/shard_map/ppermute | solution.py:49
  73.2 15.4 %collective-permute-start.10 = (bf16[256,1024]{1,0:T(8,128)(2,1)S(1)}, bf16[256,1024]{1,0:T(8,128)(2,1)S(1)}, u32[]{:S(2)}, u32[]{:S(2)}) collective-permute-start(bf16[256,1024]{1,0:T(8,128)(2,1)S(1)} %slice.20), channel_id=1, source_target_pairs={{0,256},{256,0},{1,257},{257,1},{2,258},{258,2},{3,259},{259,3},{4... | collective-permute-start | bytes 1572872 | tf_op jit(solution)/shard_map/ppermute | solution.py:49
  75.2 28.2 %collective-permute-start.9 = (bf16[96,3584]{1,0:T(8,128)(2,1)S(1)}, bf16[96,3584]{1,0:T(8,128)(2,1)S(1)}, u32[]{:S(2)}, u32[]{:S(2)}) collective-permute-start(bf16[96,3584]{1,0:T(8,128)(2,1)S(1)} %shard_map.138.refs_1_), channel_id=1, source_target_pairs={{0,256},{256,0},{1,257},{257,1},{2,258},{258,2},{3,259},{259,3},{4... | collective-permute-start | bytes 2064392 | tf_op jit(solution)/shard_map/ppermute | solution.py:49
  78.6 23.1 %collective-permute-start.7 = (bf16[48,3584]{1,0:T(8,128)(2,1)S(1)}, bf16[48,3584]{1,0:T(8,128)(2,1)S(1)}, u32[]{:S(2)}, u32[]{:S(2)}) collective-permute-start(bf16[48,3584]{1,0:T(8,128)(2,1)S(1)} %collective-permute-done.4.refs_0_), channel_id=1, source_target_pairs={{0,240},{16,0},{32,16},{48,32},{64,48},{80,64},{96,80},{112,96},{1... | collective-permute-start | bytes 1032200 | tf_op jit(solution)/shard_map/ppermute | solution.py:49
  81.9 19.8 %collective-permute-start.8 = (bf16[48,3584]{1,0:T(8,128)(2,1)S(1)}, bf16[48,3584]{1,0:T(8,128)(2,1)S(1)}, u32[]{:S(2)}, u32[]{:S(2)}) collective-permute-start(bf16[48,3584]{1,0:T(8,128)(2,1)S(1)} %collective-permute-done.5.refs_1_), channel_id=1, source_target_pairs={{0,16},{16,32},{32,48},{48,64},{64,80},{80,96},{96,112},{112,128},... | collective-permute-start | bytes 1032200 | tf_op jit(solution)/shard_map/ppermute | solution.py:49
  88.7 13.0 %collective-permute-start.3 = (bf16[16,3584]{1,0:T(8,128)(2,1)S(1)}, bf16[16,3584]{1,0:T(8,128)(2,1)S(1)}, u32[]{:S(2)}, u32[]{:S(2)}) collective-permute-start(bf16[16,3584]{1,0:T(8,128)(2,1)S(1)} %collective-permute-done.refs_1_), channel_id=1, source_target_pairs={{0,208},{16,224},{32,240},{48,0},{64,16},{80,32},{96,48},{112,64},... | collective-permute-start | bytes 344072 | tf_op jit(solution)/shard_map/ppermute | solution.py:49
  103.4 33.8 %all-to-all-start.1 = ((bf16[16,16,1024]{2,1,0:T(8,128)(2,1)}), bf16[16,16,1024]{2,1,0:T(8,128)(2,1)}, u32[]{:S(2)}, u32[]{:S(2)}) async-start(bf16[16,16,1024]{2,1,0:T(8,128)(2,1)} %bitcast.10), calls=%async_computation.1 | async-start | bytes 1048576 | tf_op jit(solution)/shard_map/all_to_all | solution.py:242
  107.7 20.6 %collective-permute-start.11 = (bf16[112,3584]{1,0:T(8,128)(2,1)S(1)}, bf16[112,3584]{1,0:T(8,128)(2,1)S(1)}, u32[]{:S(2)}, u32[]{:S(2)}) collective-permute-start(bf16[112,3584]{1,0:T(8,128)(2,1)S(1)} %shard_map.139.refs_3_), channel_id=1, source_target_pairs={{0,256},{256,0},{1,257},{257,1},{2,258},{258,2},{3,259},{259,3},{4... | collective-permute-start | bytes 2408456 | tf_op jit(solution)/shard_map/ppermute | solution.py:49
  137.2 34.0 %all-to-all-start.2 = ((bf16[16,64,448]{2,1,0:T(8,128)(2,1)}), bf16[16,64,448]{2,1,0:T(8,128)(2,1)S(1)}, u32[]{:S(2)}, u32[]{:S(2)}) async-start(bf16[16,64,448]{2,1,0:T(8,128)(2,1)} %bitcast.5), calls=%async_computation.2 | async-start | bytes 2097152 | tf_op jit(solution)/shard_map/all_to_all | solution.py:256
  144.9 50.6 %copy-start.5 = (s32[64]{0:T(128)S(1)}, s32[64]{0:T(128)}, u32[]{:S(2)}) copy-start(s32[64]{0:T(128)} %constant.63.clone) | copy-start | bytes 772
  144.9 50.6 %copy-start.6 = (s32[64]{0:T(128)S(1)}, s32[64]{0:T(128)}, u32[]{:S(2)}) copy-start(s32[64]{0:T(128)} %constant.62.clone) | copy-start | bytes 772
  144.9 50.6 %copy-start.7 = (s32[64]{0:T(128)S(1)}, s32[64]{0:T(128)}, u32[]{:S(2)}) copy-start(s32[64]{0:T(128)} %constant.61.clone) | copy-start | bytes 772
  171.2 19.2 %collective-permute-start.13 = (bf16[256,1024]{1,0:T(8,128)(2,1)S(1)}, bf16[256,1024]{1,0:T(8,128)(2,1)S(1)}, u32[]{:S(2)}, u32[]{:S(2)}) collective-permute-start(bf16[256,1024]{1,0:T(8,128)(2,1)S(1)} %all_gather.3.refs_0_), channel_id=1, source_target_pairs={{0,256},{256,0},{1,257},{257,1},{2,258},{258,2},{3,259},{259,3},{4... | collective-permute-start | bytes 1572872 | tf_op jit(solution)/shard_map/ppermute | solution.py:49
  174.3 23.0 %all-to-all-start.3 = ((bf16[8,64,896]{2,1,0:T(8,128)(2,1)}), bf16[8,64,896]{2,1,0:T(8,128)(2,1)S(1)}, u32[]{:S(2)}, u32[]{:S(2)}) async-start(bf16[8,64,896]{2,1,0:T(8,128)(2,1)} %shard_map.141), calls=%async_computation.3 | async-start | bytes 1835008 | tf_op jit(solution)/shard_map/all_to_all | solution.py:268
  181.3 14.2 %collective-permute-start.14 = (bf16[256,1024]{1,0:T(8,128)(2,1)S(1)}, bf16[256,1024]{1,0:T(8,128)(2,1)}, u32[]{:S(2)}, u32[]{:S(2)}) collective-permute-start(bf16[256,1024]{1,0:T(8,128)(2,1)S(1)} %all_gather.3.refs_0_), channel_id=1, source_target_pairs={{0,8},{8,0},{1,9},{9,1},{2,10},{10,2},{3,11},{11,3},{4,12},{12,4},... | collective-permute-start | bytes 1572872 | tf_op jit(solution)/shard_map/ppermute | solution.py:49
  190.5 6.9 %collective-permute-start.15 = (bf16[256,1024]{1,0:T(8,128)(2,1)S(1)}, bf16[256,1024]{1,0:T(8,128)(2,1)}, u32[]{:S(2)}, u32[]{:S(2)}) collective-permute-start(bf16[256,1024]{1,0:T(8,128)(2,1)S(1)} %collective-permute-done.13.refs_1_), channel_id=1, source_target_pairs={{0,8},{8,0},{1,9},{9,1},{2,10},{10,2},{3,11},{11,3},{4,12},{12,4},... | collective-permute-start | bytes 1572872 | tf_op jit(solution)/shard_map/ppermute | solution.py:49
  (3 other events, 2.9 us)

commit v7 on v6

--- a/solution.py
+++ b/solution.py
@@ -69,6 +69,12 @@
     return lax.dot_general(a, b, (((over_a,), (over_b,)), ((), ())), preferred_element_type=jnp.float32)
 
 
+def own_kernel(grad_ref, eig_ref, out_ref):
+    value = jnp.sum(f32(eig_ref[...]), keepdims=True)
+    padding = jnp.zeros((ROWS - OWN, grad_ref.shape[1]), jnp.float32)
+    out_ref[...] = half(with_terms(cat(f32(grad_ref[...]), padding), value, ROWS))
+
+
 def rotate_in_kernel(at_ref, in_ref, basis_ref, keep_ref, send_ref, wide_s, rows_s):
     wide_s[:TOKENS, :] = f32(in_ref[...])
     wide_s[TOKENS:, :] = jnp.zeros((8, in_ref.shape[1]), jnp.float32)
@@ -87,9 +93,10 @@
     for block in blocks:
         rows_s[at:at + block.shape[0], :] = block[...]
         at += block.shape[0]
+    column_sum = padding_sum(rows_s[:, :128])
     for i, basis in enumerate((own_ref, other_ref)):
-        product = half(dot(rows_s[...], basis[...], 1, 1))
-        out_ref[pl.ds((core_ref[0] ^ i) * HALF, HALF), :] = product
+        product = with_terms(dot(rows_s[...], basis[...], 1, 1), column_sum, SHARE)
+        out_ref[pl.ds((core_ref[0] ^ i) * HALF, HALF), :] = half(product)
 
 
 def stack_kernel(*refs):
@@ -105,17 +112,19 @@
     return jnp.sum(jnp.where((row == OWN) & (column < 3), f32(block), 0.0), keepdims=True)
 
 
-def with_terms(block, value):
+def with_terms(block, value, every):
     row = lax.broadcasted_iota(jnp.int32, block.shape, 0)
     column = lax.broadcasted_iota(jnp.int32, block.shape, 1)
     first = f32(half(value))
     second = f32(half(value - first))
     third = value - first - second
     terms = jnp.where(column == 0, first, jnp.where(column == 1, second, jnp.where(column == 2, third, 0.0)))
-    return jnp.where(row == OWN, terms, block)
-
-
-def share_kernel(parts_ref, out_ref):
+    return jnp.where(lax.rem(row, every) == OWN, terms, block)
+
+
+def share_kernel(parts_ref, out_ref, overall_ref):
+    overall = sum(padding_sum(parts_ref[i, :ROWS, :128]) for i in range(C * N))
+    overall_ref[...] = jnp.broadcast_to(overall, overall_ref.shape)
     shares = []
     for c in range(C):
         total = f32(parts_ref[c * N])
@@ -136,13 +145,13 @@
     return spans
 
 
-def score_kernel(to_out_ref, to_in_ref, ro_ref, *refs):
+def score_kernel(to_out_ref, to_in_ref, overall_ref, ro_ref, *refs):
     in_refs, (eig_ref, out_ref, ro_s, ri_s) = refs[:4], refs[4:]
 
     def place(scratch, at_ref, i, block):
         scratch[pl.ds(pl.multiple_of(at_ref[i] * ROWS, ROWS), ROWS), :] = block
 
-    overall = sum(padding_sum(ref[:, :128]) for ref in in_refs)
+    overall = overall_ref[:1, :1]
     width = ro_ref.shape[2] // C
     for i in range(PIECES):
         n, c, at = i // (C * PER), i // PER % C, i % PER * ROWS
@@ -205,7 +214,14 @@
         return ((x_me ^ order[:, 1]) * C + (core ^ order[:, 0])) * Z + lax.rem(z + order[:, 2] + Z, Z)
 
     own_basis = out_basis.T
-    own = lax.optimization_barrier(jnp.pad(grad_out, ((0, ROWS - OWN), (0, 0))))
+    own = pl.pallas_call(
+        own_kernel,
+        out_shape=jax.ShapeDtypeStruct((ROWS, grad_out.shape[1]), jnp.bfloat16),
+        in_specs=[VMEM] * 2,
+        out_specs=VMEM,
+        compiler_params=params(),
+        cost_estimate=pl.CostEstimate(flops=10**6, bytes_accessed=10**6, transcendentals=0),
+    )(grad_out, eigen_values)
     above, below = from_z(own, 5), from_z(own, -5)
     to_rows = ((c_me ^ OWNERS[:, 0]) * X + (x_me ^ OWNERS[:, 1])) * Z + OWNERS[:, 2]
     keep, send = pl.pallas_call(
@@ -220,21 +236,19 @@
         compiler_params=params(),
         cost_estimate=pl.CostEstimate(flops=3 * 10**8, bytes_accessed=3 * 10**6, transcendentals=0),
     )(to_rows, inputs, in_basis)
-    above, below, sent, eigen_values = lax.optimization_barrier((above, below, shift(send, "core", 1), eigen_values))
+    above, below, sent = lax.optimization_barrier((above, below, shift(send, "core", 1)))
     part = keep + f32(sent)
-    local_sum = jnp.full((N, 128), jnp.sum(eigen_values, dtype=jnp.float32))
-    narrow_sum = jnp.sum(lax.all_to_all(local_sum, NARROW, 0, 0, tiled=True)[:, 0])
 
     near = stack(own, above, below)
     up, down, near_x = from_z(near, 1), from_z(near, -1), shift(near, "x_lo", 1)
     across = from_z(above, 3)
     part = half(part[:RUN] + f32(shift(half(part[RUN:]), "x_lo", 1)))
-    up, down, near_x, narrow_sum, own_basis = lax.optimization_barrier((up, down, near_x, narrow_sum, own_basis))
+    up, down, near_x, across, part = lax.optimization_barrier((up, down, near_x, across, part))
+    mid = stack(up, down)
+    *far, mid_x, part, own_basis = lax.optimization_barrier(
+        (from_z(up, 1), from_z(down, -1), shift(mid, "x_lo", 1), part, own_basis)
+    )
     other_basis = shift(own_basis, "core", 1)
-    mid = stack(up, down)
-    across, *far, mid_x, part = lax.optimization_barrier(
-        (across, from_z(up, 1), from_z(down, -1), shift(mid, "x_lo", 1), part)
-    )
     far = stack(across, *far)
     far_x = shift(far, "x_lo", 1)
     blocks = [near, mid, near_x, far, mid_x, far_x]
@@ -250,16 +264,18 @@
         cost_estimate=pl.CostEstimate(flops=33 * 10**8, bytes_accessed=10**7, transcendentals=0),
     )(c_me.astype(jnp.int32).reshape(1), *blocks, own_basis, other_basis)
     pieces, partial_out = lax.optimization_barrier((pieces, partial_out))
-    own_in = jnp.sum(f32(pieces.reshape(Z, ROWS, n_in)), 0)
-    own_in = half(with_terms(own_in, narrow_sum))
+    own_in = half(jnp.sum(f32(pieces.reshape(Z, ROWS, n_in)), 0))
     column = lax.all_gather(own_in, ZZ, axis=0, tiled=True)
     parts = lax.all_to_all(partial_out, ("core",) + NARROW, 0, 0, tiled=True)
     parts, column = lax.optimization_barrier((parts, column))
-    shares = pl.pallas_call(
+    shares, overall = pl.pallas_call(
         share_kernel,
-        out_shape=jax.ShapeDtypeStruct((N, SHARE, C * n_out), jnp.bfloat16),
+        out_shape=(
+            jax.ShapeDtypeStruct((N, SHARE, C * n_out), jnp.bfloat16),
+            jax.ShapeDtypeStruct((8, 128), jnp.float32),
+        ),
         in_specs=[VMEM],
-        out_specs=VMEM,
+        out_specs=(VMEM, VMEM),
         compiler_params=params(),
         cost_estimate=pl.CostEstimate(flops=10**6, bytes_accessed=2 * 10**6, transcendentals=0),
     )(parts.reshape(C * N, SHARE, n_out))
@@ -270,12 +286,12 @@
     scores = pl.pallas_call(
         score_kernel,
         out_shape=jax.ShapeDtypeStruct((N, QUERIES, SCORED), jnp.float32),
-        in_specs=[SMEM] * 2 + [VMEM] * 6,
+        in_specs=[SMEM] * 2 + [VMEM] * 7,
         out_specs=VMEM,
         scratch_shapes=[pltpu.VMEM((ALL, n_out), jnp.bfloat16), pltpu.VMEM((ALL, n_in), jnp.bfloat16)],
         compiler_params=params(),
         cost_estimate=pl.CostEstimate(flops=3 * 10**9, bytes_accessed=5 * 10**6, transcendentals=0),
-    )(places(OUT_ORDER, 0, z_me), places(IN_ORDER, c_me, 0), rotated_out, *rotated_in, eigen_values)
+    )(places(OUT_ORDER, 0, z_me), places(IN_ORDER, c_me, 0), overall, rotated_out, *rotated_in, eigen_values)
     scores = jnp.sum(lax.all_to_all(scores, NARROW, 0, 0, tiled=True), 0)
     for axes in (("zl", "core"), ("x_lo", "zh")):
         scores = jnp.sum(lax.all_to_all(jnp.broadcast_to(scores, (8,) + scores.shape), axes, 0, 0, tiled=True), 0)

time: 248 us -> 241 us (0.972)
  blocking collectives: 82.9 us -> 70.7 us
  starting transfers between devices: 84.8 us -> 96.9 us
  waiting for transfers between devices: 51.8 us -> 48 us
    all_to_all x1 -> x0, blocking collectives: 12.7 us -> none  [on_device(): lax.all_to_all(local_sum, NARROW, 0, 0, tiled=True)[:, 0]]
    ppermute x16, starting transfers between devices: 68.6 us -> 74.4 us  [shift(): return lax.ppermute(x, axis, [(i, (i + by) % size) for i in range(size)])]
    all_to_all x1, starting transfers between devices: 4.23 us -> 8.05 us  [on_device(): pieces = lax.all_to_all(part, ZZ, 0, 0, tiled=True)]
    ppermute x16, waiting for transfers between devices: 50 us -> 46.3 us  [shift(): return lax.ppermute(x, axis, [(i, (i + by) % size) for i in range(size)])]
    all_to_all x1, starting transfers between devices: 5.07 us -> 7.94 us  [on_device(): parts = lax.all_to_all(partial_out, ('core',) + NARROW, 0, 0, tiled=True)]
  transfers between devices with their start and end apart: 19 -> 19, of which waited for: 7 -> 8; matrix products, arithmetic and copies ran while one was open for 2% -> 1% of each run, Pallas kernels for 4% -> 4%
where the time goes in v7:
time: 241 us; the launch traced here: 240 us
  starting transfers between devices  96.9 us (40%)
  blocking collectives  70.7 us (29%)
  waiting for transfers between devices  48 us (20%)
  Pallas kernels  16 us (7%)
  local copies, waits for them, and re-layouts  4.07 us (2%)
  other arithmetic  3.84 us (2%)
    ppermute x16, starting transfers between devices, shift(): return lax.ppermute(x, axis, [(i, (i + by) % size) for i in range(size)])  74.4 us
    ppermute x16, waiting for transfers between devices, shift(): return lax.ppermute(x, axis, [(i, (i + by) % size) for i in range(size)])  46.3 us
    all_to_all x2, blocking collectives, on_device(): lax.all_to_all(jnp.broadcast_to(scores, (8,) + scores.shape), axes, 0, 0,...  30.2 us
    all_gather x1, blocking collectives, on_device(): column = lax.all_gather(own_in, ZZ, axis=0, tiled=True)  27.3 us
    all_to_all x1, blocking collectives, on_device(): scores = jnp.sum(lax.all_to_all(scores, NARROW, 0, 0, tiled=True), 0)  13.2 us
    all_to_all x1, starting transfers between devices, on_device(): pieces = lax.all_to_all(part, ZZ, 0, 0, tiled=True)  8.05 us
    all_to_all x1, starting transfers between devices, on_device(): parts = lax.all_to_all(partial_out, ('core',) + NARROW, 0, 0, tiled=True)  7.94 us
    pallas_call x1, Pallas kernels, on_device(): pl.pallas_call(rotate_out_kernel, out_shape=jax.ShapeDtypeStruct((ALL, n_...  7.83 us
  transfers between devices with their start and end apart: 19, of which 8 were waited for; matrix products, arithmetic and copies ran while one was open for 1% of the time, Pallas kernels for 4%

profile of v7, /device:TPU:1, one launch (start us, length us, event | category | flops | bytes accessed | tf_op | source)
XLA Modules:
  0.0 239.7 jit_solution(9664809638225100557)
XLA Ops:
  3.9 8.8 %collective-permute-start.2 = (bf16[512,1024]{1,0:T(8,128)(2,1)S(1)}, bf16[512,1024]{1,0:T(8,128)(2,1)S(1)}, u32[]{:S(2)}, u32[]{:S(2)}) collective-permute-start(bf16[512,1024]{1,0:T(8,128)(2,1)S(1)} %get-tuple-element.26), channel_id=1, source_target_pairs={{0,8},{8,0},{1,9},{9,1},{2,10},{10,2},{3,11},{11,3},{4,12},{12,4},... | collective-permute-start | bytes 3145736 | tf_op jit(solution)/shard_map/ppermute | solution.py:49
  15.4 4.8 %collective-permute-start.1 = (bf16[16,3584]{1,0:T(8,128)(2,1)S(1)}, bf16[16,3584]{1,0:T(8,128)(2,1)S(1)}, u32[]{:S(2)}, u32[]{:S(2)}) collective-permute-start(bf16[16,3584]{1,0:T(8,128)(2,1)S(1)} %shard_map.136.refs_0_), channel_id=1, source_target_pairs={{0,80},{16,96},{32,112},{48,128},{64,144},{80,160},{96,176},{112,1... | collective-permute-start | bytes 344072 | tf_op jit(solution)/shard_map/ppermute | solution.py:49
  20.2 6.5 %collective-permute-start = (bf16[16,3584]{1,0:T(8,128)(2,1)S(1)}, bf16[16,3584]{1,0:T(8,128)(2,1)S(1)}, u32[]{:S(2)}, u32[]{:S(2)}) collective-permute-start(bf16[16,3584]{1,0:T(8,128)(2,1)S(1)} %shard_map.136.refs_0_), channel_id=1, source_target_pairs={{0,176},{16,192},{32,208},{48,224},{64,240},{80,0},{96,16},{112,32... | collective-permute-start | bytes 344072 | tf_op jit(solution)/shard_map/ppermute | solution.py:49
  28.1 9.4 %collective-permute-done.refs_1_ = bf16[16,3584]{1,0:T(8,128)(2,1)S(1)} collective-permute-done((bf16[16,3584]{1,0:T(8,128)(2,1)S(1)}, bf16[16,3584]{1,0:T(8,128)(2,1)S(1)}, u32[]{:S(2)}, u32[]{:S(2)}) %collective-permute-start) | collective-permute-done | bytes 114720 | tf_op jit(solution)/shard_map/ppermute | solution.py:49
  37.9 3.1 %collective-permute-start.7 = (bf16[256,1024]{1,0:T(8,128)(2,1)S(1)}, bf16[256,1024]{1,0:T(8,128)(2,1)S(1)}, u32[]{:S(2)}, u32[]{:S(2)}) collective-permute-start(bf16[256,1024]{1,0:T(8,128)(2,1)S(1)} %slice.15), channel_id=1, source_target_pairs={{0,256},{256,0},{1,257},{257,1},{2,258},{258,2},{3,259},{259,3},{4... | collective-permute-start | bytes 1572872 | tf_op jit(solution)/shard_map/ppermute | solution.py:49
  45.2 7.3 %collective-permute-start.3 = (bf16[48,3584]{1,0:T(8,128)(2,1)S(1)}, bf16[48,3584]{1,0:T(8,128)(2,1)S(1)}, u32[]{:S(2)}, u32[]{:S(2)}) collective-permute-start(bf16[48,3584]{1,0:T(8,128)(2,1)S(1)} %shard_map.138.refs_0_), channel_id=1, source_target_pairs={{0,240},{16,0},{32,16},{48,32},{64,48},{80,64},{96,80},{112,96},{1... | collective-permute-start | bytes 1032200 | tf_op jit(solution)/shard_map/ppermute | solution.py:49
  56.5 13.0 %collective-permute-done.6.refs_0_ = bf16[16,3584]{1,0:T(8,128)(2,1)S(1)} collective-permute-done((bf16[16,3584]{1,0:T(8,128)(2,1)S(1)}, bf16[16,3584]{1,0:T(8,128)(2,1)S(1)}, u32[]{:S(2)}, u32[]{:S(2)}) %collective-permute-start.6) | collective-permute-done | bytes 114720 | tf_op jit(solution)/shard_map/ppermute | solution.py:49
  69.6 3.1 %collective-permute-start.10 = (bf16[96,3584]{1,0:T(8,128)(2,1)S(1)}, bf16[96,3584]{1,0:T(8,128)(2,1)S(1)}, u32[]{:S(2)}, u32[]{:S(2)}) collective-permute-start(bf16[96,3584]{1,0:T(8,128)(2,1)S(1)} %shard_map.139.refs_1_), channel_id=1, source_target_pairs={{0,256},{256,0},{1,257},{257,1},{2,258},{258,2},{3,259},{259,3},{4... | collective-permute-start | bytes 2064392 | tf_op jit(solution)/shard_map/ppermute | solution.py:49
  74.6 5.4 %collective-permute-start.9 = (bf16[48,3584]{1,0:T(8,128)(2,1)S(1)}, bf16[48,3584]{1,0:T(8,128)(2,1)S(1)}, u32[]{:S(2)}, u32[]{:S(2)}) collective-permute-start(bf16[48,3584]{1,0:T(8,128)(2,1)S(1)} %collective-permute-done.4.refs_1_), channel_id=1, source_target_pairs={{0,16},{16,32},{32,48},{48,64},{64,80},{80,96},{96,112},{112,128},... | collective-permute-start | bytes 1032200 | tf_op jit(solution)/shard_map/ppermute | solution.py:49
  80.0 3.3 %collective-permute-done.8.refs_1_ = bf16[48,3584]{1,0:T(8,128)(2,1)S(1)} collective-permute-done((bf16[48,3584]{1,0:T(8,128)(2,1)S(1)}, bf16[48,3584]{1,0:T(8,128)(2,1)S(1)}, u32[]{:S(2)}, u32[]{:S(2)}) %collective-permute-start.8) | collective-permute-done | bytes 344096 | tf_op jit(solution)/shard_map/ppermute | solution.py:49
  84.4 6.7 %collective-permute-start.12 = (bf16[448,3584]{1,0:T(8,128)(2,1)}, bf16[448,3584]{1,0:T(8,128)(2,1)}, u32[]{:S(2)}, u32[]{:S(2)}) collective-permute-start(bf16[448,3584]{1,0:T(8,128)(2,1)} %bitcast.refs_6_), channel_id=1, source_target_pairs={{0,8},{8,0},{1,9},{9,1},{2,10},{10,2},{3,11},{11,3},{4,12},{12,4},... | collective-permute-start | bytes 9633800 | tf_op jit(solution)/shard_map/ppermute | solution.py:49
  91.2 8.0 %all-to-all-start = ((bf16[16,16,1024]{2,1,0:T(8,128)(2,1)}), bf16[16,16,1024]{2,1,0:T(8,128)(2,1)}, u32[]{:S(2)}, u32[]{:S(2)}) async-start(bf16[16,16,1024]{2,1,0:T(8,128)(2,1)} %bitcast.1), calls=%async_computation | async-start | bytes 1048576 | tf_op jit(solution)/shard_map/all_to_all | solution.py:256
  99.3 3.1 %collective-permute-start.11 = (bf16[112,3584]{1,0:T(8,128)(2,1)S(1)}, bf16[112,3584]{1,0:T(8,128)(2,1)S(1)}, u32[]{:S(2)}, u32[]{:S(2)}) collective-permute-start(bf16[112,3584]{1,0:T(8,128)(2,1)S(1)} %shard_map.140.refs_3_), channel_id=1, source_target_pairs={{0,256},{256,0},{1,257},{257,1},{2,258},{258,2},{3,259},{259,3},{4... | collective-permute-start | bytes 2408456 | tf_op jit(solution)/shard_map/ppermute | solution.py:49
  102.4 18.1 %collective-permute-done.11.refs_5_ = bf16[112,3584]{1,0:T(8,128)(2,1)S(1)} collective-permute-done((bf16[112,3584]{1,0:T(8,128)(2,1)S(1)}, bf16[112,3584]{1,0:T(8,128)(2,1)S(1)}, u32[]{:S(2)}, u32[]{:S(2)}) %collective-permute-start.11) | collective-permute-done | bytes 802848 | tf_op jit(solution)/shard_map/ppermute | solution.py:49
  120.5 7.8 %shard_map.141 = bf16[1024,448]{1,0:T(8,128)(2,1)} custom-call(s32[1]{0:T(128)} %bitcast.3.core_ref, bf16[48,3584]{1,0:T(8,128)(2,1)S(1)} %shard_map.138.refs_0_, bf16[96,3584]{1,0:T(8,128)(2,1)S(1)} %shard_map.139.refs_1_, bf16[48,3584]{1,0:T(8,128)(2,1)S(1)} %collective-permute-done.5.refs_2_, bf16[112,3584]{1,0:T(8,128)(2,1)S(1)} %shard_map.140.refs_3_, ...), custom_call_target="tpu_custom_call" | custom-call | flops 3300000000 | bytes 10000000 | tf_op jit(solution)/shard_map/pallas_call | solution.py:257
  128.4 7.9 %all-to-all-start.1 = ((bf16[16,64,448]{2,1,0:T(8,128)(2,1)}), bf16[16,64,448]{2,1,0:T(8,128)(2,1)S(1)}, u32[]{:S(2)}, u32[]{:S(2)}) async-start(bf16[16,64,448]{2,1,0:T(8,128)(2,1)} %bitcast.4), calls=%async_computation.1 | async-start | bytes 2097152 | tf_op jit(solution)/shard_map/all_to_all | solution.py:269
  137.6 27.3 %all_gather.3.refs_0_ = bf16[256,1024]{1,0:T(8,128)(2,1)S(1)} all-gather(bf16[16,1024]{1,0:T(8,128)(2,1)S(1)} %reduce_sum.39), channel_id=1, replica_groups=mesh['x_lo'=2,'zh'=4,'zl'=4,'core'=2,'y'=4,'x_hi'=2] {'zh','zl'}, dimensions={0}, use_global_device_ids=true | all-gather | bytes 557056 | tf_op jit(solution)/shard_map/all_gather | solution.py:268
  168.2 6.5 %all-to-all-start.2 = ((bf16[8,64,896]{2,1,0:T(8,128)(2,1)}), bf16[8,64,896]{2,1,0:T(8,128)(2,1)S(1)}, u32[]{:S(2)}, u32[]{:S(2)}) async-start(bf16[8,64,896]{2,1,0:T(8,128)(2,1)} %get-tuple-element.45), calls=%async_computation.2 | async-start | bytes 1835008 | tf_op jit(solution)/shard_map/all_to_all | solution.py:284
  174.7 9.5 %collective-permute-start.14 = (bf16[256,1024]{1,0:T(8,128)(2,1)S(1)}, bf16[256,1024]{1,0:T(8,128)(2,1)S(1)}, u32[]{:S(2)}, u32[]{:S(2)}) collective-permute-start(bf16[256,1024]{1,0:T(8,128)(2,1)S(1)} %all_gather.3.refs_0_), channel_id=1, source_target_pairs={{0,8},{8,0},{1,9},{9,1},{2,10},{10,2},{3,11},{11,3},{4,12},{12,4},... | collective-permute-start | bytes 1572872 | tf_op jit(solution)/shard_map/ppermute | solution.py:49
  184.2 4.8 %collective-permute-start.15 = (bf16[256,1024]{1,0:T(8,128)(2,1)S(1)}, bf16[256,1024]{1,0:T(8,128)(2,1)}, u32[]{:S(2)}, u32[]{:S(2)}) collective-permute-start(bf16[256,1024]{1,0:T(8,128)(2,1)S(1)} %collective-permute-done.13.refs_1_), channel_id=1, source_target_pairs={{0,8},{8,0},{1,9},{9,1},{2,10},{10,2},{3,11},{11,3},{4,12},{12,4},... | collective-permute-start | bytes 1572872 | tf_op jit(solution)/shard_map/ppermute | solution.py:49
  190.7 5.0 %shard_map.143 = f32[8,4,384]{2,1,0:T(4,128)S(1)} custom-call(s32[64]{0:T(128)S(1)} %fusion.2.to_out_ref, s32[64]{0:T(128)S(1)} %get-tuple-element.48.to_in_ref, f32[8,128]{1,0:T(8,128)S(1)} %get-tuple-element.44.overall_ref, bf16[8,64,896]{2,1,0:T(8,128)(2,1)S(1)} %all-to-all-done.2.ro_ref, bf16[256,1024]{1,0:T(8,128)(2,1)S(1)} %all_gather.3.refs_0_, ...), custom_call_target="tpu_custom_call" | custom-call | flops 3000000000 | bytes 5000000 | tf_op jit(solution)/shard_map/pallas_call | solution.py:286
  195.7 13.2 %all_to_all.44 = f32[8,4,384]{2,1,0:T(4,128)S(1)} all-to-all(f32[8,4,384]{2,1,0:T(4,128)S(1)} %shard_map.143), channel_id=1, replica_groups=mesh['x_lo'=2,'zh'=4,'zl'=4,'core'=2,'y'=4,'x_hi'=2] {'y','x_hi'}, dimensions={0} | all-to-all | bytes 98304 | tf_op jit(solution)/shard_map/all_to_all | solution.py:295
  208.9 10.2 %all_to_all.45 = f32[8,4,384]{2,1,0:T(4,128)S(1)} all-to-all(f32[8,4,384]{2,1,0:T(4,128)S(1)} %broadcast_in_dim.6), channel_id=1, replica_groups=mesh['x_lo'=2,'zh'=4,'zl'=4,'core'=2,'y'=4,'x_hi'=2] {'zl','core'}, dimensions={0} | all-to-all | bytes 98304 | tf_op jit(solution)/shard_map/all_to_all | solution.py:297
  219.2 19.9 %all_to_all.46 = f32[8,4,384]{2,1,0:T(4,128)S(1)} all-to-all(f32[8,4,384]{2,1,0:T(4,128)S(1)} %broadcast_in_dim.7), channel_id=1, replica_groups=mesh['x_lo'=2,'zh'=4,'zl'=4,'core'=2,'y'=4,'x_hi'=2] {'x_lo','zh'}, dimensions={0} | all-to-all | bytes 98304 | tf_op jit(solution)/shard_map/all_to_all | solution.py:297
  (53 shorter events, 26.6 us)
Async XLA Ops:
  3.9 33.6 %collective-permute-start.2 = (bf16[512,1024]{1,0:T(8,128)(2,1)S(1)}, bf16[512,1024]{1,0:T(8,128)(2,1)S(1)}, u32[]{:S(2)}, u32[]{:S(2)}) collective-permute-start(bf16[512,1024]{1,0:T(8,128)(2,1)S(1)} %get-tuple-element.26), channel_id=1, source_target_pairs={{0,8},{8,0},{1,9},{9,1},{2,10},{10,2},{3,11},{11,3},{4,12},{12,4},... | collective-permute-start | bytes 3145736 | tf_op jit(solution)/shard_map/ppermute | solution.py:49
  12.7 1.2 copy-start
  15.4 12.7 %collective-permute-start.1 = (bf16[16,3584]{1,0:T(8,128)(2,1)S(1)}, bf16[16,3584]{1,0:T(8,128)(2,1)S(1)}, u32[]{:S(2)}, u32[]{:S(2)}) collective-permute-start(bf16[16,3584]{1,0:T(8,128)(2,1)S(1)} %shard_map.136.refs_0_), channel_id=1, source_target_pairs={{0,80},{16,96},{32,112},{48,128},{64,144},{80,160},{96,176},{112,1... | collective-permute-start | bytes 344072 | tf_op jit(solution)/shard_map/ppermute | solution.py:49
  20.2 17.3 %collective-permute-start = (bf16[16,3584]{1,0:T(8,128)(2,1)S(1)}, bf16[16,3584]{1,0:T(8,128)(2,1)S(1)}, u32[]{:S(2)}, u32[]{:S(2)}) collective-permute-start(bf16[16,3584]{1,0:T(8,128)(2,1)S(1)} %shard_map.136.refs_0_), channel_id=1, source_target_pairs={{0,176},{16,192},{32,208},{48,224},{64,240},{80,0},{96,16},{112,32... | collective-permute-start | bytes 344072 | tf_op jit(solution)/shard_map/ppermute | solution.py:49
  37.9 17.6 %collective-permute-start.7 = (bf16[256,1024]{1,0:T(8,128)(2,1)S(1)}, bf16[256,1024]{1,0:T(8,128)(2,1)S(1)}, u32[]{:S(2)}, u32[]{:S(2)}) collective-permute-start(bf16[256,1024]{1,0:T(8,128)(2,1)S(1)} %slice.15), channel_id=1, source_target_pairs={{0,256},{256,0},{1,257},{257,1},{2,258},{258,2},{3,259},{259,3},{4... | collective-permute-start | bytes 1572872 | tf_op jit(solution)/shard_map/ppermute | solution.py:49
  41.1 28.4 %collective-permute-start.5 = (bf16[48,3584]{1,0:T(8,128)(2,1)S(1)}, bf16[48,3584]{1,0:T(8,128)(2,1)S(1)}, u32[]{:S(2)}, u32[]{:S(2)}) collective-permute-start(bf16[48,3584]{1,0:T(8,128)(2,1)S(1)} %shard_map.138.refs_0_), channel_id=1, source_target_pairs={{0,256},{256,0},{1,257},{257,1},{2,258},{258,2},{3,259},{259,3},{4... | collective-permute-start | bytes 1032200 | tf_op jit(solution)/shard_map/ppermute | solution.py:49
  43.2 26.2 %collective-permute-start.4 = (bf16[48,3584]{1,0:T(8,128)(2,1)S(1)}, bf16[48,3584]{1,0:T(8,128)(2,1)S(1)}, u32[]{:S(2)}, u32[]{:S(2)}) collective-permute-start(bf16[48,3584]{1,0:T(8,128)(2,1)S(1)} %shard_map.138.refs_0_), channel_id=1, source_target_pairs={{0,16},{16,32},{32,48},{48,64},{64,80},{80,96},{96,112},{112,128},... | collective-permute-start | bytes 1032200 | tf_op jit(solution)/shard_map/ppermute | solution.py:49
  45.2 24.3 %collective-permute-start.3 = (bf16[48,3584]{1,0:T(8,128)(2,1)S(1)}, bf16[48,3584]{1,0:T(8,128)(2,1)S(1)}, u32[]{:S(2)}, u32[]{:S(2)}) collective-permute-start(bf16[48,3584]{1,0:T(8,128)(2,1)S(1)} %shard_map.138.refs_0_), channel_id=1, source_target_pairs={{0,240},{16,0},{32,16},{48,32},{64,48},{80,64},{96,80},{112,96},{1... | collective-permute-start | bytes 1032200 | tf_op jit(solution)/shard_map/ppermute | solution.py:49
  52.5 17.0 %collective-permute-start.6 = (bf16[16,3584]{1,0:T(8,128)(2,1)S(1)}, bf16[16,3584]{1,0:T(8,128)(2,1)S(1)}, u32[]{:S(2)}, u32[]{:S(2)}) collective-permute-start(bf16[16,3584]{1,0:T(8,128)(2,1)S(1)} %collective-permute-done.refs_1_), channel_id=1, source_target_pairs={{0,208},{16,224},{32,240},{48,0},{64,16},{80,32},{96,48},{112,64},... | collective-permute-start | bytes 344072 | tf_op jit(solution)/shard_map/ppermute | solution.py:49
  69.6 14.9 %collective-permute-start.10 = (bf16[96,3584]{1,0:T(8,128)(2,1)S(1)}, bf16[96,3584]{1,0:T(8,128)(2,1)S(1)}, u32[]{:S(2)}, u32[]{:S(2)}) collective-permute-start(bf16[96,3584]{1,0:T(8,128)(2,1)S(1)} %shard_map.139.refs_1_), channel_id=1, source_target_pairs={{0,256},{256,0},{1,257},{257,1},{2,258},{258,2},{3,259},{259,3},{4... | collective-permute-start | bytes 2064392 | tf_op jit(solution)/shard_map/ppermute | solution.py:49
  72.7 10.6 %collective-permute-start.8 = (bf16[48,3584]{1,0:T(8,128)(2,1)S(1)}, bf16[48,3584]{1,0:T(8,128)(2,1)S(1)}, u32[]{:S(2)}, u32[]{:S(2)}) collective-permute-start(bf16[48,3584]{1,0:T(8,128)(2,1)S(1)} %collective-permute-done.3.refs_0_), channel_id=1, source_target_pairs={{0,240},{16,0},{32,16},{48,32},{64,48},{80,64},{96,80},{112,96},{1... | collective-permute-start | bytes 1032200 | tf_op jit(solution)/shard_map/ppermute | solution.py:49
  74.6 9.6 %collective-permute-start.9 = (bf16[48,3584]{1,0:T(8,128)(2,1)S(1)}, bf16[48,3584]{1,0:T(8,128)(2,1)S(1)}, u32[]{:S(2)}, u32[]{:S(2)}) collective-permute-start(bf16[48,3584]{1,0:T(8,128)(2,1)S(1)} %collective-permute-done.4.refs_1_), channel_id=1, source_target_pairs={{0,16},{16,32},{32,48},{48,64},{64,80},{80,96},{96,112},{112,128},... | collective-permute-start | bytes 1032200 | tf_op jit(solution)/shard_map/ppermute | solution.py:49
  84.4 36.1 %collective-permute-start.12 = (bf16[448,3584]{1,0:T(8,128)(2,1)}, bf16[448,3584]{1,0:T(8,128)(2,1)}, u32[]{:S(2)}, u32[]{:S(2)}) collective-permute-start(bf16[448,3584]{1,0:T(8,128)(2,1)} %bitcast.refs_6_), channel_id=1, source_target_pairs={{0,8},{8,0},{1,9},{9,1},{2,10},{10,2},{3,11},{11,3},{4,12},{12,4},... | collective-permute-start | bytes 9633800 | tf_op jit(solution)/shard_map/ppermute | solution.py:49
  91.2 37.1 %all-to-all-start = ((bf16[16,16,1024]{2,1,0:T(8,128)(2,1)}), bf16[16,16,1024]{2,1,0:T(8,128)(2,1)}, u32[]{:S(2)}, u32[]{:S(2)}) async-start(bf16[16,16,1024]{2,1,0:T(8,128)(2,1)} %bitcast.1), calls=%async_computation | async-start | bytes 1048576 | tf_op jit(solution)/shard_map/all_to_all | solution.py:256
  99.3 21.2 %collective-permute-start.11 = (bf16[112,3584]{1,0:T(8,128)(2,1)S(1)}, bf16[112,3584]{1,0:T(8,128)(2,1)S(1)}, u32[]{:S(2)}, u32[]{:S(2)}) collective-permute-start(bf16[112,3584]{1,0:T(8,128)(2,1)S(1)} %shard_map.140.refs_3_), channel_id=1, source_target_pairs={{0,256},{256,0},{1,257},{257,1},{2,258},{258,2},{3,259},{259,3},{4... | collective-permute-start | bytes 2408456 | tf_op jit(solution)/shard_map/ppermute | solution.py:49
  128.4 36.5 %all-to-all-start.1 = ((bf16[16,64,448]{2,1,0:T(8,128)(2,1)}), bf16[16,64,448]{2,1,0:T(8,128)(2,1)S(1)}, u32[]{:S(2)}, u32[]{:S(2)}) async-start(bf16[16,64,448]{2,1,0:T(8,128)(2,1)} %bitcast.4), calls=%async_computation.1 | async-start | bytes 2097152 | tf_op jit(solution)/shard_map/all_to_all | solution.py:269
  136.3 52.7 %copy-start.5 = (s32[64]{0:T(128)S(1)}, s32[64]{0:T(128)}, u32[]{:S(2)}) copy-start(s32[64]{0:T(128)} %constant.56.clone) | copy-start | bytes 772
  136.3 52.7 %copy-start.6 = (s32[64]{0:T(128)S(1)}, s32[64]{0:T(128)}, u32[]{:S(2)}) copy-start(s32[64]{0:T(128)} %constant.55.clone) | copy-start | bytes 772
  136.3 52.7 %copy-start.7 = (s32[64]{0:T(128)S(1)}, s32[64]{0:T(128)}, u32[]{:S(2)}) copy-start(s32[64]{0:T(128)} %constant.54.clone) | copy-start | bytes 772
  136.3 54.4 %copy-start.1 = (bf16[448,1024]{1,0:T(8,128)(2,1)S(1)}, bf16[448,1024]{1,0:T(8,128)(2,1)}, u32[]{:S(2)}) copy-start(bf16[448,1024]{1,0:T(8,128)(2,1)} %refs_4_.1) | copy-start | bytes 2752516
  164.9 19.3 %collective-permute-start.13 = (bf16[256,1024]{1,0:T(8,128)(2,1)S(1)}, bf16[256,1024]{1,0:T(8,128)(2,1)S(1)}, u32[]{:S(2)}, u32[]{:S(2)}) collective-permute-start(bf16[256,1024]{1,0:T(8,128)(2,1)S(1)} %all_gather.3.refs_0_), channel_id=1, source_target_pairs={{0,256},{256,0},{1,257},{257,1},{2,258},{258,2},{3,259},{259,3},{4... | collective-permute-start | bytes 1572872 | tf_op jit(solution)/shard_map/ppermute | solution.py:49
  168.2 22.5 %all-to-all-start.2 = ((bf16[8,64,896]{2,1,0:T(8,128)(2,1)}), bf16[8,64,896]{2,1,0:T(8,128)(2,1)S(1)}, u32[]{:S(2)}, u32[]{:S(2)}) async-start(bf16[8,64,896]{2,1,0:T(8,128)(2,1)} %get-tuple-element.45), calls=%async_computation.2 | async-start | bytes 1835008 | tf_op jit(solution)/shard_map/all_to_all | solution.py:284
  174.7 14.4 %collective-permute-start.14 = (bf16[256,1024]{1,0:T(8,128)(2,1)S(1)}, bf16[256,1024]{1,0:T(8,128)(2,1)S(1)}, u32[]{:S(2)}, u32[]{:S(2)}) collective-permute-start(bf16[256,1024]{1,0:T(8,128)(2,1)S(1)} %all_gather.3.refs_0_), channel_id=1, source_target_pairs={{0,8},{8,0},{1,9},{9,1},{2,10},{10,2},{3,11},{11,3},{4,12},{12,4},... | collective-permute-start | bytes 1572872 | tf_op jit(solution)/shard_map/ppermute | solution.py:49
  184.2 6.5 %collective-permute-start.15 = (bf16[256,1024]{1,0:T(8,128)(2,1)S(1)}, bf16[256,1024]{1,0:T(8,128)(2,1)}, u32[]{:S(2)}, u32[]{:S(2)}) collective-permute-start(bf16[256,1024]{1,0:T(8,128)(2,1)S(1)} %collective-permute-done.13.refs_1_), channel_id=1, source_target_pairs={{0,8},{8,0},{1,9},{9,1},{2,10},{10,2},{3,11},{11,3},{4,12},{12,4},... | collective-permute-start | bytes 1572872 | tf_op jit(solution)/shard_map/ppermute | solution.py:49
  (3 other events, 2.8 us)
